TPU v7x, 128 devices: a whole 4x4x4 slice. The times are simulated.
128 devices in a mesh: layer: 4 (over z_lo, core), latent: 32 (over x, z_hi, y).
Axes of the slice: x: 4, y: 4, z: 4 (z_hi: 2, z_lo: 2; z = z_hi * 2 + z_lo), core: 2. Of those that a mesh axis runs over, the one named last changes fastest.
Arguments:
- residuals: bfloat16 [4, 512, 3584], P('layer', 'latent'), may hold values from -6 to 6
- enc_weight: bfloat16 [4, 3584, 24576], P('layer', None, 'latent'), may hold values from -0.046875 to 0.046875
- dec_weight: bfloat16 [4, 24576, 3584], P('layer', 'latent'), may hold values from -0.0390625 to 0.0390625
- enc_bias: float32 [24576], P('latent'), may hold values from -1 to 0.5
- dec_bias: float32 [4, 3584], P('layer'), may hold values from -3 to 3
Outputs:
- enc_grad: bfloat16 [4, 3584, 24576], P('layer', None, 'latent')
- dec_grad: bfloat16 [4, 24576, 3584], P('layer', 'latent')
- enc_bias_grad: float32 [24576], P('latent')
All inputs are finite; a program needn't handle non-finite values.
Results may differ from a plain program's by a relative error of at most 0.02.
Values may be sent and summed in bfloat16 or wider, within the bound.
No kernel may reach another device: no remote copies, remote signals or barrier semaphores. Data moves between devices by JAX's collectives and lax.ppermute only.
A program may use at most 128 MiB of HBM per device.

v0:
```python
import jax
import jax.numpy as jnp
from jax import lax
from jax.sharding import PartitionSpec as P

sparsity_weight = 0.5
sharpness = 4.0


def per_device(residuals, enc_weight, dec_weight, enc_bias, dec_bias):
    own_rows = residuals[0]
    enc_local = enc_weight[0]
    dec_local = dec_weight[0]
    gathered = lax.all_gather(own_rows, "latent", axis=0, tiled=True)
    pre_part = jnp.dot(gathered, enc_local, preferred_element_type=jnp.float32)
    row_norms = jnp.sqrt(jnp.sum(jnp.square(dec_local.astype(jnp.float32)), axis=1) + 1e-06)
    pre_total, weight_sum = lax.psum((pre_part, row_norms), "layer")
    pre_full = pre_total + enc_bias[None, :]
    latents = (jax.nn.softplus(sharpness * pre_full) / sharpness).astype(jnp.bfloat16)
    gate_all = jax.nn.sigmoid(sharpness * pre_full)
    act_sum = jnp.sum(latents.astype(jnp.float32), axis=0)
    lat_rows = latents
    rebuilt = lax.psum_scatter(
        jnp.dot(lat_rows, dec_local, preferred_element_type=jnp.float32).astype(jnp.bfloat16),
        "latent",
        scatter_dimension=0,
        tiled=True,
    ).astype(jnp.float32)
    misfit = rebuilt + dec_bias[0][None, :] - own_rows.astype(jnp.float32)
    err_grad = (2.0 * misfit).astype(jnp.bfloat16)
    err_piece = lax.all_gather(err_grad, "latent", axis=0, tiled=True)
    lat_rows = latents
    dec_acc = lax.dot_general(
        lat_rows, err_piece, (((0,), (0,)), ((), ())), preferred_element_type=jnp.float32
    )
    back_rows = lax.dot_general(
        err_piece, dec_local, (((1,), (1,)), ((), ())), preferred_element_type=jnp.float32
    )
    lat_part = back_rows
    dec_acc, lat_part = (dec_acc, lat_part)
    penalty = sparsity_weight * weight_sum[None, :]
    lat_grad = lax.psum(lat_part.astype(jnp.bfloat16), "layer").astype(jnp.float32) + penalty
    pre_grad = (lat_grad * gate_all).astype(jnp.bfloat16)
    enc_grad = lax.dot_general(
        gathered, pre_grad, (((0,), (0,)), ((), ())), preferred_element_type=jnp.float32
    ).astype(jnp.bfloat16)
    enc_bias_grad = jnp.sum(pre_grad.astype(jnp.float32), axis=0)
    penalty_term = (
        sparsity_weight * act_sum[:, None] * dec_local.astype(jnp.float32) / row_norms[:, None]
    )
    dec_grad = (dec_acc + penalty_term).astype(jnp.bfloat16)
    return (enc_grad[None], dec_grad[None], enc_bias_grad)


def solution(mesh):
    in_specs = (
        P("layer", "latent", None),
        P("layer", None, "latent"),
        P("layer", "latent", None),
        P("latent"),
        P("layer", None),
    )
    out_specs = (P("layer", None, "latent"), P("layer", "latent", None), P("latent"))
    return jax.shard_map(
        per_device, mesh=mesh, in_specs=in_specs, out_specs=out_specs, check_vma=False
    )
```

profile of v0, /device:TPU:1, one launch (start us, length us, event | category | flops | bytes accessed | tf_op | source)
XLA Modules:
  0.0 496.8 jit_solution(12142019913235078704)
XLA Ops:
  7.2 0.0 all-gather.6.cloned.1.call-start
  7.2 0.7 all-gather.6.cloned.1.call-update
  7.9 0.0 copy-start.2
  7.9 0.0 all-reduce.3.cloned.1.call-start
  8.0 84.8 %all-gather.6.cloned.1.call-done = bf16[1,512,3584]{2,1,0:T(8,128)(2,1)} async-done(((bf16[1,16,3584]{2,1,0:T(8,128)(2,1)}), bf16[1,512,3584]{2,1,0:T(8,128)(2,1)}) %all-gather.6.cloned.1.call-update) | async-done | bytes 3670032 | tf_op jit(solution)/shard_map/all_gather | solution.py:14
  92.7 7.8 %fusion.9 = f32[512,768]{1,0:T(8,128)} fusion(bf16[1,3584,768]{2,1,0:T(8,128)(2,1)} %param.6, bf16[1,512,3584]{2,1,0:T(8,128)(2,1)} %all-gather.6.cloned.1.call-done), kind=kOutput, calls=%fused_computation.13 | convolution fusion | flops 2818572288 | bytes 10747904 | tf_op jit(solution)/shard_map/dot_general | solution.py:15
  100.6 0.0 all-reduce.3.cloned.1.call-update
  100.6 0.0 reduce-scatter.2.cloned.1.call-start
  100.6 47.8 %all-reduce.3.cloned.1.call-done = f32[512,768]{1,0:T(8,128)} async-done(((f32[512,768]{1,0:T(8,128)}), f32[512,768]{1,0:T(8,128)}) %all-reduce.3.cloned.1.call-update) | async-done | bytes 1572880 | tf_op jit(solution)/shard_map/psum | solution.py:17
  148.5 0.0 copy-done.2
  148.5 2.6 convert_reduce_fusion.1
  151.0 7.0 %convolution_convert_fusion.1 = bf16[512,3584]{1,0:T(8,128)(2,1)} fusion(bf16[512,768]{1,0:T(8,128)(2,1)S(1)} %get-tuple-element.9, bf16[1,768,3584]{2,1,0:T(8,128)(2,1)} %param.7), kind=kOutput, calls=%fused_computation.9 | convolution fusion | flops 2820407296 | bytes 9961472 | tf_op jit(solution)/shard_map/dot_general | solution.py:24
  158.1 0.0 copy-start.3
  158.1 0.0 copy-start.1
  158.1 0.0 reduce-scatter.2.cloned.1.call-update
  158.1 0.0 all-gather.4.cloned.1.call-start
  158.1 0.6 copy-done.3
  158.8 168.0 %reduce-scatter.2.cloned.1.call-done = bf16[16,3584]{1,0:T(8,128)(2,1)} async-done(((bf16[512,3584]{1,0:T(8,128)(2,1)}), bf16[16,3584]{1,0:T(8,128)(2,1)}) %reduce-scatter.2.cloned.1.call-update) | async-done | bytes 114704 | tf_op jit(solution)/shard_map/reduce_scatter | solution.py:23
  326.8 0.0 copy-done.1
  326.8 1.6 fusion.19
  328.4 0.0 all-gather.4.cloned.1.call-update
  328.4 0.0 all-reduce.5.cloned.1.call-start
  328.5 3.7 fusion
  332.2 28.6 %psum.23 = f32[768]{0:T(1024)S(1)} all-reduce(f32[768]{0:T(1024)S(1)} %add_sqrt_fusion), channel_id=1, replica_groups=mesh['layer'=4,'latent'=32] {'layer'}, use_global_device_ids=true, to_apply=%region_4.5 | all-reduce | flops 768 | bytes 6144 | tf_op jit(solution)/shard_map/psum | solution.py:17
  360.8 66.0 %all-gather.4.cloned.1.call-done = bf16[512,3584]{1,0:T(8,128)(2,1)} async-done(((bf16[16,3584]{1,0:T(8,128)(2,1)}), bf16[512,3584]{1,0:T(8,128)(2,1)}) %all-gather.4.cloned.1.call-update) | async-done | bytes 3670032 | tf_op jit(solution)/shard_map/all_gather | solution.py:31
  426.8 7.6 %fusion.15 = bf16[512,768]{1,0:T(8,128)(2,1)} fusion(bf16[512,3584]{1,0:T(8,128)(2,1)} %all-gather.4.cloned.1.call-done, bf16[1,768,3584]{2,1,0:T(8,128)(2,1)} %param.7), kind=kOutput, calls=%fused_computation.24 | convolution fusion | flops 2818965504 | bytes 9961472 | tf_op jit(solution)/shard_map/dot_general | solution.py:36
  434.4 0.0 all-reduce.5.cloned.1.call-update
  434.4 0.0 copy-start
  434.4 8.4 %fusion.4 = bf16[1,768,3584]{2,1,0:T(8,128)(2,1)} fusion(bf16[512,768]{1,0:T(8,128)(2,1)S(1)} %get-tuple-element.9, bf16[512,3584]{1,0:T(8,128)(2,1)} %all-gather.4.cloned.1.call-done, bf16[1,768,3584]{2,1,0:T(8,128)(2,1)} %param.7, f32[768]{0:T(1024)S(1)} %add_sqrt_fusion, f32[768]{0:T(1024)S(1)} %broadcast_multiply_fusion), kind=kOutput, calls=%fused_computation.7 | convolution fusion | flops 2832334848 | bytes 15472640 | tf_op jit(solution)/shard_map/dot_general | solution.py:33
  442.9 29.9 %all-reduce.5.cloned.1.call-done = bf16[512,768]{1,0:T(8,128)(2,1)} async-done(((bf16[512,768]{1,0:T(8,128)(2,1)}), bf16[512,768]{1,0:T(8,128)(2,1)}) %all-reduce.5.cloned.1.call-update) | async-done | bytes 786448 | tf_op jit(solution)/shard_map/psum | solution.py:42
  472.8 0.0 copy-done
  472.8 2.3 convert_reduce_fusion
  475.1 6.9 %fusion.5 = bf16[1,3584,768]{1,2,0:T(8,128)(2,1)} fusion(bf16[512,768]{1,0:T(8,128)(2,1)S(1)} %get-tuple-element.7, bf16[1,512,3584]{2,1,0:T(8,128)(2,1)} %all-gather.6.cloned.1.call-done), kind=kOutput, calls=%fused_computation.8 | convolution fusion | flops 2821324800 | bytes 9961472 | tf_op jit(solution)/shard_map/dot_general | solution.py:44
  482.0 8.3 %copy.8 = bf16[1,3584,768]{2,1,0:T(8,128)(2,1)} copy(bf16[1,3584,768]{1,2,0:T(8,128)(2,1)} %fusion.5) | data formatting | bytes 11010048
  (4 shorter events, 0.1 us)
Async XLA Ops:
  7.2 85.6 %all-gather.6.cloned.1.call-start = ((), (), s32[]{:S(2)}) async-start(), calls=%async_computation.5 | async-start | bytes 3784704 | tf_op jit(solution)/shard_map/all_gather | solution.py:14
  7.9 140.6 %copy-start.2 = (f32[768]{0:T(1024)S(1)}, f32[768]{0:T(1024)}, u32[]{:S(2)}) copy-start(f32[768]{0:T(1024)} %param.8) | copy-start | bytes 9220
  7.9 140.6 %all-reduce.3.cloned.1.call-start = ((), (), s32[]{:S(2)}) async-start(), calls=%async_computation.1 | async-start | bytes 3145728 | tf_op jit(solution)/shard_map/psum | solution.py:17
  100.6 226.2 %reduce-scatter.2.cloned.1.call-start = ((), (), s32[]{:S(2)}) async-start(), calls=%async_computation.2 | async-start | bytes 3784704 | tf_op jit(solution)/shard_map/reduce_scatter | solution.py:23
  158.1 0.7 copy-start.3
  158.1 168.8 %copy-start.1 = (bf16[1,16,3584]{2,1,0:T(8,128)(2,1)S(1)}, bf16[1,16,3584]{2,1,0:T(8,128)(2,1)}, u32[]{:S(2)}) copy-start(bf16[1,16,3584]{2,1,0:T(8,128)(2,1)} %param.5) | copy-start | bytes 344068
  158.1 268.7 %all-gather.4.cloned.1.call-start = ((), (), s32[]{:S(2)}) async-start(), calls=%async_computation.3 | async-start | bytes 3784704 | tf_op jit(solution)/shard_map/all_gather | solution.py:31
  328.4 144.4 %all-reduce.5.cloned.1.call-start = ((), (), s32[]{:S(2)}) async-start(), calls=%async_computation.4 | async-start | bytes 1572864 | tf_op jit(solution)/shard_map/psum | solution.py:42
  434.4 38.4 %copy-start = (f32[512,768]{1,0:T(8,128)S(1)}, f32[512,768]{1,0:T(8,128)}, u32[]{:S(2)}) copy-start(f32[512,768]{1,0:T(8,128)} %all-reduce.3.cloned.1.call-done) | copy-start | bytes 4718596
Sparse Core Ops, SparseCore 0:
  11.0 81.7 all-gather.5
  100.7 47.7 all-reduce.2
  158.2 168.5 reduce-scatter.1
  330.7 96.1 all-gather.3
  434.6 38.1 all-reduce.4
where the time goes:
time: 497 us
  waiting for transfers between devices  397 us (80%)
  matrix products  37.7 us (8%)
  blocking collectives  28.6 us (6%)
  between operations  13.8 us (3%)
  other arithmetic  10.2 us (2%)
  local copies, waits for them, and re-layouts  8.91 us (2%)
    reduce_scatter x1, waiting for transfers between devices, per_device(): lax.psum_scatter(jnp.dot(lat_rows, dec_local, preferred_element_type=jnp....  168 us
    all_gather x1, waiting for transfers between devices, per_device(): gathered = lax.all_gather(own_rows, 'latent', axis=0, tiled=True)  84.8 us
    all_gather x1, waiting for transfers between devices, per_device(): err_piece = lax.all_gather(err_grad, 'latent', axis=0, tiled=True)  66 us
    psum x1, waiting for transfers between devices, per_device(): pre_total, weight_sum = lax.psum((pre_part, row_norms), 'layer')  47.8 us
    psum x1, waiting for transfers between devices, per_device(): lax.psum(lat_part.astype(jnp.bfloat16), 'layer').astype(jnp.float32)  29.9 us
    psum x1, blocking collectives, per_device(): pre_total, weight_sum = lax.psum((pre_part, row_norms), 'layer')  28.6 us
  transfers between devices with their start and end apart: 5, of which 5 were waited for; matrix products, arithmetic and copies ran while one was open for 2% of the time, Pallas kernels for 0%

commit v1 on v0

v1 whole, which is shorter than its diff:
```python
import jax
import jax.numpy as jnp
from jax import lax
from jax.sharding import PartitionSpec as P

sparsity_weight = 0.5
sharpness = 4.0

SIZES = {"x": 4, "zh": 2, "y": 4}
STRIDES = {"x": 8, "zh": 4, "y": 1}


def latent_shift(value, axis, by):
    size, stride = SIZES[axis], STRIDES[axis]
    pairs = []
    for i in range(32):
        at = i // stride % size
        pairs.append((i, i + ((at + by) % size - at) * stride))
    return lax.ppermute(value, "latent", pairs)


def layer_swap(value, bit):
    return lax.ppermute(value, "layer", [(i, i ^ bit) for i in range(4)])


def gather_rows(rows, first, second):
    rows = jnp.concatenate([rows, latent_shift(rows, "zh", 1)], axis=0)
    for axis in (first, second):
        rows = jnp.concatenate([rows] + [latent_shift(rows, axis, -k) for k in (1, 2, 3)], axis=0)
    return rows


def scatter_sum(rows, first, second):
    for axis, size in ((second, 4), (first, 4), ("zh", 2)):
        step = rows.shape[0] // size
        total = rows[:step].astype(jnp.float32)
        for k in range(1, size):
            got = latent_shift(rows[k * step : (k + 1) * step], axis, k)
            total = total + got.astype(jnp.float32)
        rows = total if axis == "zh" else total.astype(jnp.bfloat16)
    return rows


def layer_scatter(part, upper_core, upper_z):
    half = part.shape[0] // 2
    low, high = part[:half], part[half:]
    keep, send = jnp.where(upper_core, high, low), jnp.where(upper_core, low, high)
    part = keep + layer_swap(send, 1)
    half //= 2
    low, high = part[:half], part[half:]
    keep, send = jnp.where(upper_z, high, low), jnp.where(upper_z, low, high)
    return keep + layer_swap(send.astype(jnp.bfloat16), 2).astype(jnp.float32)


def layer_gather(rows, upper_core, upper_z):
    for upper, bit in ((upper_z, 2), (upper_core, 1)):
        other = layer_swap(rows, bit)
        rows = jnp.concatenate(
            [jnp.where(upper, other, rows), jnp.where(upper, rows, other)], axis=0
        )
    return rows


def per_device(residuals, enc_weight, dec_weight, enc_bias, dec_bias):
    own_rows = residuals[0]
    enc_local = enc_weight[0]
    dec_local = dec_weight[0]
    layer = lax.axis_index("layer")
    upper_core, upper_z = layer % 2 == 1, layer >= 2

    row_norms = jnp.sqrt(jnp.sum(jnp.square(dec_local.astype(jnp.float32)), axis=1) + 1e-06)
    weight_sum = row_norms + layer_swap(row_norms, 1)
    weight_sum = weight_sum + layer_swap(weight_sum, 2)
    penalty = sparsity_weight * weight_sum[None, :]

    ways = (("y", "x"), ("x", "y"))
    halves = [own_rows[:8], own_rows[8:]]
    gathered = [gather_rows(h, *w) for h, w in zip(halves, ways)]
    latents, gates, errors, pre_grads = [], [], [], []
    for part in range(2):
        pre = jnp.dot(gathered[part], enc_local, preferred_element_type=jnp.float32)
        pre = layer_scatter(pre, upper_core, upper_z) + enc_bias[None, :]
        lat = (jax.nn.softplus(sharpness * pre) / sharpness).astype(jnp.bfloat16)
        gates.append(jax.nn.sigmoid(sharpness * pre))
        latents.append(layer_gather(lat, upper_core, upper_z))
    for part in range(2):
        rebuilt = jnp.dot(latents[part], dec_local, preferred_element_type=jnp.float32)
        rebuilt = scatter_sum(rebuilt.astype(jnp.bfloat16), *ways[part])
        misfit = rebuilt + dec_bias[0][None, :] - halves[part].astype(jnp.float32)
        error = (2.0 * misfit).astype(jnp.bfloat16)
        errors.append(gather_rows(error, *ways[part]))
    for part in range(2):
        back = lax.dot_general(
            errors[part], dec_local, (((1,), (1,)), ((), ())), preferred_element_type=jnp.float32
        )
        lat_grad = layer_scatter(back, upper_core, upper_z) + penalty
        pre_grads.append(
            layer_gather((lat_grad * gates[part]).astype(jnp.bfloat16), upper_core, upper_z)
        )
    all_latents = jnp.concatenate(latents, axis=0)
    act_sum = jnp.sum(all_latents.astype(jnp.float32), axis=0)
    dec_acc = lax.dot_general(
        all_latents,
        jnp.concatenate(errors, axis=0),
        (((0,), (0,)), ((), ())),
        preferred_element_type=jnp.float32,
    )
    penalty_term = (
        sparsity_weight * act_sum[:, None] * dec_local.astype(jnp.float32) / row_norms[:, None]
    )
    dec_grad = (dec_acc + penalty_term).astype(jnp.bfloat16)
    pre_grad = jnp.concatenate(pre_grads, axis=0)
    enc_grad = lax.dot_general(
        jnp.concatenate(gathered, axis=0),
        pre_grad,
        (((0,), (0,)), ((), ())),
        preferred_element_type=jnp.float32,
    ).astype(jnp.bfloat16)
    enc_bias_grad = jnp.sum(pre_grad.astype(jnp.float32), axis=0)
    return (enc_grad[None], dec_grad[None], enc_bias_grad)


def solution(mesh):
    in_specs = (
        P("layer", "latent", None),
        P("layer", None, "latent"),
        P("layer", "latent", None),
        P("latent"),
        P("layer", None),
    )
    out_specs = (P("layer", None, "latent"), P("layer", "latent", None), P("latent"))
    return jax.shard_map(
        per_device, mesh=mesh, in_specs=in_specs, out_specs=out_specs, check_vma=False
    )
```

time: 497 us -> 288 us (0.58)
  waiting for transfers between devices: 397 us -> 148 us
  starting transfers between devices: 0.2 us -> 82.2 us
  blocking collectives: 28.6 us -> 0 us
  between operations: 13.8 us -> 1.18 us
  local copies, waits for them, and re-layouts: 8.91 us -> 15.8 us
  matrix products: 37.7 us -> 31.6 us
    reduce_scatter x1 -> x0, waiting for transfers between devices: 168 us -> none  [per_device(): lax.psum_scatter(jnp.dot(lat_rows, dec_local, preferred_element_type=jnp....]
    all_gather x2 -> x0, waiting for transfers between devices: 151 us -> none  [the longest x1 84.8 us: per_device(): gathered = lax.all_gather(own_rows, 'latent', axis=0, tiled=True)]
    ppermute x0 -> x60, waiting for transfers between devices: none -> 148 us  [the longest x42 126 us: latent_shift(): return lax.ppermute(value, 'latent', pairs)]
    ppermute x0 -> x60, starting transfers between devices: none -> 82.2 us  [the longest x42 54.6 us: latent_shift(): return lax.ppermute(value, 'latent', pairs)]
    psum x2 -> x0, waiting for transfers between devices: 77.8 us -> none  [the longest x1 47.8 us: per_device(): pre_total, weight_sum = lax.psum((pre_part, row_norms), 'layer')]
    psum x1 -> x0, blocking collectives: 28.6 us -> none  [per_device(): pre_total, weight_sum = lax.psum((pre_part, row_norms), 'layer')]
    dot_general x5 -> x8, matrix products: 37.7 us -> 31.6 us  [the longest x2 8.43 us: per_device(): pre = jnp.dot(gathered[part], enc_local, preferred_element_type=jnp.float32)]
    unnamed x9 -> x47, local copies, waits for them, and re-layouts: 8.91 us -> 11.4 us
  transfers between devices with their start and end apart: 5 -> 60, of which waited for: 5 -> 32; matrix products, arithmetic and copies ran while one was open for 2% -> 12% of each run, Pallas kernels for 0% -> 0%
where the time goes in v1:
time: 288 us
  waiting for transfers between devices  148 us (51%)
  starting transfers between devices  82.2 us (29%)
  matrix products  31.6 us (11%)
  local copies, waits for them, and re-layouts  15.8 us (5%)
  other arithmetic  8.77 us (3%)
    ppermute x42, waiting for transfers between devices, latent_shift(): return lax.ppermute(value, 'latent', pairs)  126 us
    ppermute x42, starting transfers between devices, latent_shift(): return lax.ppermute(value, 'latent', pairs)  54.6 us
    ppermute x18, starting transfers between devices, layer_swap(): return lax.ppermute(value, 'layer', [(i, i ^ bit) for i in range(4)])  27.5 us
    ppermute x18, waiting for transfers between devices, layer_swap(): return lax.ppermute(value, 'layer', [(i, i ^ bit) for i in range(4)])  22.6 us
    unnamed x47, local copies, waits for them, and re-layouts  11.4 us
    dot_general x2, matrix products, per_device(): pre = jnp.dot(gathered[part], enc_local, preferred_element_type=jnp.float32)  8.43 us
    dot_general x1, matrix products, per_device(): lax.dot_general(jnp.concatenate(gathered, axis=0), pre_grad, (((0,), (0,)...  7.54 us
    dot_general x1, matrix products, per_device(): lax.dot_general(all_latents, jnp.concatenate(errors, axis=0), (((0,), (0,...  6.54 us
  transfers between devices with their start and end apart: 60, of which 32 were waited for; matrix products, arithmetic and copies ran while one was open for 12% of the time, Pallas kernels for 0%

profile of v1, /device:TPU:1, one launch (start us, length us, event | category | flops | bytes accessed | tf_op | source)
XLA Modules:
  0.0 287.7 jit_solution(1431682689176660755)
XLA Ops:
  2.1 4.4 %collective-permute-start = (bf16[8,3584]{1,0:T(8,128)(2,1)S(1)}, bf16[8,3584]{1,0:T(8,128)(2,1)S(1)}, u32[]{:S(2)}, u32[]{:S(2)}) collective-permute-start(bf16[8,3584]{1,0:T(8,128)(2,1)S(1)} %get-tuple-element.104), channel_id=1, source_target_pairs={{0,4},{1,5},{2,6},{3,7},{4,0},{5,1},{6,2},{7,3},{8,12},{9,13},{10,... | collective-permute-start | bytes 172040 | tf_op jit(solution)/shard_map/ppermute | solution.py:19
  9.5 2.6 collective-permute-start.2
  13.8 3.3 %collective-permute-done.1 = bf16[16,3584]{1,0:T(8,128)(2,1)S(1)} collective-permute-done((bf16[16,3584]{1,0:T(8,128)(2,1)S(1)}, bf16[16,3584]{1,0:T(8,128)(2,1)S(1)}, u32[]{:S(2)}, u32[]{:S(2)}) %collective-permute-start.1) | collective-permute-done | bytes 114720 | tf_op jit(solution)/shard_map/ppermute | solution.py:19
  19.1 2.5 collective-permute-start.4
  21.6 1.7 collective-permute-start.5
  23.3 7.0 %collective-permute-done.4 = bf16[64,3584]{1,0:T(8,128)(2,1)S(1)} collective-permute-done((bf16[64,3584]{1,0:T(8,128)(2,1)S(1)}, bf16[64,3584]{1,0:T(8,128)(2,1)S(1)}, u32[]{:S(2)}, u32[]{:S(2)}) %collective-permute-start.4) | collective-permute-done | bytes 458784 | tf_op jit(solution)/shard_map/ppermute | solution.py:19
  31.1 10.4 %collective-permute-done.5 = bf16[64,3584]{1,0:T(8,128)(2,1)S(1)} collective-permute-done((bf16[64,3584]{1,0:T(8,128)(2,1)S(1)}, bf16[64,3584]{1,0:T(8,128)(2,1)S(1)}, u32[]{:S(2)}, u32[]{:S(2)}) %collective-permute-start.5) | collective-permute-done | bytes 458784 | tf_op jit(solution)/shard_map/ppermute | solution.py:19
  43.3 4.1 %fusion.16 = f32[256,768]{1,0:T(8,128)S(1)} fusion(bf16[256,3584]{1,0:T(8,128)(2,1)S(1)} %get-tuple-element.37, bf16[1,3584,768]{2,1,0:T(8,128)(2,1)} %param.6), kind=kOutput, calls=%fused_computation.19 | convolution fusion | flops 1409286144 | bytes 8126464 | tf_op jit(solution)/shard_map/dot_general | solution.py:81
  47.5 3.2 %collective-permute-start.14 = (f32[128,768]{1,0:T(8,128)S(1)}, f32[128,768]{1,0:T(8,128)S(1)}, u32[]{:S(2)}, u32[]{:S(2)}) collective-permute-start(f32[128,768]{1,0:T(8,128)S(1)} %slice_select_fusion.3), channel_id=1, source_target_pairs={{0,32},{32,0},{64,96},{96,64},{1,33},{33,1},{65,97},{97,65},{2,34}... | collective-permute-start | bytes 1179656 | tf_op jit(solution)/shard_map/ppermute | solution.py:23
  53.0 3.3 %collective-permute-done.15 = bf16[64,768]{1,0:T(8,128)(2,1)S(1)} collective-permute-done((bf16[64,768]{1,0:T(8,128)(2,1)S(1)}, bf16[64,768]{1,0:T(8,128)(2,1)S(1)}, u32[]{:S(2)}, u32[]{:S(2)}) %collective-permute-start.15) | collective-permute-done | bytes 98336 | tf_op jit(solution)/shard_map/ppermute | solution.py:23
  57.2 2.7 collective-permute-done.16
  60.0 2.4 collective-permute-start.17
  63.6 4.3 %fusion.18 = bf16[256,3584]{1,0:T(8,128)(2,1)S(1)} fusion(bf16[1,768,3584]{2,1,0:T(8,128)(2,1)} %param.7, bf16[128,768]{1,0:T(8,128)(2,1)S(1)} %get-tuple-element.50, bf16[128,768]{1,0:T(8,128)(2,1)S(1)} %get-tuple-element.49), kind=kOutput, calls=%fused_computation.21 | convolution fusion | flops 1410990080 | bytes 7733248 | tf_op jit(solution)/shard_map/dot_general | solution.py:87
  68.9 2.7 collective-permute-start.20
  74.5 2.7 collective-permute-start.7
  79.4 2.6 collective-permute-done.18
  82.0 10.1 %collective-permute-done.19 = bf16[64,3584]{1,0:T(8,128)(2,1)} collective-permute-done((bf16[64,3584]{1,0:T(8,128)(2,1)S(1)}, bf16[64,3584]{1,0:T(8,128)(2,1)}, u32[]{:S(2)}, u32[]{:S(2)}) %collective-permute-start.19) | collective-permute-done | bytes 458784 | tf_op jit(solution)/shard_map/ppermute | solution.py:19
  93.7 2.7 collective-permute-start.23
  98.5 3.6 %collective-permute-done.22 = bf16[16,3584]{1,0:T(8,128)(2,1)S(1)} collective-permute-done((bf16[16,3584]{1,0:T(8,128)(2,1)S(1)}, bf16[16,3584]{1,0:T(8,128)(2,1)S(1)}, u32[]{:S(2)}, u32[]{:S(2)}) %collective-permute-start.22) | collective-permute-done | bytes 114720 | tf_op jit(solution)/shard_map/ppermute | solution.py:19
  102.1 2.9 collective-permute-start.24
  106.8 2.8 collective-permute-start.9
  111.7 1.8 collective-permute-done.8
  118.5 4.3 %collective-permute-done.25 = bf16[8,3584]{1,0:T(8,128)(2,1)S(1)} collective-permute-done((bf16[8,3584]{1,0:T(8,128)(2,1)S(1)}, bf16[8,3584]{1,0:T(8,128)(2,1)S(1)}, u32[]{:S(2)}, u32[]{:S(2)}) %collective-permute-start.25) | collective-permute-done | bytes 57376 | tf_op jit(solution)/shard_map/ppermute | solution.py:19
  123.4 1.9 collective-permute-start.27
  125.3 13.9 %collective-permute-done.11 = bf16[64,3584]{1,0:T(8,128)(2,1)S(1)} collective-permute-done((bf16[64,3584]{1,0:T(8,128)(2,1)S(1)}, bf16[64,3584]{1,0:T(8,128)(2,1)S(1)}, u32[]{:S(2)}, u32[]{:S(2)}) %collective-permute-start.11) | collective-permute-done | bytes 458784 | tf_op jit(solution)/shard_map/ppermute | solution.py:19
  139.2 3.4 %collective-permute-start.26 = (bf16[16,3584]{1,0:T(8,128)(2,1)S(1)}, bf16[16,3584]{1,0:T(8,128)(2,1)S(1)}, u32[]{:S(2)}, u32[]{:S(2)}) collective-permute-start(bf16[16,3584]{1,0:T(8,128)(2,1)S(1)} %pad_maximum_fusion.10), channel_id=1, source_target_pairs={{0,3},{1,0},{2,1},{3,2},{4,7},{5,4},{6,5},{7,6},{8,11},{9,8},{10,9... | collective-permute-start | bytes 344072 | tf_op jit(solution)/shard_map/ppermute | solution.py:19
  145.1 4.3 %fusion.14 = f32[256,768]{1,0:T(8,128)S(1)} fusion(bf16[256,3584]{1,0:T(8,128)(2,1)S(1)} %get-tuple-element.28, bf16[1,3584,768]{2,1,0:T(8,128)(2,1)} %param.6), kind=kOutput, calls=%fused_computation.17 | convolution fusion | flops 1409286144 | bytes 8126464 | tf_op jit(solution)/shard_map/dot_general | solution.py:81
  153.0 3.2 %collective-permute-done.39 = bf16[64,768]{1,0:T(8,128)(2,1)S(1)} collective-permute-done((bf16[64,768]{1,0:T(8,128)(2,1)S(1)}, bf16[64,768]{1,0:T(8,128)(2,1)S(1)}, u32[]{:S(2)}, u32[]{:S(2)}) %collective-permute-start.39) | collective-permute-done | bytes 98336 | tf_op jit(solution)/shard_map/ppermute | solution.py:23
  157.2 2.7 collective-permute-done.40
  160.0 2.4 collective-permute-start.41
  162.7 2.5 collective-permute-start.30
  168.0 2.7 collective-permute-start.44
  170.7 15.3 %collective-permute-done.29 = bf16[64,3584]{1,0:T(8,128)(2,1)S(1)} collective-permute-done((bf16[64,3584]{1,0:T(8,128)(2,1)S(1)}, bf16[64,3584]{1,0:T(8,128)(2,1)S(1)}, u32[]{:S(2)}, u32[]{:S(2)}) %collective-permute-start.29) | collective-permute-done | bytes 458784 | tf_op jit(solution)/shard_map/ppermute | solution.py:19
  186.0 12.3 %collective-permute-done.43 = bf16[64,3584]{1,0:T(8,128)(2,1)S(1)} collective-permute-done((bf16[64,3584]{1,0:T(8,128)(2,1)S(1)}, bf16[64,3584]{1,0:T(8,128)(2,1)S(1)}, u32[]{:S(2)}, u32[]{:S(2)}) %collective-permute-start.43) | collective-permute-done | bytes 458784 | tf_op jit(solution)/shard_map/ppermute | solution.py:19
  198.6 2.4 collective-permute-start.45
  204.6 4.5 %collective-permute-done.46 = bf16[16,3584]{1,0:T(8,128)(2,1)S(1)} collective-permute-done((bf16[16,3584]{1,0:T(8,128)(2,1)S(1)}, bf16[16,3584]{1,0:T(8,128)(2,1)S(1)}, u32[]{:S(2)}, u32[]{:S(2)}) %collective-permute-start.46) | collective-permute-done | bytes 114720 | tf_op jit(solution)/shard_map/ppermute | solution.py:19
  209.5 4.3 %collective-permute-done.48 = bf16[8,3584]{1,0:T(8,128)(2,1)S(1)} collective-permute-done((bf16[8,3584]{1,0:T(8,128)(2,1)S(1)}, bf16[8,3584]{1,0:T(8,128)(2,1)S(1)}, u32[]{:S(2)}, u32[]{:S(2)}) %collective-permute-start.48) | collective-permute-done | bytes 57376 | tf_op jit(solution)/shard_map/ppermute | solution.py:19
  214.1 4.3 %collective-permute-done.49 = bf16[8,3584]{1,0:T(8,128)(2,1)S(1)} collective-permute-done((bf16[8,3584]{1,0:T(8,128)(2,1)S(1)}, bf16[8,3584]{1,0:T(8,128)(2,1)S(1)}, u32[]{:S(2)}, u32[]{:S(2)}) %collective-permute-start.49) | collective-permute-done | bytes 57376 | tf_op jit(solution)/shard_map/ppermute | solution.py:19
  218.6 2.2 collective-permute-start.51
  221.2 4.0 %collective-permute-done.50 = bf16[16,3584]{1,0:T(8,128)(2,1)S(1)} collective-permute-done((bf16[16,3584]{1,0:T(8,128)(2,1)S(1)}, bf16[16,3584]{1,0:T(8,128)(2,1)S(1)}, u32[]{:S(2)}, u32[]{:S(2)}) %collective-permute-start.50) | collective-permute-done | bytes 114720 | tf_op jit(solution)/shard_map/ppermute | solution.py:19
  227.1 5.3 %collective-permute-start.32 = (f32[128,768]{1,0:T(8,128)S(1)}, f32[128,768]{1,0:T(8,128)S(1)}, u32[]{:S(2)}, u32[]{:S(2)}) collective-permute-start(f32[128,768]{1,0:T(8,128)S(1)} %slice_select_fusion.2), channel_id=1, source_target_pairs={{0,32},{32,0},{64,96},{96,64},{1,33},{33,1},{65,97},{97,65},{2,34}... | collective-permute-start | bytes 1179656 | tf_op jit(solution)/shard_map/ppermute | solution.py:23
  232.4 1.7 collective-permute-start.55
  234.3 20.4 %collective-permute-done.54 = bf16[64,3584]{1,0:T(8,128)(2,1)S(1)} collective-permute-done((bf16[64,3584]{1,0:T(8,128)(2,1)S(1)}, bf16[64,3584]{1,0:T(8,128)(2,1)S(1)}, u32[]{:S(2)}, u32[]{:S(2)}) %collective-permute-start.54) | collective-permute-done | bytes 458784 | tf_op jit(solution)/shard_map/ppermute | solution.py:19
  260.5 2.3 collective-permute-done.33
  262.8 2.1 collective-permute-done.57
  266.0 6.5 %fusion.4 = bf16[1,768,3584]{2,1,0:T(8,128)(2,1)} fusion(bf16[512,3584]{1,0:T(8,128)(2,1)S(1)} %get-tuple-element.13, bf16[1,768,3584]{2,1,0:T(8,128)(2,1)S(1)} %bitcast.55, f32[768]{0:T(1024)} %add_sqrt_fusion, f32[768]{0:T(1024)S(1)} %broadcast_multiply_fusion, bf16[128,768]{1,0:T(8,128)(2,1)S(1)} %get-tuple-element.48, ...), kind=kOutput, calls=%fused_computation.7 | convolution fusion | flops 2835480576 | bytes 15472640 | tf_op jit(solution)/shard_map/dot_general | solution.py:102
  276.0 2.3 collective-permute-start.59
  280.2 7.5 %fusion.5 = bf16[1,3584,768]{2,1,0:T(8,128)(2,1)} fusion(bf16[512,3584]{1,0:T(8,128)(2,1)} %get-tuple-element.29, bf16[128,768]{1,0:T(8,128)(2,1)S(1)} %get-tuple-element.46, bf16[128,768]{1,0:T(8,128)(2,1)S(1)} %get-tuple-element.45, bf16[128,768]{1,0:T(8,128)(2,1)S(1)} %get-tuple-element.44, bf16[128,768]{1,0:T(8,128)(2,1)S(1)} %get-tuple-element.43), kind=kOutput, calls=%fused_computation.8 | convolution fusion | flops 2824470528 | bytes 9961472 | tf_op jit(solution)/shard_map/dot_general | solution.py:113
  (185 shorter events, 63.8 us)
Async XLA Ops:
  2.1 6.0 %collective-permute-start = (bf16[8,3584]{1,0:T(8,128)(2,1)S(1)}, bf16[8,3584]{1,0:T(8,128)(2,1)S(1)}, u32[]{:S(2)}, u32[]{:S(2)}) collective-permute-start(bf16[8,3584]{1,0:T(8,128)(2,1)S(1)} %get-tuple-element.104), channel_id=1, source_target_pairs={{0,4},{1,5},{2,6},{3,7},{4,0},{5,1},{6,2},{7,3},{8,12},{9,13},{10,... | collective-permute-start | bytes 172040 | tf_op jit(solution)/shard_map/ppermute | solution.py:19
  8.1 10.3 %collective-permute-start.3 = (bf16[16,3584]{1,0:T(8,128)(2,1)S(1)}, bf16[16,3584]{1,0:T(8,128)(2,1)S(1)}, u32[]{:S(2)}, u32[]{:S(2)}) collective-permute-start(bf16[16,3584]{1,0:T(8,128)(2,1)S(1)} %pad_maximum_fusion.8), channel_id=1, source_target_pairs={{0,1},{1,2},{2,3},{3,0},{4,5},{5,6},{6,7},{7,4},{8,9},{9,10},{10,1... | collective-permute-start | bytes 344072 | tf_op jit(solution)/shard_map/ppermute | solution.py:19
  9.5 8.3 %collective-permute-start.2 = (bf16[16,3584]{1,0:T(8,128)(2,1)S(1)}, bf16[16,3584]{1,0:T(8,128)(2,1)S(1)}, u32[]{:S(2)}, u32[]{:S(2)}) collective-permute-start(bf16[16,3584]{1,0:T(8,128)(2,1)S(1)} %pad_maximum_fusion.8), channel_id=1, source_target_pairs={{0,2},{1,3},{2,0},{3,1},{4,6},{5,7},{6,4},{7,5},{8,10},{9,11},{10,... | collective-permute-start | bytes 344072 | tf_op jit(solution)/shard_map/ppermute | solution.py:19
  12.1 5.0 %collective-permute-start.1 = (bf16[16,3584]{1,0:T(8,128)(2,1)S(1)}, bf16[16,3584]{1,0:T(8,128)(2,1)S(1)}, u32[]{:S(2)}, u32[]{:S(2)}) collective-permute-start(bf16[16,3584]{1,0:T(8,128)(2,1)S(1)} %pad_maximum_fusion.8), channel_id=1, source_target_pairs={{0,3},{1,0},{2,1},{3,2},{4,7},{5,4},{6,5},{7,6},{8,11},{9,8},{10,9... | collective-permute-start | bytes 344072 | tf_op jit(solution)/shard_map/ppermute | solution.py:19
  19.1 11.2 %collective-permute-start.4 = (bf16[64,3584]{1,0:T(8,128)(2,1)S(1)}, bf16[64,3584]{1,0:T(8,128)(2,1)S(1)}, u32[]{:S(2)}, u32[]{:S(2)}) collective-permute-start(bf16[64,3584]{1,0:T(8,128)(2,1)S(1)} %get-tuple-element.93), channel_id=1, source_target_pairs={{0,24},{1,25},{2,26},{3,27},{4,28},{5,29},{6,30},{7,31},{8,0},{9,1... | collective-permute-start | bytes 1376264 | tf_op jit(solution)/shard_map/ppermute | solution.py:19
  21.6 20.8 %collective-permute-start.6 = (bf16[64,3584]{1,0:T(8,128)(2,1)S(1)}, bf16[64,3584]{1,0:T(8,128)(2,1)S(1)}, u32[]{:S(2)}, u32[]{:S(2)}) collective-permute-start(bf16[64,3584]{1,0:T(8,128)(2,1)S(1)} %get-tuple-element.93), channel_id=1, source_target_pairs={{0,8},{1,9},{2,10},{3,11},{4,12},{5,13},{6,14},{7,15},{8,16},{9,17... | collective-permute-start | bytes 1376264 | tf_op jit(solution)/shard_map/ppermute | solution.py:19
  21.6 20.0 %collective-permute-start.5 = (bf16[64,3584]{1,0:T(8,128)(2,1)S(1)}, bf16[64,3584]{1,0:T(8,128)(2,1)S(1)}, u32[]{:S(2)}, u32[]{:S(2)}) collective-permute-start(bf16[64,3584]{1,0:T(8,128)(2,1)S(1)} %get-tuple-element.93), channel_id=1, source_target_pairs={{0,16},{1,17},{2,18},{3,19},{4,20},{5,21},{6,22},{7,23},{8,24},{9,... | collective-permute-start | bytes 1376264 | tf_op jit(solution)/shard_map/ppermute | solution.py:19
  47.5 4.6 %collective-permute-start.14 = (f32[128,768]{1,0:T(8,128)S(1)}, f32[128,768]{1,0:T(8,128)S(1)}, u32[]{:S(2)}, u32[]{:S(2)}) collective-permute-start(f32[128,768]{1,0:T(8,128)S(1)} %slice_select_fusion.3), channel_id=1, source_target_pairs={{0,32},{32,0},{64,96},{96,64},{1,33},{33,1},{65,97},{97,65},{2,34}... | collective-permute-start | bytes 1179656 | tf_op jit(solution)/shard_map/ppermute | solution.py:23
  68.9 13.2 %collective-permute-start.18 = (bf16[64,3584]{1,0:T(8,128)(2,1)}, bf16[64,3584]{1,0:T(8,128)(2,1)S(1)}, u32[]{:S(2)}, u32[]{:S(2)}) collective-permute-start(bf16[64,3584]{1,0:T(8,128)(2,1)} %get-tuple-element.10), channel_id=1, source_target_pairs={{0,8},{1,9},{2,10},{3,11},{4,12},{5,13},{6,14},{7,15},{8,16},{9,17... | collective-permute-start | bytes 1376264 | tf_op jit(solution)/shard_map/ppermute | solution.py:19
  68.9 13.2 %collective-permute-start.20 = (bf16[64,3584]{1,0:T(8,128)(2,1)}, bf16[64,3584]{1,0:T(8,128)(2,1)}, u32[]{:S(2)}, u32[]{:S(2)}) collective-permute-start(bf16[64,3584]{1,0:T(8,128)(2,1)} %get-tuple-element.11), channel_id=1, source_target_pairs={{0,24},{1,25},{2,26},{3,27},{4,28},{5,29},{6,30},{7,31},{8,0},{9,1... | collective-permute-start | bytes 1376264 | tf_op jit(solution)/shard_map/ppermute | solution.py:19
  71.6 20.6 %collective-permute-start.19 = (bf16[64,3584]{1,0:T(8,128)(2,1)S(1)}, bf16[64,3584]{1,0:T(8,128)(2,1)}, u32[]{:S(2)}, u32[]{:S(2)}) collective-permute-start(bf16[64,3584]{1,0:T(8,128)(2,1)S(1)} %get-tuple-element.12), channel_id=1, source_target_pairs={{0,16},{1,17},{2,18},{3,19},{4,20},{5,21},{6,22},{7,23},{8,24},{9,... | collective-permute-start | bytes 1376264 | tf_op jit(solution)/shard_map/ppermute | solution.py:19
  74.5 30.5 %collective-permute-start.7 = (bf16[8,3584]{1,0:T(8,128)(2,1)}, bf16[8,3584]{1,0:T(8,128)(2,1)}, u32[]{:S(2)}, u32[]{:S(2)}) collective-permute-start(bf16[8,3584]{1,0:T(8,128)(2,1)} %get-tuple-element.103), channel_id=1, source_target_pairs={{0,4},{1,5},{2,6},{3,7},{4,0},{5,1},{6,2},{7,3},{8,12},{9,13},{10,... | collective-permute-start | bytes 172040 | tf_op jit(solution)/shard_map/ppermute | solution.py:19
  78.6 18.4 %collective-permute-start.35 = (f32[768]{0:T(1024)S(1)}, f32[768]{0:T(1024)S(1)}, u32[]{:S(2)}, u32[]{:S(2)}) collective-permute-start(f32[768]{0:T(1024)S(1)} %fusion.38), channel_id=1, source_target_pairs={{0,64},{32,96},{64,0},{96,32},{1,65},{33,97},{65,1},{97,33},{2,66}... | collective-permute-start | bytes 9224 | tf_op jit(solution)/shard_map/ppermute | solution.py:23
  93.6 4.9 %collective-permute-start.21 = (bf16[16,3584]{1,0:T(8,128)(2,1)S(1)}, bf16[16,3584]{1,0:T(8,128)(2,1)S(1)}, u32[]{:S(2)}, u32[]{:S(2)}) collective-permute-start(bf16[16,3584]{1,0:T(8,128)(2,1)S(1)} %get-tuple-element.34), channel_id=1, source_target_pairs={{0,1},{1,2},{2,3},{3,0},{4,5},{5,6},{6,7},{7,4},{8,9},{9,10},{10,1... | collective-permute-start | bytes 344072 | tf_op jit(solution)/shard_map/ppermute | solution.py:19
  93.7 4.8 %collective-permute-start.23 = (bf16[16,3584]{1,0:T(8,128)(2,1)S(1)}, bf16[16,3584]{1,0:T(8,128)(2,1)S(1)}, u32[]{:S(2)}, u32[]{:S(2)}) collective-permute-start(bf16[16,3584]{1,0:T(8,128)(2,1)S(1)} %get-tuple-element.35), channel_id=1, source_target_pairs={{0,3},{1,0},{2,1},{3,2},{4,7},{5,4},{6,5},{7,6},{8,11},{9,8},{10,9... | collective-permute-start | bytes 344072 | tf_op jit(solution)/shard_map/ppermute | solution.py:19
  96.3 5.7 %collective-permute-start.22 = (bf16[16,3584]{1,0:T(8,128)(2,1)S(1)}, bf16[16,3584]{1,0:T(8,128)(2,1)S(1)}, u32[]{:S(2)}, u32[]{:S(2)}) collective-permute-start(bf16[16,3584]{1,0:T(8,128)(2,1)S(1)} %get-tuple-element.36), channel_id=1, source_target_pairs={{0,2},{1,3},{2,0},{3,1},{4,6},{5,7},{6,4},{7,5},{8,10},{9,11},{10,... | collective-permute-start | bytes 344072 | tf_op jit(solution)/shard_map/ppermute | solution.py:19
  102.1 7.5 %collective-permute-start.24 = (bf16[8,3584]{1,0:T(8,128)(2,1)S(1)}, bf16[8,3584]{1,0:T(8,128)(2,1)S(1)}, u32[]{:S(2)}, u32[]{:S(2)}) collective-permute-start(bf16[8,3584]{1,0:T(8,128)(2,1)S(1)} %slice.173), channel_id=1, source_target_pairs={{0,4},{1,5},{2,6},{3,7},{4,0},{5,1},{6,2},{7,3},{8,12},{9,13},{10,... | collective-permute-start | bytes 172040 | tf_op jit(solution)/shard_map/ppermute | solution.py:19
  105.8 9.0 %collective-permute-start.10 = (bf16[16,3584]{1,0:T(8,128)(2,1)S(1)}, bf16[16,3584]{1,0:T(8,128)(2,1)S(1)}, u32[]{:S(2)}, u32[]{:S(2)}) collective-permute-start(bf16[16,3584]{1,0:T(8,128)(2,1)S(1)} %pad_maximum_fusion.9), channel_id=1, source_target_pairs={{0,8},{1,9},{2,10},{3,11},{4,12},{5,13},{6,14},{7,15},{8,16},{9,17... | collective-permute-start | bytes 344072 | tf_op jit(solution)/shard_map/ppermute | solution.py:19
  106.8 7.4 %collective-permute-start.9 = (bf16[16,3584]{1,0:T(8,128)(2,1)S(1)}, bf16[16,3584]{1,0:T(8,128)(2,1)S(1)}, u32[]{:S(2)}, u32[]{:S(2)}) collective-permute-start(bf16[16,3584]{1,0:T(8,128)(2,1)S(1)} %pad_maximum_fusion.9), channel_id=1, source_target_pairs={{0,16},{1,17},{2,18},{3,19},{4,20},{5,21},{6,22},{7,23},{8,24},{9,... | collective-permute-start | bytes 344072 | tf_op jit(solution)/shard_map/ppermute | solution.py:19
  115.6 28.7 %collective-permute-start.13 = (bf16[64,3584]{1,0:T(8,128)(2,1)S(1)}, bf16[64,3584]{1,0:T(8,128)(2,1)S(1)}, u32[]{:S(2)}, u32[]{:S(2)}) collective-permute-start(bf16[64,3584]{1,0:T(8,128)(2,1)S(1)} %get-tuple-element.79), channel_id=1, source_target_pairs={{0,1},{1,2},{2,3},{3,0},{4,5},{5,6},{6,7},{7,4},{8,9},{9,10},{10,1... | collective-permute-start | bytes 1376264 | tf_op jit(solution)/shard_map/ppermute | solution.py:19
  115.6 27.9 %collective-permute-start.12 = (bf16[64,3584]{1,0:T(8,128)(2,1)S(1)}, bf16[64,3584]{1,0:T(8,128)(2,1)S(1)}, u32[]{:S(2)}, u32[]{:S(2)}) collective-permute-start(bf16[64,3584]{1,0:T(8,128)(2,1)S(1)} %get-tuple-element.79), channel_id=1, source_target_pairs={{0,2},{1,3},{2,0},{3,1},{4,6},{5,7},{6,4},{7,5},{8,10},{9,11},{10,... | collective-permute-start | bytes 1376264 | tf_op jit(solution)/shard_map/ppermute | solution.py:19
  117.1 22.1 %collective-permute-start.11 = (bf16[64,3584]{1,0:T(8,128)(2,1)S(1)}, bf16[64,3584]{1,0:T(8,128)(2,1)S(1)}, u32[]{:S(2)}, u32[]{:S(2)}) collective-permute-start(bf16[64,3584]{1,0:T(8,128)(2,1)S(1)} %get-tuple-element.79), channel_id=1, source_target_pairs={{0,3},{1,0},{2,1},{3,2},{4,7},{5,4},{6,5},{7,6},{8,11},{9,8},{10,9... | collective-permute-start | bytes 1376264 | tf_op jit(solution)/shard_map/ppermute | solution.py:19
  118.2 4.5 %collective-permute-start.25 = (bf16[8,3584]{1,0:T(8,128)(2,1)S(1)}, bf16[8,3584]{1,0:T(8,128)(2,1)S(1)}, u32[]{:S(2)}, u32[]{:S(2)}) collective-permute-start(bf16[8,3584]{1,0:T(8,128)(2,1)S(1)} %get-tuple-element.90), channel_id=1, source_target_pairs={{0,4},{1,5},{2,6},{3,7},{4,0},{5,1},{6,2},{7,3},{8,12},{9,13},{10,... | collective-permute-start | bytes 172040 | tf_op jit(solution)/shard_map/ppermute | solution.py:19
  122.8 39.6 %collective-permute-start.28 = (bf16[16,3584]{1,0:T(8,128)(2,1)S(1)}, bf16[16,3584]{1,0:T(8,128)(2,1)S(1)}, u32[]{:S(2)}, u32[]{:S(2)}) collective-permute-start(bf16[16,3584]{1,0:T(8,128)(2,1)S(1)} %pad_maximum_fusion.10), channel_id=1, source_target_pairs={{0,1},{1,2},{2,3},{3,0},{4,5},{5,6},{6,7},{7,4},{8,9},{9,10},{10,1... | collective-permute-start | bytes 344072 | tf_op jit(solution)/shard_map/ppermute | solution.py:19
  123.4 33.7 %collective-permute-start.27 = (bf16[16,3584]{1,0:T(8,128)(2,1)S(1)}, bf16[16,3584]{1,0:T(8,128)(2,1)S(1)}, u32[]{:S(2)}, u32[]{:S(2)}) collective-permute-start(bf16[16,3584]{1,0:T(8,128)(2,1)S(1)} %pad_maximum_fusion.10), channel_id=1, source_target_pairs={{0,2},{1,3},{2,0},{3,1},{4,6},{5,7},{6,4},{7,5},{8,10},{9,11},{10,... | collective-permute-start | bytes 344072 | tf_op jit(solution)/shard_map/ppermute | solution.py:19
  139.2 13.7 %collective-permute-start.26 = (bf16[16,3584]{1,0:T(8,128)(2,1)S(1)}, bf16[16,3584]{1,0:T(8,128)(2,1)S(1)}, u32[]{:S(2)}, u32[]{:S(2)}) collective-permute-start(bf16[16,3584]{1,0:T(8,128)(2,1)S(1)} %pad_maximum_fusion.10), channel_id=1, source_target_pairs={{0,3},{1,0},{2,1},{3,2},{4,7},{5,4},{6,5},{7,6},{8,11},{9,8},{10,9... | collective-permute-start | bytes 344072 | tf_op jit(solution)/shard_map/ppermute | solution.py:19
  160.0 6.2 %collective-permute-start.41 = (bf16[128,768]{1,0:T(8,128)(2,1)S(1)}, bf16[128,768]{1,0:T(8,128)(2,1)S(1)}, u32[]{:S(2)}, u32[]{:S(2)}) collective-permute-start(bf16[128,768]{1,0:T(8,128)(2,1)S(1)} %pad_maximum_fusion.4), channel_id=1, source_target_pairs={{0,32},{32,0},{64,96},{96,64},{1,33},{33,1},{65,97},{97,65},{2,34}... | collective-permute-start | bytes 589832 | tf_op jit(solution)/shard_map/ppermute | solution.py:23
  162.4 47.1 %collective-permute-start.31 = (bf16[64,3584]{1,0:T(8,128)(2,1)S(1)}, bf16[64,3584]{1,0:T(8,128)(2,1)S(1)}, u32[]{:S(2)}, u32[]{:S(2)}) collective-permute-start(bf16[64,3584]{1,0:T(8,128)(2,1)S(1)} %get-tuple-element.70), channel_id=1, source_target_pairs={{0,8},{1,9},{2,10},{3,11},{4,12},{5,13},{6,14},{7,15},{8,16},{9,17... | collective-permute-start | bytes 1376264 | tf_op jit(solution)/shard_map/ppermute | solution.py:19
  162.7 40.9 %collective-permute-start.30 = (bf16[64,3584]{1,0:T(8,128)(2,1)S(1)}, bf16[64,3584]{1,0:T(8,128)(2,1)S(1)}, u32[]{:S(2)}, u32[]{:S(2)}) collective-permute-start(bf16[64,3584]{1,0:T(8,128)(2,1)S(1)} %get-tuple-element.70), channel_id=1, source_target_pairs={{0,16},{1,17},{2,18},{3,19},{4,20},{5,21},{6,22},{7,23},{8,24},{9,... | collective-permute-start | bytes 1376264 | tf_op jit(solution)/shard_map/ppermute | solution.py:19
  165.2 20.8 %collective-permute-start.29 = (bf16[64,3584]{1,0:T(8,128)(2,1)S(1)}, bf16[64,3584]{1,0:T(8,128)(2,1)S(1)}, u32[]{:S(2)}, u32[]{:S(2)}) collective-permute-start(bf16[64,3584]{1,0:T(8,128)(2,1)S(1)} %get-tuple-element.70), channel_id=1, source_target_pairs={{0,24},{1,25},{2,26},{3,27},{4,28},{5,29},{6,30},{7,31},{8,0},{9,1... | collective-permute-start | bytes 1376264 | tf_op jit(solution)/shard_map/ppermute | solution.py:19
  167.9 18.1 %collective-permute-start.42 = (bf16[64,3584]{1,0:T(8,128)(2,1)S(1)}, bf16[64,3584]{1,0:T(8,128)(2,1)S(1)}, u32[]{:S(2)}, u32[]{:S(2)}) collective-permute-start(bf16[64,3584]{1,0:T(8,128)(2,1)S(1)} %get-tuple-element.7), channel_id=1, source_target_pairs={{0,1},{1,2},{2,3},{3,0},{4,5},{5,6},{6,7},{7,4},{8,9},{9,10},{10,1... | collective-permute-start | bytes 1376264 | tf_op jit(solution)/shard_map/ppermute | solution.py:19
  168.0 18.0 %collective-permute-start.44 = (bf16[64,3584]{1,0:T(8,128)(2,1)S(1)}, bf16[64,3584]{1,0:T(8,128)(2,1)S(1)}, u32[]{:S(2)}, u32[]{:S(2)}) collective-permute-start(bf16[64,3584]{1,0:T(8,128)(2,1)S(1)} %get-tuple-element.8), channel_id=1, source_target_pairs={{0,3},{1,0},{2,1},{3,2},{4,7},{5,4},{6,5},{7,6},{8,11},{9,8},{10,9... | collective-permute-start | bytes 1376264 | tf_op jit(solution)/shard_map/ppermute | solution.py:19
  186.0 12.4 %collective-permute-start.43 = (bf16[64,3584]{1,0:T(8,128)(2,1)S(1)}, bf16[64,3584]{1,0:T(8,128)(2,1)S(1)}, u32[]{:S(2)}, u32[]{:S(2)}) collective-permute-start(bf16[64,3584]{1,0:T(8,128)(2,1)S(1)} %get-tuple-element.9), channel_id=1, source_target_pairs={{0,2},{1,3},{2,0},{3,1},{4,6},{5,7},{6,4},{7,5},{8,10},{9,11},{10,... | collective-permute-start | bytes 1376264 | tf_op jit(solution)/shard_map/ppermute | solution.py:19
  198.6 6.0 %collective-permute-start.45 = (bf16[16,3584]{1,0:T(8,128)(2,1)S(1)}, bf16[16,3584]{1,0:T(8,128)(2,1)S(1)}, u32[]{:S(2)}, u32[]{:S(2)}) collective-permute-start(bf16[16,3584]{1,0:T(8,128)(2,1)S(1)} %get-tuple-element.25), channel_id=1, source_target_pairs={{0,8},{1,9},{2,10},{3,11},{4,12},{5,13},{6,14},{7,15},{8,16},{9,17... | collective-permute-start | bytes 344072 | tf_op jit(solution)/shard_map/ppermute | solution.py:19
  202.5 6.7 %collective-permute-start.46 = (bf16[16,3584]{1,0:T(8,128)(2,1)S(1)}, bf16[16,3584]{1,0:T(8,128)(2,1)S(1)}, u32[]{:S(2)}, u32[]{:S(2)}) collective-permute-start(bf16[16,3584]{1,0:T(8,128)(2,1)S(1)} %get-tuple-element.27), channel_id=1, source_target_pairs={{0,16},{1,17},{2,18},{3,19},{4,20},{5,21},{6,22},{7,23},{8,24},{9,... | collective-permute-start | bytes 344072 | tf_op jit(solution)/shard_map/ppermute | solution.py:19
  209.2 4.6 %collective-permute-start.48 = (bf16[8,3584]{1,0:T(8,128)(2,1)S(1)}, bf16[8,3584]{1,0:T(8,128)(2,1)S(1)}, u32[]{:S(2)}, u32[]{:S(2)}) collective-permute-start(bf16[8,3584]{1,0:T(8,128)(2,1)S(1)} %slice.191), channel_id=1, source_target_pairs={{0,4},{1,5},{2,6},{3,7},{4,0},{5,1},{6,2},{7,3},{8,12},{9,13},{10,... | collective-permute-start | bytes 172040 | tf_op jit(solution)/shard_map/ppermute | solution.py:19
  213.8 4.6 %collective-permute-start.49 = (bf16[8,3584]{1,0:T(8,128)(2,1)S(1)}, bf16[8,3584]{1,0:T(8,128)(2,1)S(1)}, u32[]{:S(2)}, u32[]{:S(2)}) collective-permute-start(bf16[8,3584]{1,0:T(8,128)(2,1)S(1)} %get-tuple-element.4), channel_id=1, source_target_pairs={{0,4},{1,5},{2,6},{3,7},{4,0},{5,1},{6,2},{7,3},{8,12},{9,13},{10,... | collective-permute-start | bytes 172040 | tf_op jit(solution)/shard_map/ppermute | solution.py:19
  218.5 6.8 %collective-permute-start.52 = (bf16[16,3584]{1,0:T(8,128)(2,1)S(1)}, bf16[16,3584]{1,0:T(8,128)(2,1)S(1)}, u32[]{:S(2)}, u32[]{:S(2)}) collective-permute-start(bf16[16,3584]{1,0:T(8,128)(2,1)S(1)} %pad_maximum_fusion.11), channel_id=1, source_target_pairs={{0,8},{1,9},{2,10},{3,11},{4,12},{5,13},{6,14},{7,15},{8,16},{9,17... | collective-permute-start | bytes 344072 | tf_op jit(solution)/shard_map/ppermute | solution.py:19
  218.6 6.7 %collective-permute-start.51 = (bf16[16,3584]{1,0:T(8,128)(2,1)S(1)}, bf16[16,3584]{1,0:T(8,128)(2,1)S(1)}, u32[]{:S(2)}, u32[]{:S(2)}) collective-permute-start(bf16[16,3584]{1,0:T(8,128)(2,1)S(1)} %pad_maximum_fusion.11), channel_id=1, source_target_pairs={{0,16},{1,17},{2,18},{3,19},{4,20},{5,21},{6,22},{7,23},{8,24},{9,... | collective-permute-start | bytes 344072 | tf_op jit(solution)/shard_map/ppermute | solution.py:19
  220.7 4.5 %collective-permute-start.50 = (bf16[16,3584]{1,0:T(8,128)(2,1)S(1)}, bf16[16,3584]{1,0:T(8,128)(2,1)S(1)}, u32[]{:S(2)}, u32[]{:S(2)}) collective-permute-start(bf16[16,3584]{1,0:T(8,128)(2,1)S(1)} %pad_maximum_fusion.11), channel_id=1, source_target_pairs={{0,24},{1,25},{2,26},{3,27},{4,28},{5,29},{6,30},{7,31},{8,0},{9,1... | collective-permute-start | bytes 344072 | tf_op jit(solution)/shard_map/ppermute | solution.py:19
  225.4 8.8 %collective-permute-start.53 = (bf16[64,3584]{1,0:T(8,128)(2,1)S(1)}, bf16[64,3584]{1,0:T(8,128)(2,1)S(1)}, u32[]{:S(2)}, u32[]{:S(2)}) collective-permute-start(bf16[64,3584]{1,0:T(8,128)(2,1)S(1)} %get-tuple-element.61), channel_id=1, source_target_pairs={{0,3},{1,0},{2,1},{3,2},{4,7},{5,4},{6,5},{7,6},{8,11},{9,8},{10,9... | collective-permute-start | bytes 1376264 | tf_op jit(solution)/shard_map/ppermute | solution.py:19
  227.1 31.1 %collective-permute-start.32 = (f32[128,768]{1,0:T(8,128)S(1)}, f32[128,768]{1,0:T(8,128)S(1)}, u32[]{:S(2)}, u32[]{:S(2)}) collective-permute-start(f32[128,768]{1,0:T(8,128)S(1)} %slice_select_fusion.2), channel_id=1, source_target_pairs={{0,32},{32,0},{64,96},{96,64},{1,33},{33,1},{65,97},{97,65},{2,34}... | collective-permute-start | bytes 1179656 | tf_op jit(solution)/shard_map/ppermute | solution.py:23
  232.4 23.1 %collective-permute-start.55 = (bf16[64,3584]{1,0:T(8,128)(2,1)S(1)}, bf16[64,3584]{1,0:T(8,128)(2,1)S(1)}, u32[]{:S(2)}, u32[]{:S(2)}) collective-permute-start(bf16[64,3584]{1,0:T(8,128)(2,1)S(1)} %get-tuple-element.61), channel_id=1, source_target_pairs={{0,1},{1,2},{2,3},{3,0},{4,5},{5,6},{6,7},{7,4},{8,9},{9,10},{10,1... | collective-permute-start | bytes 1376264 | tf_op jit(solution)/shard_map/ppermute | solution.py:19
  234.2 20.5 %collective-permute-start.54 = (bf16[64,3584]{1,0:T(8,128)(2,1)S(1)}, bf16[64,3584]{1,0:T(8,128)(2,1)S(1)}, u32[]{:S(2)}, u32[]{:S(2)}) collective-permute-start(bf16[64,3584]{1,0:T(8,128)(2,1)S(1)} %get-tuple-element.61), channel_id=1, source_target_pairs={{0,2},{1,3},{2,0},{3,1},{4,6},{5,7},{6,4},{7,5},{8,10},{9,11},{10,... | collective-permute-start | bytes 1376264 | tf_op jit(solution)/shard_map/ppermute | solution.py:19
  258.3 4.5 %collective-permute-start.33 = (bf16[64,768]{1,0:T(8,128)(2,1)S(1)}, bf16[64,768]{1,0:T(8,128)(2,1)S(1)}, u32[]{:S(2)}, u32[]{:S(2)}) collective-permute-start(bf16[64,768]{1,0:T(8,128)(2,1)S(1)} %select_convert_fusion.2), channel_id=1, source_target_pairs={{0,64},{32,96},{64,0},{96,32},{1,65},{33,97},{65,1},{97,33},{2,66}... | collective-permute-start | bytes 294920 | tf_op jit(solution)/shard_map/ppermute | solution.py:23
  259.7 5.3 %collective-permute-start.57 = (bf16[64,768]{1,0:T(8,128)(2,1)S(1)}, bf16[64,768]{1,0:T(8,128)(2,1)S(1)}, u32[]{:S(2)}, u32[]{:S(2)}) collective-permute-start(bf16[64,768]{1,0:T(8,128)(2,1)S(1)} %select_convert_fusion), channel_id=1, source_target_pairs={{0,64},{32,96},{64,0},{96,32},{1,65},{33,97},{65,1},{97,33},{2,66}... | collective-permute-start | bytes 294920 | tf_op jit(solution)/shard_map/ppermute | solution.py:23
  265.1 8.1 %collective-permute-start.36 = (bf16[64,768]{1,0:T(8,128)(2,1)S(1)}, bf16[64,768]{1,0:T(8,128)(2,1)S(1)}, u32[]{:S(2)}, u32[]{:S(2)}) collective-permute-start(bf16[64,768]{1,0:T(8,128)(2,1)S(1)} %get-tuple-element.121), channel_id=1, source_target_pairs={{0,64},{32,96},{64,0},{96,32},{1,65},{33,97},{65,1},{97,33},{2,66}... | collective-permute-start | bytes 294920 | tf_op jit(solution)/shard_map/ppermute | solution.py:23
  273.3 5.1 %collective-permute-start.37 = (bf16[128,768]{1,0:T(8,128)(2,1)S(1)}, bf16[128,768]{1,0:T(8,128)(2,1)S(1)}, u32[]{:S(2)}, u32[]{:S(2)}) collective-permute-start(bf16[128,768]{1,0:T(8,128)(2,1)S(1)} %pad_maximum_fusion.3), channel_id=1, source_target_pairs={{0,32},{32,0},{64,96},{96,64},{1,33},{33,1},{65,97},{97,65},{2,34}... | collective-permute-start | bytes 589832 | tf_op jit(solution)/shard_map/ppermute | solution.py:23
  (22 other events, 162.1 us)

commit v2 on v0

v2 whole, which is shorter than its diff:
```python
import jax
import jax.numpy as jnp
from jax import lax
from jax.sharding import PartitionSpec as P

sparsity_weight = 0.5
sharpness = 4.0

SIZES = {"x": 4, "zh": 2, "y": 4}
STRIDES = {"x": 8, "zh": 4, "y": 1}
ORDER = (("y", "x"), ("x", "y"))


def shift(value, slot, stage, by):
    pairs = []
    for layer in range(4):
        axis = "zh" if stage == "zh" else ORDER[(layer + slot) % 2][stage]
        size, stride = SIZES[axis], STRIDES[axis]
        for i in range(32):
            at = i // stride % size
            pairs.append((layer * 32 + i, layer * 32 + i + ((at + by) % size - at) * stride))
    return lax.ppermute(value, ("layer", "latent"), pairs)


def layer_swap(value, bit):
    return lax.ppermute(value, "layer", [(i, i ^ bit) for i in range(4)])


def join(*rows):
    return jnp.concatenate(rows, axis=0)


def rounded(value):
    return lax.reduce_precision(value, 8, 7)


def wide(value):
    return value.astype(jnp.float32)


def narrow(value):
    return value.astype(jnp.bfloat16)


def ring_gather(rows, slot, stage):
    half = rows.shape[0] // 2
    after, before = shift(rows, slot, stage, -1), shift(rows, slot, stage, 1)
    far = shift(after[:half], slot, stage, -1), shift(before[half:], slot, stage, 1)
    return join(rows, after, *far, before)


def near_gather(rows, slot, stage):
    far, after, before = (shift(rows, slot, stage, by) for by in (2, -1, 1))
    return join(rows, after, far, before)


def ring_scatter(rows, slot, stage):
    n = rows.shape[0] // 4
    half = n // 2
    up = shift(rows[n + half : 2 * n + half], slot, stage, 1)
    down = shift(rows[2 * n + half : 3 * n + half], slot, stage, -1)
    up_far = narrow(wide(rows[n : n + half]) + wide(up[half:]))
    down_far = narrow(wide(rows[3 * n + half :]) + wide(down[:half]))
    up_far, down_far = shift(up_far, slot, stage, 1), shift(down_far, slot, stage, -1)
    return (
        wide(rows[:n])
        + join(wide(up_far), wide(up[:half]))
        + join(wide(down[half:]), wide(down_far))
    )


def near_scatter(rows, slot, stage):
    n = rows.shape[0] // 4
    total = wide(rows[:n])
    for k in (2, 1, 3):
        total = total + wide(shift(rows[k * n : (k + 1) * n], slot, stage, k))
    return total


def gather_rows(pair, slot):
    return ring_gather(near_gather(pair, slot, 0), slot, 1)


def scatter_sum(rows, slot):
    pair = rounded(near_scatter(narrow(ring_scatter(rows, slot, 1)), slot, 0))
    other = wide(shift(narrow(pair), slot, "zh", 1))
    half = pair.shape[0] // 2
    return pair + join(other[half:], other[:half])


def layer_sum(keep, send):
    part = rounded(keep + layer_swap(send, 1))
    return part + wide(layer_swap(narrow(part), 2))


def per_device(residuals, enc_weight, dec_weight, enc_bias, dec_bias):
    own_rows = residuals[0]
    enc_local = enc_weight[0]
    dec_local = dec_weight[0]
    upper = lax.axis_index("layer") % 2 == 1

    row_norms = jnp.sqrt(jnp.sum(jnp.square(wide(dec_local)), axis=1) + 1e-06)
    weight_sum = row_norms + layer_swap(row_norms, 1)
    weight_sum = weight_sum + layer_swap(weight_sum, 2)
    penalty = sparsity_weight * weight_sum[None, :]

    other_rows = shift(own_rows, 0, "zh", 1)
    low, high = join(own_rows[:8], other_rows[:8]), join(own_rows[8:], other_rows[8:])
    pairs = [jnp.where(upper, high, low), jnp.where(upper, low, high)]
    gathered = [gather_rows(pairs[slot], slot) for slot in (0, 1)]
    gathered = list(lax.optimization_barrier(tuple(gathered)))
    pre = [jnp.dot(rows, enc_local, preferred_element_type=jnp.float32) for rows in gathered]
    pre = layer_sum(*pre) + enc_bias[None, :]
    kept = narrow(jax.nn.softplus(sharpness * pre) / sharpness)
    gate = jax.nn.sigmoid(sharpness * pre)
    latents = [kept, layer_swap(kept, 1)]
    latents = list(lax.optimization_barrier(tuple(latents)))
    errors = []
    for slot in (0, 1):
        rebuilt = jnp.dot(latents[slot], dec_local, preferred_element_type=jnp.float32)
        rebuilt = scatter_sum(narrow(rebuilt), slot)
        misfit = rebuilt + dec_bias[0][None, :] - wide(pairs[slot])
        errors.append(narrow(2.0 * misfit))
    errors = list(lax.optimization_barrier(tuple(errors)))
    errors = [gather_rows(errors[slot], slot) for slot in (0, 1)]
    errors = list(lax.optimization_barrier(tuple(errors)))
    back = [
        lax.dot_general(
            rows, dec_local, (((1,), (1,)), ((), ())), preferred_element_type=jnp.float32
        )
        for rows in errors
    ]
    lat_grad = layer_sum(*back) + penalty
    kept = narrow(lat_grad * gate)
    pre_grads = [kept, layer_swap(kept, 1)]
    act_sum = jnp.sum(wide(join(*latents)), axis=0)
    dec_acc = lax.dot_general(
        join(*latents),
        join(*errors),
        (((0,), (0,)), ((), ())),
        preferred_element_type=jnp.float32,
    )
    penalty_term = sparsity_weight * act_sum[:, None] * wide(dec_local) / row_norms[:, None]
    dec_grad = narrow(dec_acc + penalty_term)
    enc_grad = narrow(
        lax.dot_general(
            join(*gathered),
            join(*pre_grads),
            (((0,), (0,)), ((), ())),
            preferred_element_type=jnp.float32,
        )
    )
    enc_bias_grad = jnp.sum(wide(pre_grads[0]), axis=0) + jnp.sum(wide(pre_grads[1]), axis=0)
    return (enc_grad[None], dec_grad[None], enc_bias_grad)


def solution(mesh):
    in_specs = (
        P("layer", "latent", None),
        P("layer", None, "latent"),
        P("layer", "latent", None),
        P("latent"),
        P("layer", None),
    )
    out_specs = (P("layer", None, "latent"), P("layer", "latent", None), P("latent"))
    return jax.shard_map(
        per_device, mesh=mesh, in_specs=in_specs, out_specs=out_specs, check_vma=False
    )
```

time: 497 us -> 181 us (0.36)
  waiting for transfers between devices: 397 us -> 74.4 us
  starting transfers between devices: 0.2 us -> 76.7 us
  blocking collectives: 28.6 us -> 0 us
  matrix products: 37.7 us -> 22.3 us
  between operations: 13.8 us -> 1.37 us
  local copies, waits for them, and re-layouts: 8.91 us -> 1.96 us
  other arithmetic: 10.2 us -> 3.97 us
    reduce_scatter x1 -> x0, waiting for transfers between devices: 168 us -> none  [per_device(): lax.psum_scatter(jnp.dot(lat_rows, dec_local, preferred_element_type=jnp....]
    all_gather x2 -> x0, waiting for transfers between devices: 151 us -> none  [the longest x1 84.8 us: per_device(): gathered = lax.all_gather(own_rows, 'latent', axis=0, tiled=True)]
    psum x2 -> x0, waiting for transfers between devices: 77.8 us -> none  [the longest x1 47.8 us: per_device(): pre_total, weight_sum = lax.psum((pre_part, row_norms), 'layer')]
    ppermute x0 -> x53, starting transfers between devices: none -> 76.7 us  [the longest x45 56.5 us: shift(): return lax.ppermute(value, ('layer', 'latent'), pairs)]
    ppermute x0 -> x53, waiting for transfers between devices: none -> 74.4 us  [the longest x45 50.4 us: shift(): return lax.ppermute(value, ('layer', 'latent'), pairs)]
    psum x1 -> x0, blocking collectives: 28.6 us -> none  [per_device(): pre_total, weight_sum = lax.psum((pre_part, row_norms), 'layer')]
    dot_general x5 -> x8, matrix products: 37.7 us -> 22.3 us  [the longest x2 5.73 us: per_device(): jnp.dot(latents[slot], dec_local, preferred_element_type=jnp.float32)]
    unnamed x9 -> x42, local copies, waits for them, and re-layouts: 8.91 us -> 0.5 us
  transfers between devices with their start and end apart: 5 -> 53, of which waited for: 5 -> 28; matrix products, arithmetic and copies ran while one was open for 2% -> 6% of each run, Pallas kernels for 0% -> 0%
where the time goes in v2:
time: 181 us
  starting transfers between devices  76.7 us (42%)
  waiting for transfers between devices  74.4 us (41%)
  matrix products  22.3 us (12%)
  other arithmetic  3.97 us (2%)
  local copies, waits for them, and re-layouts  1.96 us (1%)
    ppermute x45, starting transfers between devices, shift(): return lax.ppermute(value, ('layer', 'latent'), pairs)  56.5 us
    ppermute x45, waiting for transfers between devices, shift(): return lax.ppermute(value, ('layer', 'latent'), pairs)  50.4 us
    ppermute x8, waiting for transfers between devices, layer_swap(): return lax.ppermute(value, 'layer', [(i, i ^ bit) for i in range(4)])  24 us
    ppermute x8, starting transfers between devices, layer_swap(): return lax.ppermute(value, 'layer', [(i, i ^ bit) for i in range(4)])  20.2 us
    dot_general x2, matrix products, per_device(): jnp.dot(latents[slot], dec_local, preferred_element_type=jnp.float32)  5.73 us
    dot_general x1, matrix products, per_device(): lax.dot_general(join(*latents), join(*errors), (((0,), (0,)), ((), ())),...  5.3 us
    dot_general x1, matrix products, per_device(): lax.dot_general(join(*gathered), join(*pre_grads), (((0,), (0,)), ((), ()...  4.83 us
  transfers between devices with their start and end apart: 53, of which 28 were waited for; matrix products, arithmetic and copies ran while one was open for 6% of the time, Pallas kernels for 0%

profile of v2, /device:TPU:1, one launch (start us, length us, event | category | flops | bytes accessed | tf_op | source)
XLA Modules:
  0.0 180.6 jit_solution(4104873942909770761)
XLA Ops:
  0.6 4.5 %collective-permute-start = (bf16[16,3584]{1,0:T(8,128)(2,1)}, bf16[16,3584]{1,0:T(8,128)(2,1)S(1)}, u32[]{:S(2)}, u32[]{:S(2)}) collective-permute-start(bf16[16,3584]{1,0:T(8,128)(2,1)} %bitcast.50), channel_id=1, source_target_pairs={{0,4},{1,5},{2,6},{3,7},{4,0},{5,1},{6,2},{7,3},{8,12},{9,13},{10,... | collective-permute-start | bytes 344072 | tf_op jit(solution)/shard_map/ppermute | solution.py:22
  6.0 2.2 %collective-permute-done = bf16[16,3584]{1,0:T(8,128)(2,1)S(1)} collective-permute-done((bf16[16,3584]{1,0:T(8,128)(2,1)}, bf16[16,3584]{1,0:T(8,128)(2,1)S(1)}, u32[]{:S(2)}, u32[]{:S(2)}) %collective-permute-start) | collective-permute-done | bytes 114720 | tf_op jit(solution)/shard_map/ppermute | solution.py:22
  9.6 2.5 %collective-permute-start.2 = (bf16[16,3584]{1,0:T(8,128)(2,1)S(1)}, bf16[16,3584]{1,0:T(8,128)(2,1)S(1)}, u32[]{:S(2)}, u32[]{:S(2)}) collective-permute-start(bf16[16,3584]{1,0:T(8,128)(2,1)S(1)} %get-tuple-element.40), channel_id=1, source_target_pairs={{0,2},{1,3},{2,0},{3,1},{4,6},{5,7},{6,4},{7,5},{8,10},{9,11},{10,... | collective-permute-start | bytes 344072 | tf_op jit(solution)/shard_map/ppermute | solution.py:22
  14.5 2.6 %collective-permute-start.9 = (bf16[16,3584]{1,0:T(8,128)(2,1)S(1)}, bf16[16,3584]{1,0:T(8,128)(2,1)S(1)}, u32[]{:S(2)}, u32[]{:S(2)}) collective-permute-start(bf16[16,3584]{1,0:T(8,128)(2,1)S(1)} %get-tuple-element.22), channel_id=1, source_target_pairs={{0,16},{1,17},{2,18},{3,19},{4,20},{5,21},{6,22},{7,23},{8,24},{9,... | collective-permute-start | bytes 344072 | tf_op jit(solution)/shard_map/ppermute | solution.py:22
  18.7 2.3 %collective-permute-start.4 = (bf16[64,3584]{1,0:T(8,128)(2,1)S(1)}, bf16[64,3584]{1,0:T(8,128)(2,1)S(1)}, u32[]{:S(2)}, u32[]{:S(2)}) collective-permute-start(bf16[64,3584]{1,0:T(8,128)(2,1)S(1)} %pad_maximum_fusion), channel_id=1, source_target_pairs={{0,24},{1,25},{2,26},{3,27},{4,28},{5,29},{6,30},{7,31},{8,0},{9,1... | collective-permute-start | bytes 1376264 | tf_op jit(solution)/shard_map/ppermute | solution.py:22
  21.5 2.3 %collective-permute-start.11 = (bf16[64,3584]{1,0:T(8,128)(2,1)S(1)}, bf16[64,3584]{1,0:T(8,128)(2,1)S(1)}, u32[]{:S(2)}, u32[]{:S(2)}) collective-permute-start(bf16[64,3584]{1,0:T(8,128)(2,1)S(1)} %pad_maximum_fusion.1), channel_id=1, source_target_pairs={{0,3},{1,0},{2,1},{3,2},{4,7},{5,4},{6,5},{7,6},{8,11},{9,8},{10,9... | collective-permute-start | bytes 1376264 | tf_op jit(solution)/shard_map/ppermute | solution.py:22
  23.9 3.2 %collective-permute-done.6 = bf16[64,3584]{1,0:T(8,128)(2,1)S(1)} collective-permute-done((bf16[64,3584]{1,0:T(8,128)(2,1)S(1)}, bf16[64,3584]{1,0:T(8,128)(2,1)S(1)}, u32[]{:S(2)}, u32[]{:S(2)}) %collective-permute-start.6) | collective-permute-done | bytes 458784 | tf_op jit(solution)/shard_map/ppermute | solution.py:22
  27.2 2.7 %collective-permute-start.5 = (bf16[32,3584]{1,0:T(8,128)(2,1)S(1)}, bf16[32,3584]{1,0:T(8,128)(2,1)S(1)}, u32[]{:S(2)}, u32[]{:S(2)}) collective-permute-start(bf16[32,3584]{1,0:T(8,128)(2,1)S(1)} %slice.178), channel_id=1, source_target_pairs={{0,24},{1,25},{2,26},{3,27},{4,28},{5,29},{6,30},{7,31},{8,0},{9,1... | collective-permute-start | bytes 688136 | tf_op jit(solution)/shard_map/ppermute | solution.py:22
  30.0 4.5 %collective-permute-done.13 = bf16[64,3584]{1,0:T(8,128)(2,1)S(1)} collective-permute-done((bf16[64,3584]{1,0:T(8,128)(2,1)S(1)}, bf16[64,3584]{1,0:T(8,128)(2,1)S(1)}, u32[]{:S(2)}, u32[]{:S(2)}) %collective-permute-start.13) | collective-permute-done | bytes 458784 | tf_op jit(solution)/shard_map/ppermute | solution.py:22
  34.6 2.7 %collective-permute-start.12 = (bf16[32,3584]{1,0:T(8,128)(2,1)S(1)}, bf16[32,3584]{1,0:T(8,128)(2,1)S(1)}, u32[]{:S(2)}, u32[]{:S(2)}) collective-permute-start(bf16[32,3584]{1,0:T(8,128)(2,1)S(1)} %slice.180), channel_id=1, source_target_pairs={{0,3},{1,0},{2,1},{3,2},{4,7},{5,4},{6,5},{7,6},{8,11},{9,8},{10,9... | collective-permute-start | bytes 688136 | tf_op jit(solution)/shard_map/ppermute | solution.py:22
  37.5 3.6 %collective-permute-done.12 = bf16[32,3584]{1,0:T(8,128)(2,1)S(1)} collective-permute-done((bf16[32,3584]{1,0:T(8,128)(2,1)S(1)}, bf16[32,3584]{1,0:T(8,128)(2,1)S(1)}, u32[]{:S(2)}, u32[]{:S(2)}) %collective-permute-start.12) | collective-permute-done | bytes 229408 | tf_op jit(solution)/shard_map/ppermute | solution.py:22
  42.1 1.6 fusion.14
  43.7 4.1 %collective-permute-start.15 = (f32[256,768]{1,0:T(8,128)S(1)}, f32[256,768]{1,0:T(8,128)S(1)}, u32[]{:S(2)}, u32[]{:S(2)}) collective-permute-start(f32[256,768]{1,0:T(8,128)S(1)} %fusion.14), channel_id=1, source_target_pairs={{0,32},{32,0},{64,96},{96,64},{1,33},{33,1},{65,97},{97,65},{2,34}... | collective-permute-start | bytes 2359304 | tf_op jit(solution)/shard_map/ppermute | solution.py:26
  47.8 1.9 %collective-permute-done.15 = f32[256,768]{1,0:T(8,128)S(1)} collective-permute-done((f32[256,768]{1,0:T(8,128)S(1)}, f32[256,768]{1,0:T(8,128)S(1)}, u32[]{:S(2)}, u32[]{:S(2)}) %collective-permute-start.15) | collective-permute-done | bytes 786464 | tf_op jit(solution)/shard_map/ppermute | solution.py:26
  49.7 1.6 fusion.67
  52.3 9.4 %collective-permute-done.16 = bf16[256,768]{1,0:T(8,128)(2,1)S(1)} collective-permute-done((bf16[256,768]{1,0:T(8,128)(2,1)S(1)}, bf16[256,768]{1,0:T(8,128)(2,1)S(1)}, u32[]{:S(2)}, u32[]{:S(2)}) %collective-permute-start.16) | collective-permute-done | bytes 393248 | tf_op jit(solution)/shard_map/ppermute | solution.py:26
  64.9 4.1 %fusion.21 = bf16[256,3584]{1,0:T(8,128)(2,1)S(1)} fusion(bf16[256,768]{1,0:T(8,128)(2,1)S(1)} %collective-permute-done.17, bf16[1,768,3584]{2,1,0:T(8,128)(2,1)} %param.7), kind=kOutput, calls=%fused_computation.22 | convolution fusion | flops 1410203648 | bytes 7733248 | tf_op jit(solution)/shard_map/dot_general | solution.py:120
  70.7 1.6 fusion.18
  72.4 3.2 %collective-permute-start.20 = (bf16[64,3584]{1,0:T(8,128)(2,1)S(1)}, bf16[64,3584]{1,0:T(8,128)(2,1)S(1)}, u32[]{:S(2)}, u32[]{:S(2)}) collective-permute-start(bf16[64,3584]{1,0:T(8,128)(2,1)S(1)} %get-tuple-element.31), channel_id=1, source_target_pairs={{0,24},{1,25},{2,26},{3,27},{4,28},{5,29},{6,30},{7,31},{8,0},{9,1... | collective-permute-start | bytes 1376264 | tf_op jit(solution)/shard_map/ppermute | solution.py:22
  76.8 1.9 %collective-permute-done.26 = bf16[64,3584]{1,0:T(8,128)(2,1)S(1)} collective-permute-done((bf16[64,3584]{1,0:T(8,128)(2,1)S(1)}, bf16[64,3584]{1,0:T(8,128)(2,1)S(1)}, u32[]{:S(2)}, u32[]{:S(2)}) %collective-permute-start.26) | collective-permute-done | bytes 458784 | tf_op jit(solution)/shard_map/ppermute | solution.py:22
  80.4 3.1 %collective-permute-done.20 = bf16[64,3584]{1,0:T(8,128)(2,1)S(1)} collective-permute-done((bf16[64,3584]{1,0:T(8,128)(2,1)S(1)}, bf16[64,3584]{1,0:T(8,128)(2,1)S(1)}, u32[]{:S(2)}, u32[]{:S(2)}) %collective-permute-start.20) | collective-permute-done | bytes 458784 | tf_op jit(solution)/shard_map/ppermute | solution.py:22
  83.5 3.4 %collective-permute-done.18 = bf16[64,3584]{1,0:T(8,128)(2,1)S(1)} collective-permute-done((bf16[64,3584]{1,0:T(8,128)(2,1)S(1)}, bf16[64,3584]{1,0:T(8,128)(2,1)S(1)}, u32[]{:S(2)}, u32[]{:S(2)}) %collective-permute-start.18) | collective-permute-done | bytes 458784 | tf_op jit(solution)/shard_map/ppermute | solution.py:22
  88.9 2.4 %collective-permute-start.32 = (bf16[16,3584]{1,0:T(8,128)(2,1)S(1)}, bf16[16,3584]{1,0:T(8,128)(2,1)S(1)}, u32[]{:S(2)}, u32[]{:S(2)}) collective-permute-start(bf16[16,3584]{1,0:T(8,128)(2,1)S(1)} %get-tuple-element.34), channel_id=1, source_target_pairs={{0,24},{1,25},{2,26},{3,27},{4,28},{5,29},{6,30},{7,31},{8,0},{9,1... | collective-permute-start | bytes 344072 | tf_op jit(solution)/shard_map/ppermute | solution.py:22
  91.3 2.3 %collective-permute-done.21 = bf16[32,3584]{1,0:T(8,128)(2,1)S(1)} collective-permute-done((bf16[32,3584]{1,0:T(8,128)(2,1)S(1)}, bf16[32,3584]{1,0:T(8,128)(2,1)S(1)}, u32[]{:S(2)}, u32[]{:S(2)}) %collective-permute-start.21) | collective-permute-done | bytes 229408 | tf_op jit(solution)/shard_map/ppermute | solution.py:22
  93.7 2.2 %collective-permute-done.19 = bf16[32,3584]{1,0:T(8,128)(2,1)S(1)} collective-permute-done((bf16[32,3584]{1,0:T(8,128)(2,1)S(1)}, bf16[32,3584]{1,0:T(8,128)(2,1)S(1)}, u32[]{:S(2)}, u32[]{:S(2)}) %collective-permute-start.19) | collective-permute-done | bytes 229408 | tf_op jit(solution)/shard_map/ppermute | solution.py:22
  97.8 2.9 %collective-permute-start.33 = (bf16[16,3584]{1,0:T(8,128)(2,1)S(1)}, bf16[16,3584]{1,0:T(8,128)(2,1)S(1)}, u32[]{:S(2)}, u32[]{:S(2)}) collective-permute-start(bf16[16,3584]{1,0:T(8,128)(2,1)S(1)} %fusion.56), channel_id=1, source_target_pairs={{0,4},{1,5},{2,6},{3,7},{4,0},{5,1},{6,2},{7,3},{8,12},{9,13},{10,... | collective-permute-start | bytes 344072 | tf_op jit(solution)/shard_map/ppermute | solution.py:22
  100.8 2.0 %collective-permute-done.22 = bf16[16,3584]{1,0:T(8,128)(2,1)S(1)} collective-permute-done((bf16[16,3584]{1,0:T(8,128)(2,1)S(1)}, bf16[16,3584]{1,0:T(8,128)(2,1)S(1)}, u32[]{:S(2)}, u32[]{:S(2)}) %collective-permute-start.22) | collective-permute-done | bytes 114720 | tf_op jit(solution)/shard_map/ppermute | solution.py:22
  102.8 2.5 %collective-permute-done.23 = bf16[16,3584]{1,0:T(8,128)(2,1)S(1)} collective-permute-done((bf16[16,3584]{1,0:T(8,128)(2,1)S(1)}, bf16[16,3584]{1,0:T(8,128)(2,1)S(1)}, u32[]{:S(2)}, u32[]{:S(2)}) %collective-permute-start.23) | collective-permute-done | bytes 114720 | tf_op jit(solution)/shard_map/ppermute | solution.py:22
  105.3 2.9 %collective-permute-start.25 = (bf16[16,3584]{1,0:T(8,128)(2,1)S(1)}, bf16[16,3584]{1,0:T(8,128)(2,1)S(1)}, u32[]{:S(2)}, u32[]{:S(2)}) collective-permute-start(bf16[16,3584]{1,0:T(8,128)(2,1)S(1)} %fusion.55), channel_id=1, source_target_pairs={{0,4},{1,5},{2,6},{3,7},{4,0},{5,1},{6,2},{7,3},{8,12},{9,13},{10,... | collective-permute-start | bytes 344072 | tf_op jit(solution)/shard_map/ppermute | solution.py:22
  108.3 2.9 %collective-permute-done.25 = bf16[16,3584]{1,0:T(8,128)(2,1)S(1)} collective-permute-done((bf16[16,3584]{1,0:T(8,128)(2,1)S(1)}, bf16[16,3584]{1,0:T(8,128)(2,1)S(1)}, u32[]{:S(2)}, u32[]{:S(2)}) %collective-permute-start.25) | collective-permute-done | bytes 114720 | tf_op jit(solution)/shard_map/ppermute | solution.py:22
  114.2 4.0 %collective-permute-done.34 = bf16[16,3584]{1,0:T(8,128)(2,1)S(1)} collective-permute-done((bf16[16,3584]{1,0:T(8,128)(2,1)S(1)}, bf16[16,3584]{1,0:T(8,128)(2,1)S(1)}, u32[]{:S(2)}, u32[]{:S(2)}) %collective-permute-start.34) | collective-permute-done | bytes 114720 | tf_op jit(solution)/shard_map/ppermute | solution.py:22
  118.3 1.5 collective-permute-start.39
  121.1 1.9 %collective-permute-done.41 = bf16[16,3584]{1,0:T(8,128)(2,1)S(1)} collective-permute-done((bf16[16,3584]{1,0:T(8,128)(2,1)S(1)}, bf16[16,3584]{1,0:T(8,128)(2,1)S(1)}, u32[]{:S(2)}, u32[]{:S(2)}) %collective-permute-start.41) | collective-permute-done | bytes 114720 | tf_op jit(solution)/shard_map/ppermute | solution.py:22
  123.8 2.0 %collective-permute-start.44 = (bf16[64,3584]{1,0:T(8,128)(2,1)S(1)}, bf16[64,3584]{1,0:T(8,128)(2,1)S(1)}, u32[]{:S(2)}, u32[]{:S(2)}) collective-permute-start(bf16[64,3584]{1,0:T(8,128)(2,1)S(1)} %get-tuple-element.41), channel_id=1, source_target_pairs={{0,3},{1,0},{2,1},{3,2},{4,7},{5,4},{6,5},{7,6},{8,11},{9,8},{10,9... | collective-permute-start | bytes 1376264 | tf_op jit(solution)/shard_map/ppermute | solution.py:22
  127.8 1.5 collective-permute-done.37
  129.3 1.5 collective-permute-start.38
  130.7 2.0 %collective-permute-done.46 = bf16[64,3584]{1,0:T(8,128)(2,1)S(1)} collective-permute-done((bf16[64,3584]{1,0:T(8,128)(2,1)S(1)}, bf16[64,3584]{1,0:T(8,128)(2,1)S(1)}, u32[]{:S(2)}, u32[]{:S(2)}) %collective-permute-start.46) | collective-permute-done | bytes 458784 | tf_op jit(solution)/shard_map/ppermute | solution.py:22
  134.2 3.5 %collective-permute-start.45 = (bf16[32,3584]{1,0:T(8,128)(2,1)S(1)}, bf16[32,3584]{1,0:T(8,128)(2,1)S(1)}, u32[]{:S(2)}, u32[]{:S(2)}) collective-permute-start(bf16[32,3584]{1,0:T(8,128)(2,1)S(1)} %slice.214), channel_id=1, source_target_pairs={{0,3},{1,0},{2,1},{3,2},{4,7},{5,4},{6,5},{7,6},{8,11},{9,8},{10,9... | collective-permute-start | bytes 688136 | tf_op jit(solution)/shard_map/ppermute | solution.py:22
  137.8 2.8 %collective-permute-done.45 = bf16[32,3584]{1,0:T(8,128)(2,1)S(1)} collective-permute-done((bf16[32,3584]{1,0:T(8,128)(2,1)S(1)}, bf16[32,3584]{1,0:T(8,128)(2,1)S(1)}, u32[]{:S(2)}, u32[]{:S(2)}) %collective-permute-start.45) | collective-permute-done | bytes 229408 | tf_op jit(solution)/shard_map/ppermute | solution.py:22
  140.7 1.6 fusion.6
  142.3 9.3 %collective-permute-start.48 = (f32[256,768]{1,0:T(8,128)S(1)}, f32[256,768]{1,0:T(8,128)S(1)}, u32[]{:S(2)}, u32[]{:S(2)}) collective-permute-start(f32[256,768]{1,0:T(8,128)S(1)} %fusion.6), channel_id=1, source_target_pairs={{0,32},{32,0},{64,96},{96,64},{1,33},{33,1},{65,97},{97,65},{2,34}... | collective-permute-start | bytes 2359304 | tf_op jit(solution)/shard_map/ppermute | solution.py:26
  151.8 1.8 %collective-permute-done.50 = f32[768]{0:T(1024)S(1)} collective-permute-done((f32[768]{0:T(1024)S(1)}, f32[768]{0:T(1024)S(1)}, u32[]{:S(2)}, u32[]{:S(2)}) %collective-permute-start.50) | collective-permute-done | bytes 3104 | tf_op jit(solution)/shard_map/ppermute | solution.py:26
  154.5 1.6 collective-permute-done.51
  156.1 1.6 fusion.68
  158.9 8.0 %collective-permute-done.49 = bf16[256,768]{1,0:T(8,128)(2,1)S(1)} collective-permute-done((bf16[256,768]{1,0:T(8,128)(2,1)S(1)}, bf16[256,768]{1,0:T(8,128)(2,1)S(1)}, u32[]{:S(2)}, u32[]{:S(2)}) %collective-permute-start.49) | collective-permute-done | bytes 393248 | tf_op jit(solution)/shard_map/ppermute | solution.py:26
  167.3 2.5 %collective-permute-start.52 = (bf16[256,768]{1,0:T(8,128)(2,1)S(1)}, bf16[256,768]{1,0:T(8,128)(2,1)S(1)}, u32[]{:S(2)}, u32[]{:S(2)}) collective-permute-start(bf16[256,768]{1,0:T(8,128)(2,1)S(1)} %get-tuple-element.20), channel_id=1, source_target_pairs={{0,32},{32,0},{64,96},{96,64},{1,33},{33,1},{65,97},{97,65},{2,34}... | collective-permute-start | bytes 1179656 | tf_op jit(solution)/shard_map/ppermute | solution.py:26
  169.8 5.3 %fusion.4 = bf16[1,768,3584]{2,1,0:T(8,128)(2,1)} fusion(bf16[512,768]{1,0:T(8,128)(2,1)S(1)} %constant_dynamic-update-slice_fusion.40, bf16[1,768,3584]{2,1,0:T(8,128)(2,1)S(1)} %bitcast.49, f32[768]{0:T(1024)S(1)} %add_sqrt_fusion, f32[768]{0:T(1024)S(1)} %broadcast_multiply_fusion, bf16[256,3584]{1,0:T(8,128)(2,1)S(1)} %constant_dynamic-update-slice_fusion.32, ...), kind=kOutput, calls=%fused_computation.7 | convolution fusion | flops 2839674880 | bytes 15472640 | tf_op jit(solution)/shard_map/dot_general | solution.py:137
  175.8 4.8 %fusion.5 = bf16[1,3584,768]{2,1,0:T(8,128)(2,1)} fusion(bf16[256,3584]{1,0:T(8,128)(2,1)S(1)} %copy-done.5, bf16[256,3584]{1,0:T(8,128)(2,1)S(1)} %copy-done.3, bf16[256,768]{1,0:T(8,128)(2,1)S(1)} %collective-permute-done.52, bf16[256,768]{1,0:T(8,128)(2,1)S(1)} %get-tuple-element.20), kind=kOutput, calls=%fused_computation.8 | convolution fusion | flops 2830237696 | bytes 9961472 | tf_op jit(solution)/shard_map/dot_general | solution.py:146
  (157 shorter events, 32.9 us)
Async XLA Ops:
  0.6 7.6 %collective-permute-start = (bf16[16,3584]{1,0:T(8,128)(2,1)}, bf16[16,3584]{1,0:T(8,128)(2,1)S(1)}, u32[]{:S(2)}, u32[]{:S(2)}) collective-permute-start(bf16[16,3584]{1,0:T(8,128)(2,1)} %bitcast.50), channel_id=1, source_target_pairs={{0,4},{1,5},{2,6},{3,7},{4,0},{5,1},{6,2},{7,3},{8,12},{9,13},{10,... | collective-permute-start | bytes 344072 | tf_op jit(solution)/shard_map/ppermute | solution.py:22
  8.3 8.8 %collective-permute-start.3 = (bf16[16,3584]{1,0:T(8,128)(2,1)S(1)}, bf16[16,3584]{1,0:T(8,128)(2,1)S(1)}, u32[]{:S(2)}, u32[]{:S(2)}) collective-permute-start(bf16[16,3584]{1,0:T(8,128)(2,1)S(1)} %get-tuple-element.40), channel_id=1, source_target_pairs={{0,1},{1,2},{2,3},{3,0},{4,5},{5,6},{6,7},{7,4},{8,9},{9,10},{10,1... | collective-permute-start | bytes 344072 | tf_op jit(solution)/shard_map/ppermute | solution.py:22
  9.6 8.6 %collective-permute-start.2 = (bf16[16,3584]{1,0:T(8,128)(2,1)S(1)}, bf16[16,3584]{1,0:T(8,128)(2,1)S(1)}, u32[]{:S(2)}, u32[]{:S(2)}) collective-permute-start(bf16[16,3584]{1,0:T(8,128)(2,1)S(1)} %get-tuple-element.40), channel_id=1, source_target_pairs={{0,2},{1,3},{2,0},{3,1},{4,6},{5,7},{6,4},{7,5},{8,10},{9,11},{10,... | collective-permute-start | bytes 344072 | tf_op jit(solution)/shard_map/ppermute | solution.py:22
  12.0 6.2 %collective-permute-start.1 = (bf16[16,3584]{1,0:T(8,128)(2,1)S(1)}, bf16[16,3584]{1,0:T(8,128)(2,1)S(1)}, u32[]{:S(2)}, u32[]{:S(2)}) collective-permute-start(bf16[16,3584]{1,0:T(8,128)(2,1)S(1)} %get-tuple-element.40), channel_id=1, source_target_pairs={{0,3},{1,0},{2,1},{3,2},{4,7},{5,4},{6,5},{7,6},{8,11},{9,8},{10,9... | collective-permute-start | bytes 344072 | tf_op jit(solution)/shard_map/ppermute | solution.py:22
  13.2 7.8 %collective-permute-start.10 = (bf16[16,3584]{1,0:T(8,128)(2,1)S(1)}, bf16[16,3584]{1,0:T(8,128)(2,1)S(1)}, u32[]{:S(2)}, u32[]{:S(2)}) collective-permute-start(bf16[16,3584]{1,0:T(8,128)(2,1)S(1)} %get-tuple-element.22), channel_id=1, source_target_pairs={{0,8},{1,9},{2,10},{3,11},{4,12},{5,13},{6,14},{7,15},{8,16},{9,17... | collective-permute-start | bytes 344072 | tf_op jit(solution)/shard_map/ppermute | solution.py:22
  14.5 6.5 %collective-permute-start.9 = (bf16[16,3584]{1,0:T(8,128)(2,1)S(1)}, bf16[16,3584]{1,0:T(8,128)(2,1)S(1)}, u32[]{:S(2)}, u32[]{:S(2)}) collective-permute-start(bf16[16,3584]{1,0:T(8,128)(2,1)S(1)} %get-tuple-element.22), channel_id=1, source_target_pairs={{0,16},{1,17},{2,18},{3,19},{4,20},{5,21},{6,22},{7,23},{8,24},{9,... | collective-permute-start | bytes 344072 | tf_op jit(solution)/shard_map/ppermute | solution.py:22
  18.2 8.9 %collective-permute-start.6 = (bf16[64,3584]{1,0:T(8,128)(2,1)S(1)}, bf16[64,3584]{1,0:T(8,128)(2,1)S(1)}, u32[]{:S(2)}, u32[]{:S(2)}) collective-permute-start(bf16[64,3584]{1,0:T(8,128)(2,1)S(1)} %pad_maximum_fusion), channel_id=1, source_target_pairs={{0,8},{1,9},{2,10},{3,11},{4,12},{5,13},{6,14},{7,15},{8,16},{9,17... | collective-permute-start | bytes 1376264 | tf_op jit(solution)/shard_map/ppermute | solution.py:22
  18.7 8.5 %collective-permute-start.4 = (bf16[64,3584]{1,0:T(8,128)(2,1)S(1)}, bf16[64,3584]{1,0:T(8,128)(2,1)S(1)}, u32[]{:S(2)}, u32[]{:S(2)}) collective-permute-start(bf16[64,3584]{1,0:T(8,128)(2,1)S(1)} %pad_maximum_fusion), channel_id=1, source_target_pairs={{0,24},{1,25},{2,26},{3,27},{4,28},{5,29},{6,30},{7,31},{8,0},{9,1... | collective-permute-start | bytes 1376264 | tf_op jit(solution)/shard_map/ppermute | solution.py:22
  21.0 13.4 %collective-permute-start.13 = (bf16[64,3584]{1,0:T(8,128)(2,1)S(1)}, bf16[64,3584]{1,0:T(8,128)(2,1)S(1)}, u32[]{:S(2)}, u32[]{:S(2)}) collective-permute-start(bf16[64,3584]{1,0:T(8,128)(2,1)S(1)} %pad_maximum_fusion.1), channel_id=1, source_target_pairs={{0,1},{1,2},{2,3},{3,0},{4,5},{5,6},{6,7},{7,4},{8,9},{9,10},{10,1... | collective-permute-start | bytes 1376264 | tf_op jit(solution)/shard_map/ppermute | solution.py:22
  21.5 13.0 %collective-permute-start.11 = (bf16[64,3584]{1,0:T(8,128)(2,1)S(1)}, bf16[64,3584]{1,0:T(8,128)(2,1)S(1)}, u32[]{:S(2)}, u32[]{:S(2)}) collective-permute-start(bf16[64,3584]{1,0:T(8,128)(2,1)S(1)} %pad_maximum_fusion.1), channel_id=1, source_target_pairs={{0,3},{1,0},{2,1},{3,2},{4,7},{5,4},{6,5},{7,6},{8,11},{9,8},{10,9... | collective-permute-start | bytes 1376264 | tf_op jit(solution)/shard_map/ppermute | solution.py:22
  27.1 10.3 %collective-permute-start.7 = (bf16[32,3584]{1,0:T(8,128)(2,1)S(1)}, bf16[32,3584]{1,0:T(8,128)(2,1)S(1)}, u32[]{:S(2)}, u32[]{:S(2)}) collective-permute-start(bf16[32,3584]{1,0:T(8,128)(2,1)S(1)} %slice.179), channel_id=1, source_target_pairs={{0,8},{1,9},{2,10},{3,11},{4,12},{5,13},{6,14},{7,15},{8,16},{9,17... | collective-permute-start | bytes 688136 | tf_op jit(solution)/shard_map/ppermute | solution.py:22
  27.2 10.1 %collective-permute-start.5 = (bf16[32,3584]{1,0:T(8,128)(2,1)S(1)}, bf16[32,3584]{1,0:T(8,128)(2,1)S(1)}, u32[]{:S(2)}, u32[]{:S(2)}) collective-permute-start(bf16[32,3584]{1,0:T(8,128)(2,1)S(1)} %slice.178), channel_id=1, source_target_pairs={{0,24},{1,25},{2,26},{3,27},{4,28},{5,29},{6,30},{7,31},{8,0},{9,1... | collective-permute-start | bytes 688136 | tf_op jit(solution)/shard_map/ppermute | solution.py:22
  34.4 7.6 %collective-permute-start.14 = (bf16[32,3584]{1,0:T(8,128)(2,1)S(1)}, bf16[32,3584]{1,0:T(8,128)(2,1)S(1)}, u32[]{:S(2)}, u32[]{:S(2)}) collective-permute-start(bf16[32,3584]{1,0:T(8,128)(2,1)S(1)} %slice.181), channel_id=1, source_target_pairs={{0,1},{1,2},{2,3},{3,0},{4,5},{5,6},{6,7},{7,4},{8,9},{9,10},{10,1... | collective-permute-start | bytes 688136 | tf_op jit(solution)/shard_map/ppermute | solution.py:22
  34.6 6.5 %collective-permute-start.12 = (bf16[32,3584]{1,0:T(8,128)(2,1)S(1)}, bf16[32,3584]{1,0:T(8,128)(2,1)S(1)}, u32[]{:S(2)}, u32[]{:S(2)}) collective-permute-start(bf16[32,3584]{1,0:T(8,128)(2,1)S(1)} %slice.180), channel_id=1, source_target_pairs={{0,3},{1,0},{2,1},{3,2},{4,7},{5,4},{6,5},{7,6},{8,11},{9,8},{10,9... | collective-permute-start | bytes 688136 | tf_op jit(solution)/shard_map/ppermute | solution.py:22
  43.7 6.0 %collective-permute-start.15 = (f32[256,768]{1,0:T(8,128)S(1)}, f32[256,768]{1,0:T(8,128)S(1)}, u32[]{:S(2)}, u32[]{:S(2)}) collective-permute-start(f32[256,768]{1,0:T(8,128)S(1)} %fusion.14), channel_id=1, source_target_pairs={{0,32},{32,0},{64,96},{96,64},{1,33},{33,1},{65,97},{97,65},{2,34}... | collective-permute-start | bytes 2359304 | tf_op jit(solution)/shard_map/ppermute | solution.py:26
  51.3 10.4 %collective-permute-start.16 = (bf16[256,768]{1,0:T(8,128)(2,1)S(1)}, bf16[256,768]{1,0:T(8,128)(2,1)S(1)}, u32[]{:S(2)}, u32[]{:S(2)}) collective-permute-start(bf16[256,768]{1,0:T(8,128)(2,1)S(1)} %get-tuple-element.67), channel_id=1, source_target_pairs={{0,64},{32,96},{64,0},{96,32},{1,65},{33,97},{65,1},{97,33},{2,66}... | collective-permute-start | bytes 1179656 | tf_op jit(solution)/shard_map/ppermute | solution.py:26
  69.2 7.7 %collective-permute-start.28 = (bf16[64,3584]{1,0:T(8,128)(2,1)S(1)}, bf16[64,3584]{1,0:T(8,128)(2,1)S(1)}, u32[]{:S(2)}, u32[]{:S(2)}) collective-permute-start(bf16[64,3584]{1,0:T(8,128)(2,1)S(1)} %get-tuple-element.27), channel_id=1, source_target_pairs={{0,3},{1,0},{2,1},{3,2},{4,7},{5,4},{6,5},{7,6},{8,11},{9,8},{10,9... | collective-permute-start | bytes 1376264 | tf_op jit(solution)/shard_map/ppermute | solution.py:22
  69.9 8.8 %collective-permute-start.26 = (bf16[64,3584]{1,0:T(8,128)(2,1)S(1)}, bf16[64,3584]{1,0:T(8,128)(2,1)S(1)}, u32[]{:S(2)}, u32[]{:S(2)}) collective-permute-start(bf16[64,3584]{1,0:T(8,128)(2,1)S(1)} %get-tuple-element.28), channel_id=1, source_target_pairs={{0,1},{1,2},{2,3},{3,0},{4,5},{5,6},{6,7},{7,4},{8,9},{9,10},{10,1... | collective-permute-start | bytes 1376264 | tf_op jit(solution)/shard_map/ppermute | solution.py:22
  72.4 11.1 %collective-permute-start.20 = (bf16[64,3584]{1,0:T(8,128)(2,1)S(1)}, bf16[64,3584]{1,0:T(8,128)(2,1)S(1)}, u32[]{:S(2)}, u32[]{:S(2)}) collective-permute-start(bf16[64,3584]{1,0:T(8,128)(2,1)S(1)} %get-tuple-element.31), channel_id=1, source_target_pairs={{0,24},{1,25},{2,26},{3,27},{4,28},{5,29},{6,30},{7,31},{8,0},{9,1... | collective-permute-start | bytes 1376264 | tf_op jit(solution)/shard_map/ppermute | solution.py:22
  75.5 11.4 %collective-permute-start.18 = (bf16[64,3584]{1,0:T(8,128)(2,1)S(1)}, bf16[64,3584]{1,0:T(8,128)(2,1)S(1)}, u32[]{:S(2)}, u32[]{:S(2)}) collective-permute-start(bf16[64,3584]{1,0:T(8,128)(2,1)S(1)} %get-tuple-element.32), channel_id=1, source_target_pairs={{0,8},{1,9},{2,10},{3,11},{4,12},{5,13},{6,14},{7,15},{8,16},{9,17... | collective-permute-start | bytes 1376264 | tf_op jit(solution)/shard_map/ppermute | solution.py:22
  78.8 9.8 %collective-permute-start.29 = (bf16[32,3584]{1,0:T(8,128)(2,1)S(1)}, bf16[32,3584]{1,0:T(8,128)(2,1)S(1)}, u32[]{:S(2)}, u32[]{:S(2)}) collective-permute-start(bf16[32,3584]{1,0:T(8,128)(2,1)S(1)} %get-tuple-element.25), channel_id=1, source_target_pairs={{0,3},{1,0},{2,1},{3,2},{4,7},{5,4},{6,5},{7,6},{8,11},{9,8},{10,9... | collective-permute-start | bytes 688136 | tf_op jit(solution)/shard_map/ppermute | solution.py:22
  78.9 9.7 %collective-permute-start.27 = (bf16[32,3584]{1,0:T(8,128)(2,1)S(1)}, bf16[32,3584]{1,0:T(8,128)(2,1)S(1)}, u32[]{:S(2)}, u32[]{:S(2)}) collective-permute-start(bf16[32,3584]{1,0:T(8,128)(2,1)S(1)} %get-tuple-element.26), channel_id=1, source_target_pairs={{0,1},{1,2},{2,3},{3,0},{4,5},{5,6},{6,7},{7,4},{8,9},{9,10},{10,1... | collective-permute-start | bytes 688136 | tf_op jit(solution)/shard_map/ppermute | solution.py:22
  87.0 6.7 %collective-permute-start.21 = (bf16[32,3584]{1,0:T(8,128)(2,1)S(1)}, bf16[32,3584]{1,0:T(8,128)(2,1)S(1)}, u32[]{:S(2)}, u32[]{:S(2)}) collective-permute-start(bf16[32,3584]{1,0:T(8,128)(2,1)S(1)} %get-tuple-element.29), channel_id=1, source_target_pairs={{0,24},{1,25},{2,26},{3,27},{4,28},{5,29},{6,30},{7,31},{8,0},{9,1... | collective-permute-start | bytes 688136 | tf_op jit(solution)/shard_map/ppermute | solution.py:22
  87.1 8.8 %collective-permute-start.19 = (bf16[32,3584]{1,0:T(8,128)(2,1)S(1)}, bf16[32,3584]{1,0:T(8,128)(2,1)S(1)}, u32[]{:S(2)}, u32[]{:S(2)}) collective-permute-start(bf16[32,3584]{1,0:T(8,128)(2,1)S(1)} %get-tuple-element.30), channel_id=1, source_target_pairs={{0,8},{1,9},{2,10},{3,11},{4,12},{5,13},{6,14},{7,15},{8,16},{9,17... | collective-permute-start | bytes 688136 | tf_op jit(solution)/shard_map/ppermute | solution.py:22
  88.8 7.4 %collective-permute-start.30 = (bf16[16,3584]{1,0:T(8,128)(2,1)S(1)}, bf16[16,3584]{1,0:T(8,128)(2,1)S(1)}, u32[]{:S(2)}, u32[]{:S(2)}) collective-permute-start(bf16[16,3584]{1,0:T(8,128)(2,1)S(1)} %get-tuple-element.33), channel_id=1, source_target_pairs={{0,16},{1,17},{2,18},{3,19},{4,20},{5,21},{6,22},{7,23},{8,24},{9,... | collective-permute-start | bytes 344072 | tf_op jit(solution)/shard_map/ppermute | solution.py:22
  88.9 8.8 %collective-permute-start.32 = (bf16[16,3584]{1,0:T(8,128)(2,1)S(1)}, bf16[16,3584]{1,0:T(8,128)(2,1)S(1)}, u32[]{:S(2)}, u32[]{:S(2)}) collective-permute-start(bf16[16,3584]{1,0:T(8,128)(2,1)S(1)} %get-tuple-element.34), channel_id=1, source_target_pairs={{0,24},{1,25},{2,26},{3,27},{4,28},{5,29},{6,30},{7,31},{8,0},{9,1... | collective-permute-start | bytes 344072 | tf_op jit(solution)/shard_map/ppermute | solution.py:22
  91.3 6.4 %collective-permute-start.31 = (bf16[16,3584]{1,0:T(8,128)(2,1)S(1)}, bf16[16,3584]{1,0:T(8,128)(2,1)S(1)}, u32[]{:S(2)}, u32[]{:S(2)}) collective-permute-start(bf16[16,3584]{1,0:T(8,128)(2,1)S(1)} %get-tuple-element.35), channel_id=1, source_target_pairs={{0,8},{1,9},{2,10},{3,11},{4,12},{5,13},{6,14},{7,15},{8,16},{9,17... | collective-permute-start | bytes 344072 | tf_op jit(solution)/shard_map/ppermute | solution.py:22
  96.1 6.7 %collective-permute-start.22 = (bf16[16,3584]{1,0:T(8,128)(2,1)S(1)}, bf16[16,3584]{1,0:T(8,128)(2,1)S(1)}, u32[]{:S(2)}, u32[]{:S(2)}) collective-permute-start(bf16[16,3584]{1,0:T(8,128)(2,1)S(1)} %get-tuple-element.36), channel_id=1, source_target_pairs={{0,2},{1,3},{2,0},{3,1},{4,6},{5,7},{6,4},{7,5},{8,10},{9,11},{10,... | collective-permute-start | bytes 344072 | tf_op jit(solution)/shard_map/ppermute | solution.py:22
  96.2 6.6 %collective-permute-start.24 = (bf16[16,3584]{1,0:T(8,128)(2,1)S(1)}, bf16[16,3584]{1,0:T(8,128)(2,1)S(1)}, u32[]{:S(2)}, u32[]{:S(2)}) collective-permute-start(bf16[16,3584]{1,0:T(8,128)(2,1)S(1)} %get-tuple-element.37), channel_id=1, source_target_pairs={{0,3},{1,0},{2,1},{3,2},{4,7},{5,4},{6,5},{7,6},{8,11},{9,8},{10,9... | collective-permute-start | bytes 344072 | tf_op jit(solution)/shard_map/ppermute | solution.py:22
  96.3 9.0 %collective-permute-start.23 = (bf16[16,3584]{1,0:T(8,128)(2,1)S(1)}, bf16[16,3584]{1,0:T(8,128)(2,1)S(1)}, u32[]{:S(2)}, u32[]{:S(2)}) collective-permute-start(bf16[16,3584]{1,0:T(8,128)(2,1)S(1)} %get-tuple-element.38), channel_id=1, source_target_pairs={{0,1},{1,2},{2,3},{3,0},{4,5},{5,6},{6,7},{7,4},{8,9},{9,10},{10,1... | collective-permute-start | bytes 344072 | tf_op jit(solution)/shard_map/ppermute | solution.py:22
  97.8 10.5 %collective-permute-start.33 = (bf16[16,3584]{1,0:T(8,128)(2,1)S(1)}, bf16[16,3584]{1,0:T(8,128)(2,1)S(1)}, u32[]{:S(2)}, u32[]{:S(2)}) collective-permute-start(bf16[16,3584]{1,0:T(8,128)(2,1)S(1)} %fusion.56), channel_id=1, source_target_pairs={{0,4},{1,5},{2,6},{3,7},{4,0},{5,1},{6,2},{7,3},{8,12},{9,13},{10,... | collective-permute-start | bytes 344072 | tf_op jit(solution)/shard_map/ppermute | solution.py:22
  105.3 5.9 %collective-permute-start.25 = (bf16[16,3584]{1,0:T(8,128)(2,1)S(1)}, bf16[16,3584]{1,0:T(8,128)(2,1)S(1)}, u32[]{:S(2)}, u32[]{:S(2)}) collective-permute-start(bf16[16,3584]{1,0:T(8,128)(2,1)S(1)} %fusion.55), channel_id=1, source_target_pairs={{0,4},{1,5},{2,6},{3,7},{4,0},{5,1},{6,2},{7,3},{8,12},{9,13},{10,... | collective-permute-start | bytes 344072 | tf_op jit(solution)/shard_map/ppermute | solution.py:22
  111.4 6.8 %collective-permute-start.36 = (bf16[16,3584]{1,0:T(8,128)(2,1)S(1)}, bf16[16,3584]{1,0:T(8,128)(2,1)S(1)}, u32[]{:S(2)}, u32[]{:S(2)}) collective-permute-start(bf16[16,3584]{1,0:T(8,128)(2,1)S(1)} %get-tuple-element.15), channel_id=1, source_target_pairs={{0,1},{1,2},{2,3},{3,0},{4,5},{5,6},{6,7},{7,4},{8,9},{9,10},{10,1... | collective-permute-start | bytes 344072 | tf_op jit(solution)/shard_map/ppermute | solution.py:22
  111.5 6.7 %collective-permute-start.35 = (bf16[16,3584]{1,0:T(8,128)(2,1)S(1)}, bf16[16,3584]{1,0:T(8,128)(2,1)S(1)}, u32[]{:S(2)}, u32[]{:S(2)}) collective-permute-start(bf16[16,3584]{1,0:T(8,128)(2,1)S(1)} %get-tuple-element.15), channel_id=1, source_target_pairs={{0,2},{1,3},{2,0},{3,1},{4,6},{5,7},{6,4},{7,5},{8,10},{9,11},{10,... | collective-permute-start | bytes 344072 | tf_op jit(solution)/shard_map/ppermute | solution.py:22
  112.8 5.4 %collective-permute-start.34 = (bf16[16,3584]{1,0:T(8,128)(2,1)S(1)}, bf16[16,3584]{1,0:T(8,128)(2,1)S(1)}, u32[]{:S(2)}, u32[]{:S(2)}) collective-permute-start(bf16[16,3584]{1,0:T(8,128)(2,1)S(1)} %get-tuple-element.15), channel_id=1, source_target_pairs={{0,3},{1,0},{2,1},{3,2},{4,7},{5,4},{6,5},{7,6},{8,11},{9,8},{10,9... | collective-permute-start | bytes 344072 | tf_op jit(solution)/shard_map/ppermute | solution.py:22
  114.2 8.8 %collective-permute-start.43 = (bf16[16,3584]{1,0:T(8,128)(2,1)S(1)}, bf16[16,3584]{1,0:T(8,128)(2,1)S(1)}, u32[]{:S(2)}, u32[]{:S(2)}) collective-permute-start(bf16[16,3584]{1,0:T(8,128)(2,1)S(1)} %get-tuple-element.16), channel_id=1, source_target_pairs={{0,8},{1,9},{2,10},{3,11},{4,12},{5,13},{6,14},{7,15},{8,16},{9,17... | collective-permute-start | bytes 344072 | tf_op jit(solution)/shard_map/ppermute | solution.py:22
  114.2 8.8 %collective-permute-start.42 = (bf16[16,3584]{1,0:T(8,128)(2,1)S(1)}, bf16[16,3584]{1,0:T(8,128)(2,1)S(1)}, u32[]{:S(2)}, u32[]{:S(2)}) collective-permute-start(bf16[16,3584]{1,0:T(8,128)(2,1)S(1)} %get-tuple-element.16), channel_id=1, source_target_pairs={{0,16},{1,17},{2,18},{3,19},{4,20},{5,21},{6,22},{7,23},{8,24},{9,... | collective-permute-start | bytes 344072 | tf_op jit(solution)/shard_map/ppermute | solution.py:22
  118.3 9.3 %collective-permute-start.39 = (bf16[64,3584]{1,0:T(8,128)(2,1)S(1)}, bf16[64,3584]{1,0:T(8,128)(2,1)S(1)}, u32[]{:S(2)}, u32[]{:S(2)}) collective-permute-start(bf16[64,3584]{1,0:T(8,128)(2,1)S(1)} %get-tuple-element.49), channel_id=1, source_target_pairs={{0,8},{1,9},{2,10},{3,11},{4,12},{5,13},{6,14},{7,15},{8,16},{9,17... | collective-permute-start | bytes 1376264 | tf_op jit(solution)/shard_map/ppermute | solution.py:22
  119.8 9.4 %collective-permute-start.37 = (bf16[64,3584]{1,0:T(8,128)(2,1)S(1)}, bf16[64,3584]{1,0:T(8,128)(2,1)S(1)}, u32[]{:S(2)}, u32[]{:S(2)}) collective-permute-start(bf16[64,3584]{1,0:T(8,128)(2,1)S(1)} %get-tuple-element.49), channel_id=1, source_target_pairs={{0,24},{1,25},{2,26},{3,27},{4,28},{5,29},{6,30},{7,31},{8,0},{9,1... | collective-permute-start | bytes 1376264 | tf_op jit(solution)/shard_map/ppermute | solution.py:22
  123.1 9.6 %collective-permute-start.46 = (bf16[64,3584]{1,0:T(8,128)(2,1)S(1)}, bf16[64,3584]{1,0:T(8,128)(2,1)S(1)}, u32[]{:S(2)}, u32[]{:S(2)}) collective-permute-start(bf16[64,3584]{1,0:T(8,128)(2,1)S(1)} %get-tuple-element.41), channel_id=1, source_target_pairs={{0,1},{1,2},{2,3},{3,0},{4,5},{5,6},{6,7},{7,4},{8,9},{9,10},{10,1... | collective-permute-start | bytes 1376264 | tf_op jit(solution)/shard_map/ppermute | solution.py:22
  123.8 10.3 %collective-permute-start.44 = (bf16[64,3584]{1,0:T(8,128)(2,1)S(1)}, bf16[64,3584]{1,0:T(8,128)(2,1)S(1)}, u32[]{:S(2)}, u32[]{:S(2)}) collective-permute-start(bf16[64,3584]{1,0:T(8,128)(2,1)S(1)} %get-tuple-element.41), channel_id=1, source_target_pairs={{0,3},{1,0},{2,1},{3,2},{4,7},{5,4},{6,5},{7,6},{8,11},{9,8},{10,9... | collective-permute-start | bytes 1376264 | tf_op jit(solution)/shard_map/ppermute | solution.py:22
  127.7 10.1 %collective-permute-start.40 = (bf16[32,3584]{1,0:T(8,128)(2,1)S(1)}, bf16[32,3584]{1,0:T(8,128)(2,1)S(1)}, u32[]{:S(2)}, u32[]{:S(2)}) collective-permute-start(bf16[32,3584]{1,0:T(8,128)(2,1)S(1)} %slice.213), channel_id=1, source_target_pairs={{0,8},{1,9},{2,10},{3,11},{4,12},{5,13},{6,14},{7,15},{8,16},{9,17... | collective-permute-start | bytes 688136 | tf_op jit(solution)/shard_map/ppermute | solution.py:22
  129.3 8.5 %collective-permute-start.38 = (bf16[32,3584]{1,0:T(8,128)(2,1)S(1)}, bf16[32,3584]{1,0:T(8,128)(2,1)S(1)}, u32[]{:S(2)}, u32[]{:S(2)}) collective-permute-start(bf16[32,3584]{1,0:T(8,128)(2,1)S(1)} %slice.212), channel_id=1, source_target_pairs={{0,24},{1,25},{2,26},{3,27},{4,28},{5,29},{6,30},{7,31},{8,0},{9,1... | collective-permute-start | bytes 688136 | tf_op jit(solution)/shard_map/ppermute | solution.py:22
  132.7 7.9 %collective-permute-start.47 = (bf16[32,3584]{1,0:T(8,128)(2,1)S(1)}, bf16[32,3584]{1,0:T(8,128)(2,1)S(1)}, u32[]{:S(2)}, u32[]{:S(2)}) collective-permute-start(bf16[32,3584]{1,0:T(8,128)(2,1)S(1)} %slice.215), channel_id=1, source_target_pairs={{0,1},{1,2},{2,3},{3,0},{4,5},{5,6},{6,7},{7,4},{8,9},{9,10},{10,1... | collective-permute-start | bytes 688136 | tf_op jit(solution)/shard_map/ppermute | solution.py:22
  134.2 6.4 %collective-permute-start.45 = (bf16[32,3584]{1,0:T(8,128)(2,1)S(1)}, bf16[32,3584]{1,0:T(8,128)(2,1)S(1)}, u32[]{:S(2)}, u32[]{:S(2)}) collective-permute-start(bf16[32,3584]{1,0:T(8,128)(2,1)S(1)} %slice.214), channel_id=1, source_target_pairs={{0,3},{1,0},{2,1},{3,2},{4,7},{5,4},{6,5},{7,6},{8,11},{9,8},{10,9... | collective-permute-start | bytes 688136 | tf_op jit(solution)/shard_map/ppermute | solution.py:22
  142.3 13.8 %collective-permute-start.48 = (f32[256,768]{1,0:T(8,128)S(1)}, f32[256,768]{1,0:T(8,128)S(1)}, u32[]{:S(2)}, u32[]{:S(2)}) collective-permute-start(f32[256,768]{1,0:T(8,128)S(1)} %fusion.6), channel_id=1, source_target_pairs={{0,32},{32,0},{64,96},{96,64},{1,33},{33,1},{65,97},{97,65},{2,34}... | collective-permute-start | bytes 2359304 | tf_op jit(solution)/shard_map/ppermute | solution.py:26
  157.7 9.2 %collective-permute-start.49 = (bf16[256,768]{1,0:T(8,128)(2,1)S(1)}, bf16[256,768]{1,0:T(8,128)(2,1)S(1)}, u32[]{:S(2)}, u32[]{:S(2)}) collective-permute-start(bf16[256,768]{1,0:T(8,128)(2,1)S(1)} %get-tuple-element.69), channel_id=1, source_target_pairs={{0,64},{32,96},{64,0},{96,32},{1,65},{33,97},{65,1},{97,33},{2,66}... | collective-permute-start | bytes 1179656 | tf_op jit(solution)/shard_map/ppermute | solution.py:26
  167.3 7.8 %collective-permute-start.52 = (bf16[256,768]{1,0:T(8,128)(2,1)S(1)}, bf16[256,768]{1,0:T(8,128)(2,1)S(1)}, u32[]{:S(2)}, u32[]{:S(2)}) collective-permute-start(bf16[256,768]{1,0:T(8,128)(2,1)S(1)} %get-tuple-element.20), channel_id=1, source_target_pairs={{0,32},{32,0},{64,96},{96,64},{1,33},{33,1},{65,97},{97,65},{2,34}... | collective-permute-start | bytes 1179656 | tf_op jit(solution)/shard_map/ppermute | solution.py:26
  (14 other events, 108.1 us)

commit v3 on v2

--- a/solution.py
+++ b/solution.py
@@ -88,9 +88,8 @@
     return pair + join(other[half:], other[:half])
 
 
-def layer_sum(keep, send):
-    part = rounded(keep + layer_swap(send, 1))
-    return part + wide(layer_swap(narrow(part), 2))
+def core_sum(keep, send):
+    return rounded(lax.optimization_barrier(keep) + layer_swap(send, 1))
 
 
 def per_device(residuals, enc_weight, dec_weight, enc_bias, dec_bias):
@@ -99,18 +98,18 @@
     dec_local = dec_weight[0]
     upper = lax.axis_index("layer") % 2 == 1
 
-    row_norms = jnp.sqrt(jnp.sum(jnp.square(wide(dec_local)), axis=1) + 1e-06)
-    weight_sum = row_norms + layer_swap(row_norms, 1)
-    weight_sum = weight_sum + layer_swap(weight_sum, 2)
-    penalty = sparsity_weight * weight_sum[None, :]
-
     other_rows = shift(own_rows, 0, "zh", 1)
     low, high = join(own_rows[:8], other_rows[:8]), join(own_rows[8:], other_rows[8:])
     pairs = [jnp.where(upper, high, low), jnp.where(upper, low, high)]
     gathered = [gather_rows(pairs[slot], slot) for slot in (0, 1)]
     gathered = list(lax.optimization_barrier(tuple(gathered)))
     pre = [jnp.dot(rows, enc_local, preferred_element_type=jnp.float32) for rows in gathered]
-    pre = layer_sum(*pre) + enc_bias[None, :]
+    part = core_sum(*pre)
+    other = layer_swap(narrow(part), 2)
+    part, dec_local = lax.optimization_barrier((part, dec_local))
+    row_norms = jnp.sqrt(jnp.sum(jnp.square(wide(dec_local)), axis=1) + 1e-06)
+    other, row_norms = lax.optimization_barrier((other, row_norms))
+    pre = part + wide(other) + enc_bias[None, :]
     kept = narrow(jax.nn.softplus(sharpness * pre) / sharpness)
     gate = jax.nn.sigmoid(sharpness * pre)
     latents = [kept, layer_swap(kept, 1)]
@@ -121,7 +120,6 @@
         rebuilt = scatter_sum(narrow(rebuilt), slot)
         misfit = rebuilt + dec_bias[0][None, :] - wide(pairs[slot])
         errors.append(narrow(2.0 * misfit))
-    errors = list(lax.optimization_barrier(tuple(errors)))
     errors = [gather_rows(errors[slot], slot) for slot in (0, 1)]
     errors = list(lax.optimization_barrier(tuple(errors)))
     back = [
@@ -130,9 +128,14 @@
         )
         for rows in errors
     ]
-    lat_grad = layer_sum(*back) + penalty
-    kept = narrow(lat_grad * gate)
-    pre_grads = [kept, layer_swap(kept, 1)]
+    norm_rows = jnp.broadcast_to(row_norms[None, :], (8, row_norms.shape[0]))
+    got = layer_swap(join(back[1], norm_rows), 1)
+    part = rounded(lax.optimization_barrier(back[0]) + got[:256])
+    chip_norms = row_norms + got[256]
+    head = rounded(chip_norms)
+    tail = rounded(chip_norms - head)
+    norm_rows = jnp.where(jnp.arange(8)[:, None] < 4, head[None, :], tail[None, :])
+    other = layer_swap(narrow(join(part, norm_rows)), 2)
     act_sum = jnp.sum(wide(join(*latents)), axis=0)
     dec_acc = lax.dot_general(
         join(*latents),
@@ -142,6 +145,11 @@
     )
     penalty_term = sparsity_weight * act_sum[:, None] * wide(dec_local) / row_norms[:, None]
     dec_grad = narrow(dec_acc + penalty_term)
+    other, dec_grad = lax.optimization_barrier((other, dec_grad))
+    weight_sum = (head + tail) + (wide(other[256]) + wide(other[260]))
+    lat_grad = part + wide(other[:256]) + sparsity_weight * weight_sum[None, :]
+    kept = narrow(lat_grad * gate)
+    pre_grads = [kept, layer_swap(kept, 1)]
     enc_grad = narrow(
         lax.dot_general(
             join(*gathered),

time: 181 us -> 173 us (0.956)
  waiting for transfers between devices: 74.4 us -> 58.9 us
  starting transfers between devices: 76.7 us -> 81.5 us
  matrix products: 22.3 us -> 24.9 us
    ppermute x8 -> x6, waiting for transfers between devices: 24 us -> 15 us  [layer_swap(): return lax.ppermute(value, 'layer', [(i, i ^ bit) for i in range(4)])]
    ppermute x45, starting transfers between devices: 56.5 us -> 63.8 us  [shift(): return lax.ppermute(value, ('layer', 'latent'), pairs)]
    ppermute x45, waiting for transfers between devices: 50.4 us -> 43.9 us  [shift(): return lax.ppermute(value, ('layer', 'latent'), pairs)]
    ppermute x8 -> x6, starting transfers between devices: 20.2 us -> 17.6 us  [layer_swap(): return lax.ppermute(value, 'layer', [(i, i ^ bit) for i in range(4)])]
    dot_general x2, matrix products: 5.73 us -> 8.29 us  [per_device(): jnp.dot(latents[slot], dec_local, preferred_element_type=jnp.float32)]
  transfers between devices with their start and end apart: 53 -> 51, of which waited for: 28 -> 30; matrix products, arithmetic and copies ran while one was open for 6% -> 10% of each run, Pallas kernels for 0% -> 0%
where the time goes in v3:
time: 173 us
  starting transfers between devices  81.5 us (47%)
  waiting for transfers between devices  58.9 us (34%)
  matrix products  24.9 us (14%)
  other arithmetic  4.52 us (3%)
  local copies, waits for them, and re-layouts  1.91 us (1%)
    ppermute x45, starting transfers between devices, shift(): return lax.ppermute(value, ('layer', 'latent'), pairs)  63.8 us
    ppermute x45, waiting for transfers between devices, shift(): return lax.ppermute(value, ('layer', 'latent'), pairs)  43.9 us
    ppermute x6, starting transfers between devices, layer_swap(): return lax.ppermute(value, 'layer', [(i, i ^ bit) for i in range(4)])  17.6 us
    ppermute x6, waiting for transfers between devices, layer_swap(): return lax.ppermute(value, 'layer', [(i, i ^ bit) for i in range(4)])  15 us
    dot_general x2, matrix products, per_device(): jnp.dot(latents[slot], dec_local, preferred_element_type=jnp.float32)  8.29 us
    dot_general x1, matrix products, per_device(): lax.dot_general(join(*latents), join(*errors), (((0,), (0,)), ((), ())),...  5.39 us
    dot_general x1, matrix products, per_device(): lax.dot_general(join(*gathered), join(*pre_grads), (((0,), (0,)), ((), ()...  4.84 us
  transfers between devices with their start and end apart: 51, of which 30 were waited for; matrix products, arithmetic and copies ran while one was open for 10% of the time, Pallas kernels for 0%

profile of v3, /device:TPU:1, one launch (start us, length us, event | category | flops | bytes accessed | tf_op | source)
XLA Modules:
  0.0 173.0 jit_solution(11838778023974104899)
XLA Ops:
  0.6 4.5 %collective-permute-start = (bf16[16,3584]{1,0:T(8,128)(2,1)}, bf16[16,3584]{1,0:T(8,128)(2,1)S(1)}, u32[]{:S(2)}, u32[]{:S(2)}) collective-permute-start(bf16[16,3584]{1,0:T(8,128)(2,1)} %bitcast.35), channel_id=1, source_target_pairs={{0,4},{1,5},{2,6},{3,7},{4,0},{5,1},{6,2},{7,3},{8,12},{9,13},{10,... | collective-permute-start | bytes 344072 | tf_op jit(solution)/shard_map/ppermute | solution.py:22
  6.0 2.2 %collective-permute-done = bf16[16,3584]{1,0:T(8,128)(2,1)S(1)} collective-permute-done((bf16[16,3584]{1,0:T(8,128)(2,1)}, bf16[16,3584]{1,0:T(8,128)(2,1)S(1)}, u32[]{:S(2)}, u32[]{:S(2)}) %collective-permute-start) | collective-permute-done | bytes 114720 | tf_op jit(solution)/shard_map/ppermute | solution.py:22
  8.3 2.8 %collective-permute-start.8 = (bf16[16,3584]{1,0:T(8,128)(2,1)S(1)}, bf16[16,3584]{1,0:T(8,128)(2,1)S(1)}, u32[]{:S(2)}, u32[]{:S(2)}) collective-permute-start(bf16[16,3584]{1,0:T(8,128)(2,1)S(1)} %get-tuple-element.36), channel_id=1, source_target_pairs={{0,24},{1,25},{2,26},{3,27},{4,28},{5,29},{6,30},{7,31},{8,0},{9,1... | collective-permute-start | bytes 344072 | tf_op jit(solution)/shard_map/ppermute | solution.py:22
  12.1 2.5 %collective-permute-start.1 = (bf16[16,3584]{1,0:T(8,128)(2,1)S(1)}, bf16[16,3584]{1,0:T(8,128)(2,1)S(1)}, u32[]{:S(2)}, u32[]{:S(2)}) collective-permute-start(bf16[16,3584]{1,0:T(8,128)(2,1)S(1)} %get-tuple-element.54), channel_id=1, source_target_pairs={{0,3},{1,0},{2,1},{3,2},{4,7},{5,4},{6,5},{7,6},{8,11},{9,8},{10,9... | collective-permute-start | bytes 344072 | tf_op jit(solution)/shard_map/ppermute | solution.py:22
  16.3 1.4 collective-permute-done.10
  17.8 2.3 %collective-permute-start.11 = (bf16[64,3584]{1,0:T(8,128)(2,1)S(1)}, bf16[64,3584]{1,0:T(8,128)(2,1)S(1)}, u32[]{:S(2)}, u32[]{:S(2)}) collective-permute-start(bf16[64,3584]{1,0:T(8,128)(2,1)S(1)} %pad_maximum_fusion.2), channel_id=1, source_target_pairs={{0,3},{1,0},{2,1},{3,2},{4,7},{5,4},{6,5},{7,6},{8,11},{9,8},{10,9... | collective-permute-start | bytes 1376264 | tf_op jit(solution)/shard_map/ppermute | solution.py:22
  20.5 1.5 collective-permute-done.3
  22.0 2.7 %collective-permute-start.4 = (bf16[64,3584]{1,0:T(8,128)(2,1)S(1)}, bf16[64,3584]{1,0:T(8,128)(2,1)S(1)}, u32[]{:S(2)}, u32[]{:S(2)}) collective-permute-start(bf16[64,3584]{1,0:T(8,128)(2,1)S(1)} %pad_maximum_fusion.1), channel_id=1, source_target_pairs={{0,24},{1,25},{2,26},{3,27},{4,28},{5,29},{6,30},{7,31},{8,0},{9,1... | collective-permute-start | bytes 1376264 | tf_op jit(solution)/shard_map/ppermute | solution.py:22
  25.5 3.2 %collective-permute-start.12 = (bf16[32,3584]{1,0:T(8,128)(2,1)S(1)}, bf16[32,3584]{1,0:T(8,128)(2,1)S(1)}, u32[]{:S(2)}, u32[]{:S(2)}) collective-permute-start(bf16[32,3584]{1,0:T(8,128)(2,1)S(1)} %slice.200), channel_id=1, source_target_pairs={{0,3},{1,0},{2,1},{3,2},{4,7},{5,4},{6,5},{7,6},{8,11},{9,8},{10,9... | collective-permute-start | bytes 688136 | tf_op jit(solution)/shard_map/ppermute | solution.py:22
  28.8 5.7 %collective-permute-done.4 = bf16[64,3584]{1,0:T(8,128)(2,1)S(1)} collective-permute-done((bf16[64,3584]{1,0:T(8,128)(2,1)S(1)}, bf16[64,3584]{1,0:T(8,128)(2,1)S(1)}, u32[]{:S(2)}, u32[]{:S(2)}) %collective-permute-start.4) | collective-permute-done | bytes 458784 | tf_op jit(solution)/shard_map/ppermute | solution.py:22
  34.5 3.2 %collective-permute-start.5 = (bf16[32,3584]{1,0:T(8,128)(2,1)S(1)}, bf16[32,3584]{1,0:T(8,128)(2,1)S(1)}, u32[]{:S(2)}, u32[]{:S(2)}) collective-permute-start(bf16[32,3584]{1,0:T(8,128)(2,1)S(1)} %slice.198), channel_id=1, source_target_pairs={{0,24},{1,25},{2,26},{3,27},{4,28},{5,29},{6,30},{7,31},{8,0},{9,1... | collective-permute-start | bytes 688136 | tf_op jit(solution)/shard_map/ppermute | solution.py:22
  38.0 3.4 %collective-permute-done.5 = bf16[32,3584]{1,0:T(8,128)(2,1)S(1)} collective-permute-done((bf16[32,3584]{1,0:T(8,128)(2,1)S(1)}, bf16[32,3584]{1,0:T(8,128)(2,1)S(1)}, u32[]{:S(2)}, u32[]{:S(2)}) %collective-permute-start.5) | collective-permute-done | bytes 229408 | tf_op jit(solution)/shard_map/ppermute | solution.py:22
  41.4 3.2 %collective-permute-done.7 = bf16[32,3584]{1,0:T(8,128)(2,1)S(1)} collective-permute-done((bf16[32,3584]{1,0:T(8,128)(2,1)S(1)}, bf16[32,3584]{1,0:T(8,128)(2,1)S(1)}, u32[]{:S(2)}, u32[]{:S(2)}) %collective-permute-start.7) | collective-permute-done | bytes 229408 | tf_op jit(solution)/shard_map/ppermute | solution.py:22
  44.7 1.6 fusion.5
  46.3 2.6 %collective-permute-start.15 = (f32[256,768]{1,0:T(8,128)S(1)}, f32[256,768]{1,0:T(8,128)S(1)}, u32[]{:S(2)}, u32[]{:S(2)}) collective-permute-start(f32[256,768]{1,0:T(8,128)S(1)} %fusion.5), channel_id=1, source_target_pairs={{0,32},{32,0},{64,96},{96,64},{1,33},{33,1},{65,97},{97,65},{2,34}... | collective-permute-start | bytes 2359304 | tf_op jit(solution)/shard_map/ppermute | solution.py:26
  48.9 1.6 fusion.7
  53.5 7.9 %collective-permute-done.16 = bf16[256,768]{1,0:T(8,128)(2,1)S(1)} collective-permute-done((bf16[256,768]{1,0:T(8,128)(2,1)S(1)}, bf16[256,768]{1,0:T(8,128)(2,1)S(1)}, u32[]{:S(2)}, u32[]{:S(2)}) %collective-permute-start.16) | collective-permute-done | bytes 393248 | tf_op jit(solution)/shard_map/ppermute | solution.py:26
  62.0 1.5 collective-permute-start.17
  64.8 4.1 %convolution_convert_fusion.2 = bf16[256,3584]{1,0:T(8,128)(2,1)S(1)} fusion(bf16[256,768]{1,0:T(8,128)(2,1)S(1)} %fusion.16, bf16[768,3584]{1,0:T(8,128)(2,1)} %bitcast.25), kind=kOutput, calls=%fused_computation.13 | convolution fusion | flops 1410203648 | bytes 7733248 | tf_op jit(solution)/shard_map/dot_general | solution.py:119
  69.1 2.9 %collective-permute-start.20 = (bf16[64,3584]{1,0:T(8,128)(2,1)S(1)}, bf16[64,3584]{1,0:T(8,128)(2,1)S(1)}, u32[]{:S(2)}, u32[]{:S(2)}) collective-permute-start(bf16[64,3584]{1,0:T(8,128)(2,1)S(1)} %get-tuple-element.45), channel_id=1, source_target_pairs={{0,24},{1,25},{2,26},{3,27},{4,28},{5,29},{6,30},{7,31},{8,0},{9,1... | collective-permute-start | bytes 1376264 | tf_op jit(solution)/shard_map/ppermute | solution.py:22
  72.0 4.1 %convolution_convert_fusion.1 = bf16[256,3584]{1,0:T(8,128)(2,1)S(1)} fusion(bf16[256,768]{1,0:T(8,128)(2,1)S(1)} %collective-permute-done.17, bf16[768,3584]{1,0:T(8,128)(2,1)} %bitcast.26), kind=kOutput, calls=%fused_computation.12 | convolution fusion | flops 1410203648 | bytes 7733248 | tf_op jit(solution)/shard_map/dot_general | solution.py:119
  76.5 2.4 %collective-permute-start.35 = (bf16[64,3584]{1,0:T(8,128)(2,1)S(1)}, bf16[64,3584]{1,0:T(8,128)(2,1)S(1)}, u32[]{:S(2)}, u32[]{:S(2)}) collective-permute-start(bf16[64,3584]{1,0:T(8,128)(2,1)S(1)} %get-tuple-element.41), channel_id=1, source_target_pairs={{0,3},{1,0},{2,1},{3,2},{4,7},{5,4},{6,5},{7,6},{8,11},{9,8},{10,9... | collective-permute-start | bytes 1376264 | tf_op jit(solution)/shard_map/ppermute | solution.py:22
  79.2 2.7 %collective-permute-start.21 = (bf16[32,3584]{1,0:T(8,128)(2,1)S(1)}, bf16[32,3584]{1,0:T(8,128)(2,1)S(1)}, u32[]{:S(2)}, u32[]{:S(2)}) collective-permute-start(bf16[32,3584]{1,0:T(8,128)(2,1)S(1)} %get-tuple-element.43), channel_id=1, source_target_pairs={{0,24},{1,25},{2,26},{3,27},{4,28},{5,29},{6,30},{7,31},{8,0},{9,1... | collective-permute-start | bytes 688136 | tf_op jit(solution)/shard_map/ppermute | solution.py:22
  81.8 3.4 %collective-permute-done.33 = bf16[64,3584]{1,0:T(8,128)(2,1)S(1)} collective-permute-done((bf16[64,3584]{1,0:T(8,128)(2,1)S(1)}, bf16[64,3584]{1,0:T(8,128)(2,1)S(1)}, u32[]{:S(2)}, u32[]{:S(2)}) %collective-permute-start.33) | collective-permute-done | bytes 458784 | tf_op jit(solution)/shard_map/ppermute | solution.py:22
  85.5 2.7 %collective-permute-start.36 = (bf16[32,3584]{1,0:T(8,128)(2,1)S(1)}, bf16[32,3584]{1,0:T(8,128)(2,1)S(1)}, u32[]{:S(2)}, u32[]{:S(2)}) collective-permute-start(bf16[32,3584]{1,0:T(8,128)(2,1)S(1)} %get-tuple-element.39), channel_id=1, source_target_pairs={{0,3},{1,0},{2,1},{3,2},{4,7},{5,4},{6,5},{7,6},{8,11},{9,8},{10,9... | collective-permute-start | bytes 688136 | tf_op jit(solution)/shard_map/ppermute | solution.py:22
  90.4 1.8 %collective-permute-start.24 = (bf16[16,3584]{1,0:T(8,128)(2,1)S(1)}, bf16[16,3584]{1,0:T(8,128)(2,1)S(1)}, u32[]{:S(2)}, u32[]{:S(2)}) collective-permute-start(bf16[16,3584]{1,0:T(8,128)(2,1)S(1)} %get-tuple-element.51), channel_id=1, source_target_pairs={{0,3},{1,0},{2,1},{3,2},{4,7},{5,4},{6,5},{7,6},{8,11},{9,8},{10,9... | collective-permute-start | bytes 344072 | tf_op jit(solution)/shard_map/ppermute | solution.py:22
  94.7 1.7 collective-permute-start.39
  96.5 3.4 %collective-permute-start.25 = (bf16[16,3584]{1,0:T(8,128)(2,1)S(1)}, bf16[16,3584]{1,0:T(8,128)(2,1)S(1)}, u32[]{:S(2)}, u32[]{:S(2)}) collective-permute-start(bf16[16,3584]{1,0:T(8,128)(2,1)S(1)} %fusion.30), channel_id=1, source_target_pairs={{0,4},{1,5},{2,6},{3,7},{4,0},{5,1},{6,2},{7,3},{8,12},{9,13},{10,... | collective-permute-start | bytes 344072 | tf_op jit(solution)/shard_map/ppermute | solution.py:22
  100.0 1.8 %collective-permute-done.38 = bf16[16,3584]{1,0:T(8,128)(2,1)S(1)} collective-permute-done((bf16[16,3584]{1,0:T(8,128)(2,1)S(1)}, bf16[16,3584]{1,0:T(8,128)(2,1)S(1)}, u32[]{:S(2)}, u32[]{:S(2)}) %collective-permute-start.38) | collective-permute-done | bytes 114720 | tf_op jit(solution)/shard_map/ppermute | solution.py:22
  101.8 3.6 %collective-permute-start.40 = (bf16[16,3584]{1,0:T(8,128)(2,1)S(1)}, bf16[16,3584]{1,0:T(8,128)(2,1)S(1)}, u32[]{:S(2)}, u32[]{:S(2)}) collective-permute-start(bf16[16,3584]{1,0:T(8,128)(2,1)S(1)} %fusion.31), channel_id=1, source_target_pairs={{0,4},{1,5},{2,6},{3,7},{4,0},{5,1},{6,2},{7,3},{8,12},{9,13},{10,... | collective-permute-start | bytes 344072 | tf_op jit(solution)/shard_map/ppermute | solution.py:22
  105.5 2.8 %collective-permute-done.40 = bf16[16,3584]{1,0:T(8,128)(2,1)S(1)} collective-permute-done((bf16[16,3584]{1,0:T(8,128)(2,1)S(1)}, bf16[16,3584]{1,0:T(8,128)(2,1)S(1)}, u32[]{:S(2)}, u32[]{:S(2)}) %collective-permute-start.40) | collective-permute-done | bytes 114720 | tf_op jit(solution)/shard_map/ppermute | solution.py:22
  110.1 2.0 %collective-permute-start.26 = (bf16[16,3584]{1,0:T(8,128)(2,1)S(1)}, bf16[16,3584]{1,0:T(8,128)(2,1)S(1)}, u32[]{:S(2)}, u32[]{:S(2)}) collective-permute-start(bf16[16,3584]{1,0:T(8,128)(2,1)S(1)} %get-tuple-element.64), channel_id=1, source_target_pairs={{0,3},{1,0},{2,1},{3,2},{4,7},{5,4},{6,5},{7,6},{8,11},{9,8},{10,9... | collective-permute-start | bytes 344072 | tf_op jit(solution)/shard_map/ppermute | solution.py:22
  112.8 1.5 collective-permute-done.42
  115.5 2.1 %collective-permute-start.44 = (bf16[64,3584]{1,0:T(8,128)(2,1)S(1)}, bf16[64,3584]{1,0:T(8,128)(2,1)S(1)}, u32[]{:S(2)}, u32[]{:S(2)}) collective-permute-start(bf16[64,3584]{1,0:T(8,128)(2,1)S(1)} %pad_maximum_fusion.4), channel_id=1, source_target_pairs={{0,3},{1,0},{2,1},{3,2},{4,7},{5,4},{6,5},{7,6},{8,11},{9,8},{10,9... | collective-permute-start | bytes 1376264 | tf_op jit(solution)/shard_map/ppermute | solution.py:22
  118.6 2.3 %collective-permute-start.29 = (bf16[64,3584]{1,0:T(8,128)(2,1)S(1)}, bf16[64,3584]{1,0:T(8,128)(2,1)S(1)}, u32[]{:S(2)}, u32[]{:S(2)}) collective-permute-start(bf16[64,3584]{1,0:T(8,128)(2,1)S(1)} %pad_maximum_fusion.3), channel_id=1, source_target_pairs={{0,24},{1,25},{2,26},{3,27},{4,28},{5,29},{6,30},{7,31},{8,0},{9,1... | collective-permute-start | bytes 1376264 | tf_op jit(solution)/shard_map/ppermute | solution.py:22
  121.0 2.5 %collective-permute-done.44 = bf16[64,3584]{1,0:T(8,128)(2,1)S(1)} collective-permute-done((bf16[64,3584]{1,0:T(8,128)(2,1)S(1)}, bf16[64,3584]{1,0:T(8,128)(2,1)S(1)}, u32[]{:S(2)}, u32[]{:S(2)}) %collective-permute-start.44) | collective-permute-done | bytes 458784 | tf_op jit(solution)/shard_map/ppermute | solution.py:22
  123.5 2.9 %collective-permute-start.45 = (bf16[32,3584]{1,0:T(8,128)(2,1)S(1)}, bf16[32,3584]{1,0:T(8,128)(2,1)S(1)}, u32[]{:S(2)}, u32[]{:S(2)}) collective-permute-start(bf16[32,3584]{1,0:T(8,128)(2,1)S(1)} %slice.234), channel_id=1, source_target_pairs={{0,3},{1,0},{2,1},{3,2},{4,7},{5,4},{6,5},{7,6},{8,11},{9,8},{10,9... | collective-permute-start | bytes 688136 | tf_op jit(solution)/shard_map/ppermute | solution.py:22
  128.6 3.2 %collective-permute-start.30 = (bf16[32,3584]{1,0:T(8,128)(2,1)S(1)}, bf16[32,3584]{1,0:T(8,128)(2,1)S(1)}, u32[]{:S(2)}, u32[]{:S(2)}) collective-permute-start(bf16[32,3584]{1,0:T(8,128)(2,1)S(1)} %slice.217), channel_id=1, source_target_pairs={{0,24},{1,25},{2,26},{3,27},{4,28},{5,29},{6,30},{7,31},{8,0},{9,1... | collective-permute-start | bytes 688136 | tf_op jit(solution)/shard_map/ppermute | solution.py:22
  132.1 1.7 collective-permute-done.47
  133.9 2.6 %collective-permute-done.30 = bf16[32,3584]{1,0:T(8,128)(2,1)S(1)} collective-permute-done((bf16[32,3584]{1,0:T(8,128)(2,1)S(1)}, bf16[32,3584]{1,0:T(8,128)(2,1)S(1)}, u32[]{:S(2)}, u32[]{:S(2)}) %collective-permute-start.30) | collective-permute-done | bytes 229408 | tf_op jit(solution)/shard_map/ppermute | solution.py:22
  136.5 3.7 %collective-permute-done.32 = bf16[32,3584]{1,0:T(8,128)(2,1)S(1)} collective-permute-done((bf16[32,3584]{1,0:T(8,128)(2,1)S(1)}, bf16[32,3584]{1,0:T(8,128)(2,1)S(1)}, u32[]{:S(2)}, u32[]{:S(2)}) %collective-permute-start.32) | collective-permute-done | bytes 229408 | tf_op jit(solution)/shard_map/ppermute | solution.py:22
  140.2 1.6 fusion.45
  141.9 9.6 %collective-permute-start.48 = (f32[264,768]{1,0:T(8,128)S(1)}, f32[264,768]{1,0:T(8,128)S(1)}, u32[]{:S(2)}, u32[]{:S(2)}) collective-permute-start(f32[264,768]{1,0:T(8,128)S(1)} %pad_maximum_fusion), channel_id=1, source_target_pairs={{0,32},{32,0},{64,96},{96,64},{1,33},{33,1},{65,97},{97,65},{2,34}... | collective-permute-start | bytes 2433032 | tf_op jit(solution)/shard_map/ppermute | solution.py:26
  151.7 1.6 fusion.44
  155.1 5.4 %fusion.3 = bf16[768,3584]{1,0:T(8,128)(2,1)} fusion(bf16[768,3584]{1,0:T(8,128)(2,1)S(1)} %bitcast.34, bf16[512,768]{1,0:T(8,128)(2,1)S(1)} %constant_dynamic-update-slice_fusion.32, f32[768]{0:T(1024)S(1)} %add_sqrt_fusion, f32[768]{0:T(1024)S(1)} %broadcast_multiply_fusion, bf16[256,3584]{1,0:T(8,128)(2,1)S(1)} %constant_dynamic-update-slice_fusion.24, ...), kind=kOutput, calls=%fused_computation.5 | convolution fusion | flops 2839674880 | bytes 15472640 | tf_op jit(solution)/shard_map/dot_general | solution.py:140
  160.4 3.9 %collective-permute-done.49 = bf16[264,768]{1,0:T(8,128)(2,1)S(1)} collective-permute-done((bf16[264,768]{1,0:T(8,128)(2,1)S(1)}, bf16[264,768]{1,0:T(8,128)(2,1)S(1)}, u32[]{:S(2)}, u32[]{:S(2)}) %collective-permute-start.49) | collective-permute-done | bytes 405536 | tf_op jit(solution)/shard_map/ppermute | solution.py:26
  166.2 1.3 collective-permute-done.50
  168.2 4.8 %fusion.4 = bf16[1,3584,768]{2,1,0:T(8,128)(2,1)} fusion(bf16[256,3584]{1,0:T(8,128)(2,1)S(1)} %copy-done.5, bf16[256,3584]{1,0:T(8,128)(2,1)S(1)} %copy-done.3, bf16[256,768]{1,0:T(8,128)(2,1)S(1)} %collective-permute-done.50, bf16[256,768]{1,0:T(8,128)(2,1)S(1)} %get-tuple-element.28), kind=kOutput, calls=%fused_computation.7 | convolution fusion | flops 2830237696 | bytes 9961472 | tf_op jit(solution)/shard_map/dot_general | solution.py:154
  (168 shorter events, 27.7 us)
Async XLA Ops:
  0.6 7.6 %collective-permute-start = (bf16[16,3584]{1,0:T(8,128)(2,1)}, bf16[16,3584]{1,0:T(8,128)(2,1)S(1)}, u32[]{:S(2)}, u32[]{:S(2)}) collective-permute-start(bf16[16,3584]{1,0:T(8,128)(2,1)} %bitcast.35), channel_id=1, source_target_pairs={{0,4},{1,5},{2,6},{3,7},{4,0},{5,1},{6,2},{7,3},{8,12},{9,13},{10,... | collective-permute-start | bytes 344072 | tf_op jit(solution)/shard_map/ppermute | solution.py:22
  8.3 6.8 %collective-permute-start.8 = (bf16[16,3584]{1,0:T(8,128)(2,1)S(1)}, bf16[16,3584]{1,0:T(8,128)(2,1)S(1)}, u32[]{:S(2)}, u32[]{:S(2)}) collective-permute-start(bf16[16,3584]{1,0:T(8,128)(2,1)S(1)} %get-tuple-element.36), channel_id=1, source_target_pairs={{0,24},{1,25},{2,26},{3,27},{4,28},{5,29},{6,30},{7,31},{8,0},{9,1... | collective-permute-start | bytes 344072 | tf_op jit(solution)/shard_map/ppermute | solution.py:22
  11.1 5.3 %collective-permute-start.9 = (bf16[16,3584]{1,0:T(8,128)(2,1)S(1)}, bf16[16,3584]{1,0:T(8,128)(2,1)S(1)}, u32[]{:S(2)}, u32[]{:S(2)}) collective-permute-start(bf16[16,3584]{1,0:T(8,128)(2,1)S(1)} %get-tuple-element.36), channel_id=1, source_target_pairs={{0,16},{1,17},{2,18},{3,19},{4,20},{5,21},{6,22},{7,23},{8,24},{9,... | collective-permute-start | bytes 344072 | tf_op jit(solution)/shard_map/ppermute | solution.py:22
  11.4 6.3 %collective-permute-start.10 = (bf16[16,3584]{1,0:T(8,128)(2,1)S(1)}, bf16[16,3584]{1,0:T(8,128)(2,1)S(1)}, u32[]{:S(2)}, u32[]{:S(2)}) collective-permute-start(bf16[16,3584]{1,0:T(8,128)(2,1)S(1)} %get-tuple-element.36), channel_id=1, source_target_pairs={{0,8},{1,9},{2,10},{3,11},{4,12},{5,13},{6,14},{7,15},{8,16},{9,17... | collective-permute-start | bytes 344072 | tf_op jit(solution)/shard_map/ppermute | solution.py:22
  12.1 7.9 %collective-permute-start.1 = (bf16[16,3584]{1,0:T(8,128)(2,1)S(1)}, bf16[16,3584]{1,0:T(8,128)(2,1)S(1)}, u32[]{:S(2)}, u32[]{:S(2)}) collective-permute-start(bf16[16,3584]{1,0:T(8,128)(2,1)S(1)} %get-tuple-element.54), channel_id=1, source_target_pairs={{0,3},{1,0},{2,1},{3,2},{4,7},{5,4},{6,5},{7,6},{8,11},{9,8},{10,9... | collective-permute-start | bytes 344072 | tf_op jit(solution)/shard_map/ppermute | solution.py:22
  14.6 5.9 %collective-permute-start.2 = (bf16[16,3584]{1,0:T(8,128)(2,1)S(1)}, bf16[16,3584]{1,0:T(8,128)(2,1)S(1)}, u32[]{:S(2)}, u32[]{:S(2)}) collective-permute-start(bf16[16,3584]{1,0:T(8,128)(2,1)S(1)} %get-tuple-element.54), channel_id=1, source_target_pairs={{0,2},{1,3},{2,0},{3,1},{4,6},{5,7},{6,4},{7,5},{8,10},{9,11},{10,... | collective-permute-start | bytes 344072 | tf_op jit(solution)/shard_map/ppermute | solution.py:22
  15.1 6.8 %collective-permute-start.3 = (bf16[16,3584]{1,0:T(8,128)(2,1)S(1)}, bf16[16,3584]{1,0:T(8,128)(2,1)S(1)}, u32[]{:S(2)}, u32[]{:S(2)}) collective-permute-start(bf16[16,3584]{1,0:T(8,128)(2,1)S(1)} %get-tuple-element.54), channel_id=1, source_target_pairs={{0,1},{1,2},{2,3},{3,0},{4,5},{5,6},{6,7},{7,4},{8,9},{9,10},{10,1... | collective-permute-start | bytes 344072 | tf_op jit(solution)/shard_map/ppermute | solution.py:22
  17.8 7.7 %collective-permute-start.11 = (bf16[64,3584]{1,0:T(8,128)(2,1)S(1)}, bf16[64,3584]{1,0:T(8,128)(2,1)S(1)}, u32[]{:S(2)}, u32[]{:S(2)}) collective-permute-start(bf16[64,3584]{1,0:T(8,128)(2,1)S(1)} %pad_maximum_fusion.2), channel_id=1, source_target_pairs={{0,3},{1,0},{2,1},{3,2},{4,7},{5,4},{6,5},{7,6},{8,11},{9,8},{10,9... | collective-permute-start | bytes 1376264 | tf_op jit(solution)/shard_map/ppermute | solution.py:22
  20.0 8.6 %collective-permute-start.13 = (bf16[64,3584]{1,0:T(8,128)(2,1)S(1)}, bf16[64,3584]{1,0:T(8,128)(2,1)S(1)}, u32[]{:S(2)}, u32[]{:S(2)}) collective-permute-start(bf16[64,3584]{1,0:T(8,128)(2,1)S(1)} %pad_maximum_fusion.2), channel_id=1, source_target_pairs={{0,1},{1,2},{2,3},{3,0},{4,5},{5,6},{6,7},{7,4},{8,9},{9,10},{10,1... | collective-permute-start | bytes 1376264 | tf_op jit(solution)/shard_map/ppermute | solution.py:22
  22.0 12.5 %collective-permute-start.4 = (bf16[64,3584]{1,0:T(8,128)(2,1)S(1)}, bf16[64,3584]{1,0:T(8,128)(2,1)S(1)}, u32[]{:S(2)}, u32[]{:S(2)}) collective-permute-start(bf16[64,3584]{1,0:T(8,128)(2,1)S(1)} %pad_maximum_fusion.1), channel_id=1, source_target_pairs={{0,24},{1,25},{2,26},{3,27},{4,28},{5,29},{6,30},{7,31},{8,0},{9,1... | collective-permute-start | bytes 1376264 | tf_op jit(solution)/shard_map/ppermute | solution.py:22
  24.7 13.0 %collective-permute-start.6 = (bf16[64,3584]{1,0:T(8,128)(2,1)S(1)}, bf16[64,3584]{1,0:T(8,128)(2,1)S(1)}, u32[]{:S(2)}, u32[]{:S(2)}) collective-permute-start(bf16[64,3584]{1,0:T(8,128)(2,1)S(1)} %pad_maximum_fusion.1), channel_id=1, source_target_pairs={{0,8},{1,9},{2,10},{3,11},{4,12},{5,13},{6,14},{7,15},{8,16},{9,17... | collective-permute-start | bytes 1376264 | tf_op jit(solution)/shard_map/ppermute | solution.py:22
  25.5 12.4 %collective-permute-start.12 = (bf16[32,3584]{1,0:T(8,128)(2,1)S(1)}, bf16[32,3584]{1,0:T(8,128)(2,1)S(1)}, u32[]{:S(2)}, u32[]{:S(2)}) collective-permute-start(bf16[32,3584]{1,0:T(8,128)(2,1)S(1)} %slice.200), channel_id=1, source_target_pairs={{0,3},{1,0},{2,1},{3,2},{4,7},{5,4},{6,5},{7,6},{8,11},{9,8},{10,9... | collective-permute-start | bytes 688136 | tf_op jit(solution)/shard_map/ppermute | solution.py:22
  28.7 9.2 %collective-permute-start.14 = (bf16[32,3584]{1,0:T(8,128)(2,1)S(1)}, bf16[32,3584]{1,0:T(8,128)(2,1)S(1)}, u32[]{:S(2)}, u32[]{:S(2)}) collective-permute-start(bf16[32,3584]{1,0:T(8,128)(2,1)S(1)} %slice.201), channel_id=1, source_target_pairs={{0,1},{1,2},{2,3},{3,0},{4,5},{5,6},{6,7},{7,4},{8,9},{9,10},{10,1... | collective-permute-start | bytes 688136 | tf_op jit(solution)/shard_map/ppermute | solution.py:22
  34.5 6.8 %collective-permute-start.5 = (bf16[32,3584]{1,0:T(8,128)(2,1)S(1)}, bf16[32,3584]{1,0:T(8,128)(2,1)S(1)}, u32[]{:S(2)}, u32[]{:S(2)}) collective-permute-start(bf16[32,3584]{1,0:T(8,128)(2,1)S(1)} %slice.198), channel_id=1, source_target_pairs={{0,24},{1,25},{2,26},{3,27},{4,28},{5,29},{6,30},{7,31},{8,0},{9,1... | collective-permute-start | bytes 688136 | tf_op jit(solution)/shard_map/ppermute | solution.py:22
  37.7 6.9 %collective-permute-start.7 = (bf16[32,3584]{1,0:T(8,128)(2,1)S(1)}, bf16[32,3584]{1,0:T(8,128)(2,1)S(1)}, u32[]{:S(2)}, u32[]{:S(2)}) collective-permute-start(bf16[32,3584]{1,0:T(8,128)(2,1)S(1)} %slice.199), channel_id=1, source_target_pairs={{0,8},{1,9},{2,10},{3,11},{4,12},{5,13},{6,14},{7,15},{8,16},{9,17... | collective-permute-start | bytes 688136 | tf_op jit(solution)/shard_map/ppermute | solution.py:22
  46.3 4.5 %collective-permute-start.15 = (f32[256,768]{1,0:T(8,128)S(1)}, f32[256,768]{1,0:T(8,128)S(1)}, u32[]{:S(2)}, u32[]{:S(2)}) collective-permute-start(f32[256,768]{1,0:T(8,128)S(1)} %fusion.5), channel_id=1, source_target_pairs={{0,32},{32,0},{64,96},{96,64},{1,33},{33,1},{65,97},{97,65},{2,34}... | collective-permute-start | bytes 2359304 | tf_op jit(solution)/shard_map/ppermute | solution.py:26
  51.0 10.4 %collective-permute-start.16 = (bf16[256,768]{1,0:T(8,128)(2,1)S(1)}, bf16[256,768]{1,0:T(8,128)(2,1)S(1)}, u32[]{:S(2)}, u32[]{:S(2)}) collective-permute-start(bf16[256,768]{1,0:T(8,128)(2,1)S(1)} %get-tuple-element.33), channel_id=1, source_target_pairs={{0,64},{32,96},{64,0},{96,32},{1,65},{33,97},{65,1},{97,33},{2,66}... | collective-permute-start | bytes 1179656 | tf_op jit(solution)/shard_map/ppermute | solution.py:26
  69.0 10.0 %collective-permute-start.18 = (bf16[64,3584]{1,0:T(8,128)(2,1)S(1)}, bf16[64,3584]{1,0:T(8,128)(2,1)S(1)}, u32[]{:S(2)}, u32[]{:S(2)}) collective-permute-start(bf16[64,3584]{1,0:T(8,128)(2,1)S(1)} %get-tuple-element.46), channel_id=1, source_target_pairs={{0,8},{1,9},{2,10},{3,11},{4,12},{5,13},{6,14},{7,15},{8,16},{9,17... | collective-permute-start | bytes 1376264 | tf_op jit(solution)/shard_map/ppermute | solution.py:22
  69.1 9.9 %collective-permute-start.20 = (bf16[64,3584]{1,0:T(8,128)(2,1)S(1)}, bf16[64,3584]{1,0:T(8,128)(2,1)S(1)}, u32[]{:S(2)}, u32[]{:S(2)}) collective-permute-start(bf16[64,3584]{1,0:T(8,128)(2,1)S(1)} %get-tuple-element.45), channel_id=1, source_target_pairs={{0,24},{1,25},{2,26},{3,27},{4,28},{5,29},{6,30},{7,31},{8,0},{9,1... | collective-permute-start | bytes 1376264 | tf_op jit(solution)/shard_map/ppermute | solution.py:22
  76.2 9.1 %collective-permute-start.33 = (bf16[64,3584]{1,0:T(8,128)(2,1)S(1)}, bf16[64,3584]{1,0:T(8,128)(2,1)S(1)}, u32[]{:S(2)}, u32[]{:S(2)}) collective-permute-start(bf16[64,3584]{1,0:T(8,128)(2,1)S(1)} %get-tuple-element.42), channel_id=1, source_target_pairs={{0,1},{1,2},{2,3},{3,0},{4,5},{5,6},{6,7},{7,4},{8,9},{9,10},{10,1... | collective-permute-start | bytes 1376264 | tf_op jit(solution)/shard_map/ppermute | solution.py:22
  76.5 8.8 %collective-permute-start.35 = (bf16[64,3584]{1,0:T(8,128)(2,1)S(1)}, bf16[64,3584]{1,0:T(8,128)(2,1)S(1)}, u32[]{:S(2)}, u32[]{:S(2)}) collective-permute-start(bf16[64,3584]{1,0:T(8,128)(2,1)S(1)} %get-tuple-element.41), channel_id=1, source_target_pairs={{0,3},{1,0},{2,1},{3,2},{4,7},{5,4},{6,5},{7,6},{8,11},{9,8},{10,9... | collective-permute-start | bytes 1376264 | tf_op jit(solution)/shard_map/ppermute | solution.py:22
  79.1 9.1 %collective-permute-start.19 = (bf16[32,3584]{1,0:T(8,128)(2,1)S(1)}, bf16[32,3584]{1,0:T(8,128)(2,1)S(1)}, u32[]{:S(2)}, u32[]{:S(2)}) collective-permute-start(bf16[32,3584]{1,0:T(8,128)(2,1)S(1)} %get-tuple-element.44), channel_id=1, source_target_pairs={{0,8},{1,9},{2,10},{3,11},{4,12},{5,13},{6,14},{7,15},{8,16},{9,17... | collective-permute-start | bytes 688136 | tf_op jit(solution)/shard_map/ppermute | solution.py:22
  79.2 9.1 %collective-permute-start.21 = (bf16[32,3584]{1,0:T(8,128)(2,1)S(1)}, bf16[32,3584]{1,0:T(8,128)(2,1)S(1)}, u32[]{:S(2)}, u32[]{:S(2)}) collective-permute-start(bf16[32,3584]{1,0:T(8,128)(2,1)S(1)} %get-tuple-element.43), channel_id=1, source_target_pairs={{0,24},{1,25},{2,26},{3,27},{4,28},{5,29},{6,30},{7,31},{8,0},{9,1... | collective-permute-start | bytes 688136 | tf_op jit(solution)/shard_map/ppermute | solution.py:22
  85.4 6.8 %collective-permute-start.34 = (bf16[32,3584]{1,0:T(8,128)(2,1)S(1)}, bf16[32,3584]{1,0:T(8,128)(2,1)S(1)}, u32[]{:S(2)}, u32[]{:S(2)}) collective-permute-start(bf16[32,3584]{1,0:T(8,128)(2,1)S(1)} %get-tuple-element.40), channel_id=1, source_target_pairs={{0,1},{1,2},{2,3},{3,0},{4,5},{5,6},{6,7},{7,4},{8,9},{9,10},{10,1... | collective-permute-start | bytes 688136 | tf_op jit(solution)/shard_map/ppermute | solution.py:22
  85.5 6.9 %collective-permute-start.36 = (bf16[32,3584]{1,0:T(8,128)(2,1)S(1)}, bf16[32,3584]{1,0:T(8,128)(2,1)S(1)}, u32[]{:S(2)}, u32[]{:S(2)}) collective-permute-start(bf16[32,3584]{1,0:T(8,128)(2,1)S(1)} %get-tuple-element.39), channel_id=1, source_target_pairs={{0,3},{1,0},{2,1},{3,2},{4,7},{5,4},{6,5},{7,6},{8,11},{9,8},{10,9... | collective-permute-start | bytes 688136 | tf_op jit(solution)/shard_map/ppermute | solution.py:22
  88.5 6.3 %collective-permute-start.22 = (bf16[16,3584]{1,0:T(8,128)(2,1)S(1)}, bf16[16,3584]{1,0:T(8,128)(2,1)S(1)}, u32[]{:S(2)}, u32[]{:S(2)}) collective-permute-start(bf16[16,3584]{1,0:T(8,128)(2,1)S(1)} %get-tuple-element.50), channel_id=1, source_target_pairs={{0,2},{1,3},{2,0},{3,1},{4,6},{5,7},{6,4},{7,5},{8,10},{9,11},{10,... | collective-permute-start | bytes 344072 | tf_op jit(solution)/shard_map/ppermute | solution.py:22
  89.5 6.9 %collective-permute-start.23 = (bf16[16,3584]{1,0:T(8,128)(2,1)S(1)}, bf16[16,3584]{1,0:T(8,128)(2,1)S(1)}, u32[]{:S(2)}, u32[]{:S(2)}) collective-permute-start(bf16[16,3584]{1,0:T(8,128)(2,1)S(1)} %get-tuple-element.52), channel_id=1, source_target_pairs={{0,1},{1,2},{2,3},{3,0},{4,5},{5,6},{6,7},{7,4},{8,9},{9,10},{10,1... | collective-permute-start | bytes 344072 | tf_op jit(solution)/shard_map/ppermute | solution.py:22
  90.4 6.1 %collective-permute-start.24 = (bf16[16,3584]{1,0:T(8,128)(2,1)S(1)}, bf16[16,3584]{1,0:T(8,128)(2,1)S(1)}, u32[]{:S(2)}, u32[]{:S(2)}) collective-permute-start(bf16[16,3584]{1,0:T(8,128)(2,1)S(1)} %get-tuple-element.51), channel_id=1, source_target_pairs={{0,3},{1,0},{2,1},{3,2},{4,7},{5,4},{6,5},{7,6},{8,11},{9,8},{10,9... | collective-permute-start | bytes 344072 | tf_op jit(solution)/shard_map/ppermute | solution.py:22
  92.5 7.4 %collective-permute-start.37 = (bf16[16,3584]{1,0:T(8,128)(2,1)S(1)}, bf16[16,3584]{1,0:T(8,128)(2,1)S(1)}, u32[]{:S(2)}, u32[]{:S(2)}) collective-permute-start(bf16[16,3584]{1,0:T(8,128)(2,1)S(1)} %get-tuple-element.47), channel_id=1, source_target_pairs={{0,16},{1,17},{2,18},{3,19},{4,20},{5,21},{6,22},{7,23},{8,24},{9,... | collective-permute-start | bytes 344072 | tf_op jit(solution)/shard_map/ppermute | solution.py:22
  93.8 8.0 %collective-permute-start.38 = (bf16[16,3584]{1,0:T(8,128)(2,1)S(1)}, bf16[16,3584]{1,0:T(8,128)(2,1)S(1)}, u32[]{:S(2)}, u32[]{:S(2)}) collective-permute-start(bf16[16,3584]{1,0:T(8,128)(2,1)S(1)} %get-tuple-element.49), channel_id=1, source_target_pairs={{0,8},{1,9},{2,10},{3,11},{4,12},{5,13},{6,14},{7,15},{8,16},{9,17... | collective-permute-start | bytes 344072 | tf_op jit(solution)/shard_map/ppermute | solution.py:22
  94.7 7.0 %collective-permute-start.39 = (bf16[16,3584]{1,0:T(8,128)(2,1)S(1)}, bf16[16,3584]{1,0:T(8,128)(2,1)S(1)}, u32[]{:S(2)}, u32[]{:S(2)}) collective-permute-start(bf16[16,3584]{1,0:T(8,128)(2,1)S(1)} %get-tuple-element.48), channel_id=1, source_target_pairs={{0,24},{1,25},{2,26},{3,27},{4,28},{5,29},{6,30},{7,31},{8,0},{9,1... | collective-permute-start | bytes 344072 | tf_op jit(solution)/shard_map/ppermute | solution.py:22
  96.5 8.9 %collective-permute-start.25 = (bf16[16,3584]{1,0:T(8,128)(2,1)S(1)}, bf16[16,3584]{1,0:T(8,128)(2,1)S(1)}, u32[]{:S(2)}, u32[]{:S(2)}) collective-permute-start(bf16[16,3584]{1,0:T(8,128)(2,1)S(1)} %fusion.30), channel_id=1, source_target_pairs={{0,4},{1,5},{2,6},{3,7},{4,0},{5,1},{6,2},{7,3},{8,12},{9,13},{10,... | collective-permute-start | bytes 344072 | tf_op jit(solution)/shard_map/ppermute | solution.py:22
  101.8 6.5 %collective-permute-start.40 = (bf16[16,3584]{1,0:T(8,128)(2,1)S(1)}, bf16[16,3584]{1,0:T(8,128)(2,1)S(1)}, u32[]{:S(2)}, u32[]{:S(2)}) collective-permute-start(bf16[16,3584]{1,0:T(8,128)(2,1)S(1)} %fusion.31), channel_id=1, source_target_pairs={{0,4},{1,5},{2,6},{3,7},{4,0},{5,1},{6,2},{7,3},{8,12},{9,13},{10,... | collective-permute-start | bytes 344072 | tf_op jit(solution)/shard_map/ppermute | solution.py:22
  109.1 5.2 %collective-permute-start.42 = (bf16[16,3584]{1,0:T(8,128)(2,1)S(1)}, bf16[16,3584]{1,0:T(8,128)(2,1)S(1)}, u32[]{:S(2)}, u32[]{:S(2)}) collective-permute-start(bf16[16,3584]{1,0:T(8,128)(2,1)S(1)} %get-tuple-element.30), channel_id=1, source_target_pairs={{0,16},{1,17},{2,18},{3,19},{4,20},{5,21},{6,22},{7,23},{8,24},{9,... | collective-permute-start | bytes 344072 | tf_op jit(solution)/shard_map/ppermute | solution.py:22
  109.1 6.4 %collective-permute-start.43 = (bf16[16,3584]{1,0:T(8,128)(2,1)S(1)}, bf16[16,3584]{1,0:T(8,128)(2,1)S(1)}, u32[]{:S(2)}, u32[]{:S(2)}) collective-permute-start(bf16[16,3584]{1,0:T(8,128)(2,1)S(1)} %get-tuple-element.30), channel_id=1, source_target_pairs={{0,8},{1,9},{2,10},{3,11},{4,12},{5,13},{6,14},{7,15},{8,16},{9,17... | collective-permute-start | bytes 344072 | tf_op jit(solution)/shard_map/ppermute | solution.py:22
  110.1 7.5 %collective-permute-start.26 = (bf16[16,3584]{1,0:T(8,128)(2,1)S(1)}, bf16[16,3584]{1,0:T(8,128)(2,1)S(1)}, u32[]{:S(2)}, u32[]{:S(2)}) collective-permute-start(bf16[16,3584]{1,0:T(8,128)(2,1)S(1)} %get-tuple-element.64), channel_id=1, source_target_pairs={{0,3},{1,0},{2,1},{3,2},{4,7},{5,4},{6,5},{7,6},{8,11},{9,8},{10,9... | collective-permute-start | bytes 344072 | tf_op jit(solution)/shard_map/ppermute | solution.py:22
  112.2 5.4 %collective-permute-start.27 = (bf16[16,3584]{1,0:T(8,128)(2,1)S(1)}, bf16[16,3584]{1,0:T(8,128)(2,1)S(1)}, u32[]{:S(2)}, u32[]{:S(2)}) collective-permute-start(bf16[16,3584]{1,0:T(8,128)(2,1)S(1)} %get-tuple-element.64), channel_id=1, source_target_pairs={{0,2},{1,3},{2,0},{3,1},{4,6},{5,7},{6,4},{7,5},{8,10},{9,11},{10,... | collective-permute-start | bytes 344072 | tf_op jit(solution)/shard_map/ppermute | solution.py:22
  112.5 6.0 %collective-permute-start.28 = (bf16[16,3584]{1,0:T(8,128)(2,1)S(1)}, bf16[16,3584]{1,0:T(8,128)(2,1)S(1)}, u32[]{:S(2)}, u32[]{:S(2)}) collective-permute-start(bf16[16,3584]{1,0:T(8,128)(2,1)S(1)} %get-tuple-element.64), channel_id=1, source_target_pairs={{0,1},{1,2},{2,3},{3,0},{4,5},{5,6},{6,7},{7,4},{8,9},{9,10},{10,1... | collective-permute-start | bytes 344072 | tf_op jit(solution)/shard_map/ppermute | solution.py:22
  115.5 7.9 %collective-permute-start.44 = (bf16[64,3584]{1,0:T(8,128)(2,1)S(1)}, bf16[64,3584]{1,0:T(8,128)(2,1)S(1)}, u32[]{:S(2)}, u32[]{:S(2)}) collective-permute-start(bf16[64,3584]{1,0:T(8,128)(2,1)S(1)} %pad_maximum_fusion.4), channel_id=1, source_target_pairs={{0,3},{1,0},{2,1},{3,2},{4,7},{5,4},{6,5},{7,6},{8,11},{9,8},{10,9... | collective-permute-start | bytes 1376264 | tf_op jit(solution)/shard_map/ppermute | solution.py:22
  117.6 9.8 %collective-permute-start.46 = (bf16[64,3584]{1,0:T(8,128)(2,1)S(1)}, bf16[64,3584]{1,0:T(8,128)(2,1)S(1)}, u32[]{:S(2)}, u32[]{:S(2)}) collective-permute-start(bf16[64,3584]{1,0:T(8,128)(2,1)S(1)} %pad_maximum_fusion.4), channel_id=1, source_target_pairs={{0,1},{1,2},{2,3},{3,0},{4,5},{5,6},{6,7},{7,4},{8,9},{9,10},{10,1... | collective-permute-start | bytes 1376264 | tf_op jit(solution)/shard_map/ppermute | solution.py:22
  118.6 10.0 %collective-permute-start.29 = (bf16[64,3584]{1,0:T(8,128)(2,1)S(1)}, bf16[64,3584]{1,0:T(8,128)(2,1)S(1)}, u32[]{:S(2)}, u32[]{:S(2)}) collective-permute-start(bf16[64,3584]{1,0:T(8,128)(2,1)S(1)} %pad_maximum_fusion.3), channel_id=1, source_target_pairs={{0,24},{1,25},{2,26},{3,27},{4,28},{5,29},{6,30},{7,31},{8,0},{9,1... | collective-permute-start | bytes 1376264 | tf_op jit(solution)/shard_map/ppermute | solution.py:22
  120.9 11.0 %collective-permute-start.31 = (bf16[64,3584]{1,0:T(8,128)(2,1)S(1)}, bf16[64,3584]{1,0:T(8,128)(2,1)S(1)}, u32[]{:S(2)}, u32[]{:S(2)}) collective-permute-start(bf16[64,3584]{1,0:T(8,128)(2,1)S(1)} %pad_maximum_fusion.3), channel_id=1, source_target_pairs={{0,8},{1,9},{2,10},{3,11},{4,12},{5,13},{6,14},{7,15},{8,16},{9,17... | collective-permute-start | bytes 1376264 | tf_op jit(solution)/shard_map/ppermute | solution.py:22
  123.5 8.6 %collective-permute-start.45 = (bf16[32,3584]{1,0:T(8,128)(2,1)S(1)}, bf16[32,3584]{1,0:T(8,128)(2,1)S(1)}, u32[]{:S(2)}, u32[]{:S(2)}) collective-permute-start(bf16[32,3584]{1,0:T(8,128)(2,1)S(1)} %slice.234), channel_id=1, source_target_pairs={{0,3},{1,0},{2,1},{3,2},{4,7},{5,4},{6,5},{7,6},{8,11},{9,8},{10,9... | collective-permute-start | bytes 688136 | tf_op jit(solution)/shard_map/ppermute | solution.py:22
  127.4 6.4 %collective-permute-start.47 = (bf16[32,3584]{1,0:T(8,128)(2,1)S(1)}, bf16[32,3584]{1,0:T(8,128)(2,1)S(1)}, u32[]{:S(2)}, u32[]{:S(2)}) collective-permute-start(bf16[32,3584]{1,0:T(8,128)(2,1)S(1)} %slice.235), channel_id=1, source_target_pairs={{0,1},{1,2},{2,3},{3,0},{4,5},{5,6},{6,7},{7,4},{8,9},{9,10},{10,1... | collective-permute-start | bytes 688136 | tf_op jit(solution)/shard_map/ppermute | solution.py:22
  128.6 7.9 %collective-permute-start.30 = (bf16[32,3584]{1,0:T(8,128)(2,1)S(1)}, bf16[32,3584]{1,0:T(8,128)(2,1)S(1)}, u32[]{:S(2)}, u32[]{:S(2)}) collective-permute-start(bf16[32,3584]{1,0:T(8,128)(2,1)S(1)} %slice.217), channel_id=1, source_target_pairs={{0,24},{1,25},{2,26},{3,27},{4,28},{5,29},{6,30},{7,31},{8,0},{9,1... | collective-permute-start | bytes 688136 | tf_op jit(solution)/shard_map/ppermute | solution.py:22
  131.9 8.3 %collective-permute-start.32 = (bf16[32,3584]{1,0:T(8,128)(2,1)S(1)}, bf16[32,3584]{1,0:T(8,128)(2,1)S(1)}, u32[]{:S(2)}, u32[]{:S(2)}) collective-permute-start(bf16[32,3584]{1,0:T(8,128)(2,1)S(1)} %slice.218), channel_id=1, source_target_pairs={{0,8},{1,9},{2,10},{3,11},{4,12},{5,13},{6,14},{7,15},{8,16},{9,17... | collective-permute-start | bytes 688136 | tf_op jit(solution)/shard_map/ppermute | solution.py:22
  141.9 11.5 %collective-permute-start.48 = (f32[264,768]{1,0:T(8,128)S(1)}, f32[264,768]{1,0:T(8,128)S(1)}, u32[]{:S(2)}, u32[]{:S(2)}) collective-permute-start(f32[264,768]{1,0:T(8,128)S(1)} %pad_maximum_fusion), channel_id=1, source_target_pairs={{0,32},{32,0},{64,96},{96,64},{1,33},{33,1},{65,97},{97,65},{2,34}... | collective-permute-start | bytes 2433032 | tf_op jit(solution)/shard_map/ppermute | solution.py:26
  153.7 10.7 %collective-permute-start.49 = (bf16[264,768]{1,0:T(8,128)(2,1)S(1)}, bf16[264,768]{1,0:T(8,128)(2,1)S(1)}, u32[]{:S(2)}, u32[]{:S(2)}) collective-permute-start(bf16[264,768]{1,0:T(8,128)(2,1)S(1)} %pad_maximum_fusion.5), channel_id=1, source_target_pairs={{0,64},{32,96},{64,0},{96,32},{1,65},{33,97},{65,1},{97,33},{2,66}... | collective-permute-start | bytes 1216520 | tf_op jit(solution)/shard_map/ppermute | solution.py:26
  (14 other events, 128.0 us)

commit v4 on v3

--- a/solution.py
+++ b/solution.py
@@ -89,7 +89,7 @@
 
 
 def core_sum(keep, send):
-    return rounded(lax.optimization_barrier(keep) + layer_swap(send, 1))
+    return rounded(lax.optimization_barrier(keep) + wide(layer_swap(narrow(send), 1)))
 
 
 def per_device(residuals, enc_weight, dec_weight, enc_bias, dec_bias):
@@ -128,14 +128,16 @@
         )
         for rows in errors
     ]
-    norm_rows = jnp.broadcast_to(row_norms[None, :], (8, row_norms.shape[0]))
-    got = layer_swap(join(back[1], norm_rows), 1)
-    part = rounded(lax.optimization_barrier(back[0]) + got[:256])
-    chip_norms = row_norms + got[256]
-    head = rounded(chip_norms)
-    tail = rounded(chip_norms - head)
-    norm_rows = jnp.where(jnp.arange(8)[:, None] < 4, head[None, :], tail[None, :])
-    other = layer_swap(narrow(join(part, norm_rows)), 2)
+    def norm_rows(norms):
+        head = rounded(norms)
+        tail = rounded(norms - head)
+        return jnp.where(jnp.arange(8)[:, None] < 4, head[None, :], tail[None, :]), head + tail
+
+    extra, norms = norm_rows(row_norms)
+    got = layer_swap(narrow(join(back[1], extra)), 1)
+    part = rounded(lax.optimization_barrier(back[0]) + wide(got[:256]))
+    extra, norms = norm_rows(norms + (wide(got[256]) + wide(got[260])))
+    other = layer_swap(narrow(join(part, extra)), 2)
     act_sum = jnp.sum(wide(join(*latents)), axis=0)
     dec_acc = lax.dot_general(
         join(*latents),
@@ -146,7 +148,7 @@
     penalty_term = sparsity_weight * act_sum[:, None] * wide(dec_local) / row_norms[:, None]
     dec_grad = narrow(dec_acc + penalty_term)
     other, dec_grad = lax.optimization_barrier((other, dec_grad))
-    weight_sum = (head + tail) + (wide(other[256]) + wide(other[260]))
+    weight_sum = norms + (wide(other[256]) + wide(other[260]))
     lat_grad = part + wide(other[:256]) + sparsity_weight * weight_sum[None, :]
     kept = narrow(lat_grad * gate)
     pre_grads = [kept, layer_swap(kept, 1)]

time: 173 us -> 169 us (0.977)
  matrix products: 24.9 us -> 19.8 us
  waiting for transfers between devices: 58.9 us -> 56.6 us
    ppermute x45, starting transfers between devices: 63.8 us -> 69.6 us  [shift(): return lax.ppermute(value, ('layer', 'latent'), pairs)]
    dot_general x2, matrix products: 8.29 us -> 3.17 us  [per_device(): jnp.dot(latents[slot], dec_local, preferred_element_type=jnp.float32)]
    ppermute x6, starting transfers between devices: 17.6 us -> 13.5 us  [layer_swap(): return lax.ppermute(value, 'layer', [(i, i ^ bit) for i in range(4)])]
    ppermute x45, waiting for transfers between devices: 43.9 us -> 40.8 us  [shift(): return lax.ppermute(value, ('layer', 'latent'), pairs)]
  transfers between devices with their start and end apart: 51 -> 51, of which waited for: 30 -> 24; matrix products, arithmetic and copies ran while one was open for 10% -> 9% of each run, Pallas kernels for 0% -> 0%
where the time goes in v4:
time: 169 us
  starting transfers between devices  83.2 us (49%)
  waiting for transfers between devices  56.6 us (33%)
  matrix products  19.8 us (12%)
  other arithmetic  5.99 us (4%)
  local copies, waits for them, and re-layouts  1.86 us (1%)
    ppermute x45, starting transfers between devices, shift(): return lax.ppermute(value, ('layer', 'latent'), pairs)  69.6 us
    ppermute x45, waiting for transfers between devices, shift(): return lax.ppermute(value, ('layer', 'latent'), pairs)  40.8 us
    ppermute x6, waiting for transfers between devices, layer_swap(): return lax.ppermute(value, 'layer', [(i, i ^ bit) for i in range(4)])  15.8 us
    ppermute x6, starting transfers between devices, layer_swap(): return lax.ppermute(value, 'layer', [(i, i ^ bit) for i in range(4)])  13.5 us
    dot_general x1, matrix products, per_device(): lax.dot_general(join(*latents), join(*errors), (((0,), (0,)), ((), ())),...  5.4 us
    dot_general x1, matrix products, per_device(): lax.dot_general(join(*gathered), join(*pre_grads), (((0,), (0,)), ((), ()...  4.83 us
  transfers between devices with their start and end apart: 51, of which 24 were waited for; matrix products, arithmetic and copies ran while one was open for 9% of the time, Pallas kernels for 0%

profile of v4, /device:TPU:1, one launch (start us, length us, event | category | flops | bytes accessed | tf_op | source)
XLA Modules:
  0.0 168.7 jit_solution(267791342284475398)
XLA Ops:
  0.6 4.5 %collective-permute-start = (bf16[16,3584]{1,0:T(8,128)(2,1)}, bf16[16,3584]{1,0:T(8,128)(2,1)S(1)}, u32[]{:S(2)}, u32[]{:S(2)}) collective-permute-start(bf16[16,3584]{1,0:T(8,128)(2,1)} %bitcast.35), channel_id=1, source_target_pairs={{0,4},{1,5},{2,6},{3,7},{4,0},{5,1},{6,2},{7,3},{8,12},{9,13},{10,... | collective-permute-start | bytes 344072 | tf_op jit(solution)/shard_map/ppermute | solution.py:22
  6.0 2.2 %collective-permute-done = bf16[16,3584]{1,0:T(8,128)(2,1)S(1)} collective-permute-done((bf16[16,3584]{1,0:T(8,128)(2,1)}, bf16[16,3584]{1,0:T(8,128)(2,1)S(1)}, u32[]{:S(2)}, u32[]{:S(2)}) %collective-permute-start) | collective-permute-done | bytes 114720 | tf_op jit(solution)/shard_map/ppermute | solution.py:22
  8.9 2.7 %collective-permute-start.8 = (bf16[16,3584]{1,0:T(8,128)(2,1)S(1)}, bf16[16,3584]{1,0:T(8,128)(2,1)S(1)}, u32[]{:S(2)}, u32[]{:S(2)}) collective-permute-start(bf16[16,3584]{1,0:T(8,128)(2,1)S(1)} %get-tuple-element.36), channel_id=1, source_target_pairs={{0,24},{1,25},{2,26},{3,27},{4,28},{5,29},{6,30},{7,31},{8,0},{9,1... | collective-permute-start | bytes 344072 | tf_op jit(solution)/shard_map/ppermute | solution.py:22
  13.5 2.5 %collective-permute-start.1 = (bf16[16,3584]{1,0:T(8,128)(2,1)S(1)}, bf16[16,3584]{1,0:T(8,128)(2,1)S(1)}, u32[]{:S(2)}, u32[]{:S(2)}) collective-permute-start(bf16[16,3584]{1,0:T(8,128)(2,1)S(1)} %get-tuple-element.54), channel_id=1, source_target_pairs={{0,3},{1,0},{2,1},{3,2},{4,7},{5,4},{6,5},{7,6},{8,11},{9,8},{10,9... | collective-permute-start | bytes 344072 | tf_op jit(solution)/shard_map/ppermute | solution.py:22
  18.4 2.3 %collective-permute-start.11 = (bf16[64,3584]{1,0:T(8,128)(2,1)S(1)}, bf16[64,3584]{1,0:T(8,128)(2,1)S(1)}, u32[]{:S(2)}, u32[]{:S(2)}) collective-permute-start(bf16[64,3584]{1,0:T(8,128)(2,1)S(1)} %pad_maximum_fusion.1), channel_id=1, source_target_pairs={{0,3},{1,0},{2,1},{3,2},{4,7},{5,4},{6,5},{7,6},{8,11},{9,8},{10,9... | collective-permute-start | bytes 1376264 | tf_op jit(solution)/shard_map/ppermute | solution.py:22
  22.4 2.7 %collective-permute-start.4 = (bf16[64,3584]{1,0:T(8,128)(2,1)S(1)}, bf16[64,3584]{1,0:T(8,128)(2,1)S(1)}, u32[]{:S(2)}, u32[]{:S(2)}) collective-permute-start(bf16[64,3584]{1,0:T(8,128)(2,1)S(1)} %pad_maximum_fusion), channel_id=1, source_target_pairs={{0,24},{1,25},{2,26},{3,27},{4,28},{5,29},{6,30},{7,31},{8,0},{9,1... | collective-permute-start | bytes 1376264 | tf_op jit(solution)/shard_map/ppermute | solution.py:22
  26.1 3.5 %collective-permute-start.12 = (bf16[32,3584]{1,0:T(8,128)(2,1)S(1)}, bf16[32,3584]{1,0:T(8,128)(2,1)S(1)}, u32[]{:S(2)}, u32[]{:S(2)}) collective-permute-start(bf16[32,3584]{1,0:T(8,128)(2,1)S(1)} %slice.204), channel_id=1, source_target_pairs={{0,3},{1,0},{2,1},{3,2},{4,7},{5,4},{6,5},{7,6},{8,11},{9,8},{10,9... | collective-permute-start | bytes 688136 | tf_op jit(solution)/shard_map/ppermute | solution.py:22
  29.6 5.6 %collective-permute-done.4 = bf16[64,3584]{1,0:T(8,128)(2,1)S(1)} collective-permute-done((bf16[64,3584]{1,0:T(8,128)(2,1)S(1)}, bf16[64,3584]{1,0:T(8,128)(2,1)S(1)}, u32[]{:S(2)}, u32[]{:S(2)}) %collective-permute-start.4) | collective-permute-done | bytes 458784 | tf_op jit(solution)/shard_map/ppermute | solution.py:22
  35.3 3.5 %collective-permute-start.5 = (bf16[32,3584]{1,0:T(8,128)(2,1)S(1)}, bf16[32,3584]{1,0:T(8,128)(2,1)S(1)}, u32[]{:S(2)}, u32[]{:S(2)}) collective-permute-start(bf16[32,3584]{1,0:T(8,128)(2,1)S(1)} %slice.202), channel_id=1, source_target_pairs={{0,24},{1,25},{2,26},{3,27},{4,28},{5,29},{6,30},{7,31},{8,0},{9,1... | collective-permute-start | bytes 688136 | tf_op jit(solution)/shard_map/ppermute | solution.py:22
  39.1 4.1 %collective-permute-done.5 = bf16[32,3584]{1,0:T(8,128)(2,1)S(1)} collective-permute-done((bf16[32,3584]{1,0:T(8,128)(2,1)S(1)}, bf16[32,3584]{1,0:T(8,128)(2,1)S(1)}, u32[]{:S(2)}, u32[]{:S(2)}) %collective-permute-start.5) | collective-permute-done | bytes 229408 | tf_op jit(solution)/shard_map/ppermute | solution.py:22
  43.2 3.2 %collective-permute-done.7 = bf16[32,3584]{1,0:T(8,128)(2,1)S(1)} collective-permute-done((bf16[32,3584]{1,0:T(8,128)(2,1)S(1)}, bf16[32,3584]{1,0:T(8,128)(2,1)S(1)}, u32[]{:S(2)}, u32[]{:S(2)}) %collective-permute-start.7) | collective-permute-done | bytes 229408 | tf_op jit(solution)/shard_map/ppermute | solution.py:22
  46.4 1.6 fusion.15
  48.0 1.9 %collective-permute-start.15 = (bf16[256,768]{1,0:T(8,128)(2,1)S(1)}, bf16[256,768]{1,0:T(8,128)(2,1)S(1)}, u32[]{:S(2)}, u32[]{:S(2)}) collective-permute-start(bf16[256,768]{1,0:T(8,128)(2,1)S(1)} %fusion.15), channel_id=1, source_target_pairs={{0,32},{32,0},{64,96},{96,64},{1,33},{33,1},{65,97},{97,65},{2,34}... | collective-permute-start | bytes 1179656 | tf_op jit(solution)/shard_map/ppermute | solution.py:26
  50.0 1.6 fusion.7
  53.7 8.6 %collective-permute-done.16 = bf16[256,768]{1,0:T(8,128)(2,1)S(1)} collective-permute-done((bf16[256,768]{1,0:T(8,128)(2,1)S(1)}, bf16[256,768]{1,0:T(8,128)(2,1)S(1)}, u32[]{:S(2)}, u32[]{:S(2)}) %collective-permute-start.16) | collective-permute-done | bytes 393248 | tf_op jit(solution)/shard_map/ppermute | solution.py:26
  62.9 1.2 collective-permute-start.17
  64.2 1.3 collective-permute-done.17
  65.5 1.6 convolution_convert_fusion.2
  67.2 2.7 %collective-permute-start.20 = (bf16[64,3584]{1,0:T(8,128)(2,1)S(1)}, bf16[64,3584]{1,0:T(8,128)(2,1)S(1)}, u32[]{:S(2)}, u32[]{:S(2)}) collective-permute-start(bf16[64,3584]{1,0:T(8,128)(2,1)S(1)} %get-tuple-element.45), channel_id=1, source_target_pairs={{0,24},{1,25},{2,26},{3,27},{4,28},{5,29},{6,30},{7,31},{8,0},{9,1... | collective-permute-start | bytes 1376264 | tf_op jit(solution)/shard_map/ppermute | solution.py:22
  69.9 1.6 convolution_convert_fusion.1
  71.6 2.7 %collective-permute-start.35 = (bf16[64,3584]{1,0:T(8,128)(2,1)S(1)}, bf16[64,3584]{1,0:T(8,128)(2,1)S(1)}, u32[]{:S(2)}, u32[]{:S(2)}) collective-permute-start(bf16[64,3584]{1,0:T(8,128)(2,1)S(1)} %get-tuple-element.41), channel_id=1, source_target_pairs={{0,3},{1,0},{2,1},{3,2},{4,7},{5,4},{6,5},{7,6},{8,11},{9,8},{10,9... | collective-permute-start | bytes 1376264 | tf_op jit(solution)/shard_map/ppermute | solution.py:22
  74.5 1.5 collective-permute-done.18
  76.4 2.6 %collective-permute-start.21 = (bf16[32,3584]{1,0:T(8,128)(2,1)S(1)}, bf16[32,3584]{1,0:T(8,128)(2,1)S(1)}, u32[]{:S(2)}, u32[]{:S(2)}) collective-permute-start(bf16[32,3584]{1,0:T(8,128)(2,1)S(1)} %get-tuple-element.43), channel_id=1, source_target_pairs={{0,24},{1,25},{2,26},{3,27},{4,28},{5,29},{6,30},{7,31},{8,0},{9,1... | collective-permute-start | bytes 688136 | tf_op jit(solution)/shard_map/ppermute | solution.py:22
  79.0 2.8 %collective-permute-done.33 = bf16[64,3584]{1,0:T(8,128)(2,1)S(1)} collective-permute-done((bf16[64,3584]{1,0:T(8,128)(2,1)S(1)}, bf16[64,3584]{1,0:T(8,128)(2,1)S(1)}, u32[]{:S(2)}, u32[]{:S(2)}) %collective-permute-start.33) | collective-permute-done | bytes 458784 | tf_op jit(solution)/shard_map/ppermute | solution.py:22
  82.0 2.7 %collective-permute-start.36 = (bf16[32,3584]{1,0:T(8,128)(2,1)S(1)}, bf16[32,3584]{1,0:T(8,128)(2,1)S(1)}, u32[]{:S(2)}, u32[]{:S(2)}) collective-permute-start(bf16[32,3584]{1,0:T(8,128)(2,1)S(1)} %get-tuple-element.39), channel_id=1, source_target_pairs={{0,3},{1,0},{2,1},{3,2},{4,7},{5,4},{6,5},{7,6},{8,11},{9,8},{10,9... | collective-permute-start | bytes 688136 | tf_op jit(solution)/shard_map/ppermute | solution.py:22
  87.1 1.8 %collective-permute-start.24 = (bf16[16,3584]{1,0:T(8,128)(2,1)S(1)}, bf16[16,3584]{1,0:T(8,128)(2,1)S(1)}, u32[]{:S(2)}, u32[]{:S(2)}) collective-permute-start(bf16[16,3584]{1,0:T(8,128)(2,1)S(1)} %get-tuple-element.51), channel_id=1, source_target_pairs={{0,3},{1,0},{2,1},{3,2},{4,7},{5,4},{6,5},{7,6},{8,11},{9,8},{10,9... | collective-permute-start | bytes 344072 | tf_op jit(solution)/shard_map/ppermute | solution.py:22
  89.7 3.5 %collective-permute-start.38 = (bf16[16,3584]{1,0:T(8,128)(2,1)S(1)}, bf16[16,3584]{1,0:T(8,128)(2,1)S(1)}, u32[]{:S(2)}, u32[]{:S(2)}) collective-permute-start(bf16[16,3584]{1,0:T(8,128)(2,1)S(1)} %get-tuple-element.49), channel_id=1, source_target_pairs={{0,8},{1,9},{2,10},{3,11},{4,12},{5,13},{6,14},{7,15},{8,16},{9,17... | collective-permute-start | bytes 344072 | tf_op jit(solution)/shard_map/ppermute | solution.py:22
  94.0 3.0 %collective-permute-start.25 = (bf16[16,3584]{1,0:T(8,128)(2,1)S(1)}, bf16[16,3584]{1,0:T(8,128)(2,1)S(1)}, u32[]{:S(2)}, u32[]{:S(2)}) collective-permute-start(bf16[16,3584]{1,0:T(8,128)(2,1)S(1)} %fusion.32), channel_id=1, source_target_pairs={{0,4},{1,5},{2,6},{3,7},{4,0},{5,1},{6,2},{7,3},{8,12},{9,13},{10,... | collective-permute-start | bytes 344072 | tf_op jit(solution)/shard_map/ppermute | solution.py:22
  97.6 1.5 collective-permute-done.39
  99.2 3.0 %collective-permute-start.40 = (bf16[16,3584]{1,0:T(8,128)(2,1)S(1)}, bf16[16,3584]{1,0:T(8,128)(2,1)S(1)}, u32[]{:S(2)}, u32[]{:S(2)}) collective-permute-start(bf16[16,3584]{1,0:T(8,128)(2,1)S(1)} %fusion.33), channel_id=1, source_target_pairs={{0,4},{1,5},{2,6},{3,7},{4,0},{5,1},{6,2},{7,3},{8,12},{9,13},{10,... | collective-permute-start | bytes 344072 | tf_op jit(solution)/shard_map/ppermute | solution.py:22
  102.2 2.6 %collective-permute-done.40 = bf16[16,3584]{1,0:T(8,128)(2,1)S(1)} collective-permute-done((bf16[16,3584]{1,0:T(8,128)(2,1)S(1)}, bf16[16,3584]{1,0:T(8,128)(2,1)S(1)}, u32[]{:S(2)}, u32[]{:S(2)}) %collective-permute-start.40) | collective-permute-done | bytes 114720 | tf_op jit(solution)/shard_map/ppermute | solution.py:22
  105.1 1.9 %collective-permute-start.41 = (bf16[16,3584]{1,0:T(8,128)(2,1)S(1)}, bf16[16,3584]{1,0:T(8,128)(2,1)S(1)}, u32[]{:S(2)}, u32[]{:S(2)}) collective-permute-start(bf16[16,3584]{1,0:T(8,128)(2,1)S(1)} %get-tuple-element.30), channel_id=1, source_target_pairs={{0,24},{1,25},{2,26},{3,27},{4,28},{5,29},{6,30},{7,31},{8,0},{9,1... | collective-permute-start | bytes 344072 | tf_op jit(solution)/shard_map/ppermute | solution.py:22
  107.7 4.1 %collective-permute-start.26 = (bf16[16,3584]{1,0:T(8,128)(2,1)S(1)}, bf16[16,3584]{1,0:T(8,128)(2,1)S(1)}, u32[]{:S(2)}, u32[]{:S(2)}) collective-permute-start(bf16[16,3584]{1,0:T(8,128)(2,1)S(1)} %get-tuple-element.64), channel_id=1, source_target_pairs={{0,3},{1,0},{2,1},{3,2},{4,7},{5,4},{6,5},{7,6},{8,11},{9,8},{10,9... | collective-permute-start | bytes 344072 | tf_op jit(solution)/shard_map/ppermute | solution.py:22
  113.1 4.1 %collective-permute-start.44 = (bf16[64,3584]{1,0:T(8,128)(2,1)S(1)}, bf16[64,3584]{1,0:T(8,128)(2,1)S(1)}, u32[]{:S(2)}, u32[]{:S(2)}) collective-permute-start(bf16[64,3584]{1,0:T(8,128)(2,1)S(1)} %pad_maximum_fusion.3), channel_id=1, source_target_pairs={{0,3},{1,0},{2,1},{3,2},{4,7},{5,4},{6,5},{7,6},{8,11},{9,8},{10,9... | collective-permute-start | bytes 1376264 | tf_op jit(solution)/shard_map/ppermute | solution.py:22
  117.3 1.6 collective-permute-done.28
  118.9 1.4 collective-permute-start.29
  120.2 2.1 %collective-permute-start.31 = (bf16[64,3584]{1,0:T(8,128)(2,1)S(1)}, bf16[64,3584]{1,0:T(8,128)(2,1)S(1)}, u32[]{:S(2)}, u32[]{:S(2)}) collective-permute-start(bf16[64,3584]{1,0:T(8,128)(2,1)S(1)} %pad_maximum_fusion.2), channel_id=1, source_target_pairs={{0,8},{1,9},{2,10},{3,11},{4,12},{5,13},{6,14},{7,15},{8,16},{9,17... | collective-permute-start | bytes 1376264 | tf_op jit(solution)/shard_map/ppermute | solution.py:22
  122.7 3.5 %collective-permute-start.45 = (bf16[32,3584]{1,0:T(8,128)(2,1)S(1)}, bf16[32,3584]{1,0:T(8,128)(2,1)S(1)}, u32[]{:S(2)}, u32[]{:S(2)}) collective-permute-start(bf16[32,3584]{1,0:T(8,128)(2,1)S(1)} %slice.238), channel_id=1, source_target_pairs={{0,3},{1,0},{2,1},{3,2},{4,7},{5,4},{6,5},{7,6},{8,11},{9,8},{10,9... | collective-permute-start | bytes 688136 | tf_op jit(solution)/shard_map/ppermute | solution.py:22
  126.3 5.7 %collective-permute-done.29 = bf16[64,3584]{1,0:T(8,128)(2,1)S(1)} collective-permute-done((bf16[64,3584]{1,0:T(8,128)(2,1)S(1)}, bf16[64,3584]{1,0:T(8,128)(2,1)S(1)}, u32[]{:S(2)}, u32[]{:S(2)}) %collective-permute-start.29) | collective-permute-done | bytes 458784 | tf_op jit(solution)/shard_map/ppermute | solution.py:22
  132.2 1.5 collective-permute-start.32
  133.9 3.6 %collective-permute-done.30 = bf16[32,3584]{1,0:T(8,128)(2,1)S(1)} collective-permute-done((bf16[32,3584]{1,0:T(8,128)(2,1)S(1)}, bf16[32,3584]{1,0:T(8,128)(2,1)S(1)}, u32[]{:S(2)}, u32[]{:S(2)}) %collective-permute-start.30) | collective-permute-done | bytes 229408 | tf_op jit(solution)/shard_map/ppermute | solution.py:22
  138.4 1.6 convolution_convert_fusion.3
  140.0 7.5 %collective-permute-start.48 = (bf16[264,768]{1,0:T(8,128)(2,1)S(1)}, bf16[264,768]{1,0:T(8,128)(2,1)S(1)}, u32[]{:S(2)}, u32[]{:S(2)}) collective-permute-start(bf16[264,768]{1,0:T(8,128)(2,1)S(1)} %pad_maximum_fusion.4), channel_id=1, source_target_pairs={{0,32},{32,0},{64,96},{96,64},{1,33},{33,1},{65,97},{97,65},{2,34}... | collective-permute-start | bytes 1216520 | tf_op jit(solution)/shard_map/ppermute | solution.py:26
  147.5 1.6 fusion.50
  150.5 5.4 %fusion.3 = bf16[768,3584]{1,0:T(8,128)(2,1)} fusion(bf16[768,3584]{1,0:T(8,128)(2,1)S(1)} %bitcast.34, bf16[512,768]{1,0:T(8,128)(2,1)S(1)} %constant_dynamic-update-slice_fusion.32, f32[768]{0:T(1024)S(1)} %add_sqrt_fusion, f32[768]{0:T(1024)S(1)} %broadcast_multiply_fusion, bf16[256,3584]{1,0:T(8,128)(2,1)S(1)} %constant_dynamic-update-slice_fusion.24, ...), kind=kOutput, calls=%fused_computation.5 | convolution fusion | flops 2839674880 | bytes 15472640 | tf_op jit(solution)/shard_map/dot_general | solution.py:142
  155.9 4.5 %collective-permute-done.49 = bf16[264,768]{1,0:T(8,128)(2,1)S(1)} collective-permute-done((bf16[264,768]{1,0:T(8,128)(2,1)S(1)}, bf16[264,768]{1,0:T(8,128)(2,1)S(1)}, u32[]{:S(2)}, u32[]{:S(2)}) %collective-permute-start.49) | collective-permute-done | bytes 405536 | tf_op jit(solution)/shard_map/ppermute | solution.py:26
  161.8 1.3 collective-permute-done.50
  163.9 4.8 %fusion.4 = bf16[1,3584,768]{2,1,0:T(8,128)(2,1)} fusion(bf16[256,3584]{1,0:T(8,128)(2,1)S(1)} %constant_dynamic-update-slice_fusion.8, bf16[256,3584]{1,0:T(8,128)(2,1)S(1)} %constant_dynamic-update-slice_fusion, bf16[256,768]{1,0:T(8,128)(2,1)S(1)} %collective-permute-done.50, bf16[256,768]{1,0:T(8,128)(2,1)S(1)} %get-tuple-element.28), kind=kOutput, calls=%fused_computation.7 | convolution fusion | flops 2830237696 | bytes 9961472 | tf_op jit(solution)/shard_map/dot_general | solution.py:156
  (156 shorter events, 24.3 us)
Async XLA Ops:
  0.6 7.6 %collective-permute-start = (bf16[16,3584]{1,0:T(8,128)(2,1)}, bf16[16,3584]{1,0:T(8,128)(2,1)S(1)}, u32[]{:S(2)}, u32[]{:S(2)}) collective-permute-start(bf16[16,3584]{1,0:T(8,128)(2,1)} %bitcast.35), channel_id=1, source_target_pairs={{0,4},{1,5},{2,6},{3,7},{4,0},{5,1},{6,2},{7,3},{8,12},{9,13},{10,... | collective-permute-start | bytes 344072 | tf_op jit(solution)/shard_map/ppermute | solution.py:22
  8.9 7.6 %collective-permute-start.8 = (bf16[16,3584]{1,0:T(8,128)(2,1)S(1)}, bf16[16,3584]{1,0:T(8,128)(2,1)S(1)}, u32[]{:S(2)}, u32[]{:S(2)}) collective-permute-start(bf16[16,3584]{1,0:T(8,128)(2,1)S(1)} %get-tuple-element.36), channel_id=1, source_target_pairs={{0,24},{1,25},{2,26},{3,27},{4,28},{5,29},{6,30},{7,31},{8,0},{9,1... | collective-permute-start | bytes 344072 | tf_op jit(solution)/shard_map/ppermute | solution.py:22
  11.7 5.5 %collective-permute-start.9 = (bf16[16,3584]{1,0:T(8,128)(2,1)S(1)}, bf16[16,3584]{1,0:T(8,128)(2,1)S(1)}, u32[]{:S(2)}, u32[]{:S(2)}) collective-permute-start(bf16[16,3584]{1,0:T(8,128)(2,1)S(1)} %get-tuple-element.36), channel_id=1, source_target_pairs={{0,16},{1,17},{2,18},{3,19},{4,20},{5,21},{6,22},{7,23},{8,24},{9,... | collective-permute-start | bytes 344072 | tf_op jit(solution)/shard_map/ppermute | solution.py:22
  12.0 6.3 %collective-permute-start.10 = (bf16[16,3584]{1,0:T(8,128)(2,1)S(1)}, bf16[16,3584]{1,0:T(8,128)(2,1)S(1)}, u32[]{:S(2)}, u32[]{:S(2)}) collective-permute-start(bf16[16,3584]{1,0:T(8,128)(2,1)S(1)} %get-tuple-element.36), channel_id=1, source_target_pairs={{0,8},{1,9},{2,10},{3,11},{4,12},{5,13},{6,14},{7,15},{8,16},{9,17... | collective-permute-start | bytes 344072 | tf_op jit(solution)/shard_map/ppermute | solution.py:22
  13.5 7.1 %collective-permute-start.1 = (bf16[16,3584]{1,0:T(8,128)(2,1)S(1)}, bf16[16,3584]{1,0:T(8,128)(2,1)S(1)}, u32[]{:S(2)}, u32[]{:S(2)}) collective-permute-start(bf16[16,3584]{1,0:T(8,128)(2,1)S(1)} %get-tuple-element.54), channel_id=1, source_target_pairs={{0,3},{1,0},{2,1},{3,2},{4,7},{5,4},{6,5},{7,6},{8,11},{9,8},{10,9... | collective-permute-start | bytes 344072 | tf_op jit(solution)/shard_map/ppermute | solution.py:22
  16.0 5.3 %collective-permute-start.2 = (bf16[16,3584]{1,0:T(8,128)(2,1)S(1)}, bf16[16,3584]{1,0:T(8,128)(2,1)S(1)}, u32[]{:S(2)}, u32[]{:S(2)}) collective-permute-start(bf16[16,3584]{1,0:T(8,128)(2,1)S(1)} %get-tuple-element.54), channel_id=1, source_target_pairs={{0,2},{1,3},{2,0},{3,1},{4,6},{5,7},{6,4},{7,5},{8,10},{9,11},{10,... | collective-permute-start | bytes 344072 | tf_op jit(solution)/shard_map/ppermute | solution.py:22
  16.5 5.9 %collective-permute-start.3 = (bf16[16,3584]{1,0:T(8,128)(2,1)S(1)}, bf16[16,3584]{1,0:T(8,128)(2,1)S(1)}, u32[]{:S(2)}, u32[]{:S(2)}) collective-permute-start(bf16[16,3584]{1,0:T(8,128)(2,1)S(1)} %get-tuple-element.54), channel_id=1, source_target_pairs={{0,1},{1,2},{2,3},{3,0},{4,5},{5,6},{6,7},{7,4},{8,9},{9,10},{10,1... | collective-permute-start | bytes 344072 | tf_op jit(solution)/shard_map/ppermute | solution.py:22
  18.4 7.7 %collective-permute-start.11 = (bf16[64,3584]{1,0:T(8,128)(2,1)S(1)}, bf16[64,3584]{1,0:T(8,128)(2,1)S(1)}, u32[]{:S(2)}, u32[]{:S(2)}) collective-permute-start(bf16[64,3584]{1,0:T(8,128)(2,1)S(1)} %pad_maximum_fusion.1), channel_id=1, source_target_pairs={{0,3},{1,0},{2,1},{3,2},{4,7},{5,4},{6,5},{7,6},{8,11},{9,8},{10,9... | collective-permute-start | bytes 1376264 | tf_op jit(solution)/shard_map/ppermute | solution.py:22
  20.6 8.9 %collective-permute-start.13 = (bf16[64,3584]{1,0:T(8,128)(2,1)S(1)}, bf16[64,3584]{1,0:T(8,128)(2,1)S(1)}, u32[]{:S(2)}, u32[]{:S(2)}) collective-permute-start(bf16[64,3584]{1,0:T(8,128)(2,1)S(1)} %pad_maximum_fusion.1), channel_id=1, source_target_pairs={{0,1},{1,2},{2,3},{3,0},{4,5},{5,6},{6,7},{7,4},{8,9},{9,10},{10,1... | collective-permute-start | bytes 1376264 | tf_op jit(solution)/shard_map/ppermute | solution.py:22
  22.4 12.8 %collective-permute-start.4 = (bf16[64,3584]{1,0:T(8,128)(2,1)S(1)}, bf16[64,3584]{1,0:T(8,128)(2,1)S(1)}, u32[]{:S(2)}, u32[]{:S(2)}) collective-permute-start(bf16[64,3584]{1,0:T(8,128)(2,1)S(1)} %pad_maximum_fusion), channel_id=1, source_target_pairs={{0,24},{1,25},{2,26},{3,27},{4,28},{5,29},{6,30},{7,31},{8,0},{9,1... | collective-permute-start | bytes 1376264 | tf_op jit(solution)/shard_map/ppermute | solution.py:22
  25.1 13.7 %collective-permute-start.6 = (bf16[64,3584]{1,0:T(8,128)(2,1)S(1)}, bf16[64,3584]{1,0:T(8,128)(2,1)S(1)}, u32[]{:S(2)}, u32[]{:S(2)}) collective-permute-start(bf16[64,3584]{1,0:T(8,128)(2,1)S(1)} %pad_maximum_fusion), channel_id=1, source_target_pairs={{0,8},{1,9},{2,10},{3,11},{4,12},{5,13},{6,14},{7,15},{8,16},{9,17... | collective-permute-start | bytes 1376264 | tf_op jit(solution)/shard_map/ppermute | solution.py:22
  26.1 12.9 %collective-permute-start.12 = (bf16[32,3584]{1,0:T(8,128)(2,1)S(1)}, bf16[32,3584]{1,0:T(8,128)(2,1)S(1)}, u32[]{:S(2)}, u32[]{:S(2)}) collective-permute-start(bf16[32,3584]{1,0:T(8,128)(2,1)S(1)} %slice.204), channel_id=1, source_target_pairs={{0,3},{1,0},{2,1},{3,2},{4,7},{5,4},{6,5},{7,6},{8,11},{9,8},{10,9... | collective-permute-start | bytes 688136 | tf_op jit(solution)/shard_map/ppermute | solution.py:22
  29.6 9.4 %collective-permute-start.14 = (bf16[32,3584]{1,0:T(8,128)(2,1)S(1)}, bf16[32,3584]{1,0:T(8,128)(2,1)S(1)}, u32[]{:S(2)}, u32[]{:S(2)}) collective-permute-start(bf16[32,3584]{1,0:T(8,128)(2,1)S(1)} %slice.205), channel_id=1, source_target_pairs={{0,1},{1,2},{2,3},{3,0},{4,5},{5,6},{6,7},{7,4},{8,9},{9,10},{10,1... | collective-permute-start | bytes 688136 | tf_op jit(solution)/shard_map/ppermute | solution.py:22
  35.3 7.9 %collective-permute-start.5 = (bf16[32,3584]{1,0:T(8,128)(2,1)S(1)}, bf16[32,3584]{1,0:T(8,128)(2,1)S(1)}, u32[]{:S(2)}, u32[]{:S(2)}) collective-permute-start(bf16[32,3584]{1,0:T(8,128)(2,1)S(1)} %slice.202), channel_id=1, source_target_pairs={{0,24},{1,25},{2,26},{3,27},{4,28},{5,29},{6,30},{7,31},{8,0},{9,1... | collective-permute-start | bytes 688136 | tf_op jit(solution)/shard_map/ppermute | solution.py:22
  38.8 7.5 %collective-permute-start.7 = (bf16[32,3584]{1,0:T(8,128)(2,1)S(1)}, bf16[32,3584]{1,0:T(8,128)(2,1)S(1)}, u32[]{:S(2)}, u32[]{:S(2)}) collective-permute-start(bf16[32,3584]{1,0:T(8,128)(2,1)S(1)} %slice.203), channel_id=1, source_target_pairs={{0,8},{1,9},{2,10},{3,11},{4,12},{5,13},{6,14},{7,15},{8,16},{9,17... | collective-permute-start | bytes 688136 | tf_op jit(solution)/shard_map/ppermute | solution.py:22
  51.7 10.7 %collective-permute-start.16 = (bf16[256,768]{1,0:T(8,128)(2,1)S(1)}, bf16[256,768]{1,0:T(8,128)(2,1)S(1)}, u32[]{:S(2)}, u32[]{:S(2)}) collective-permute-start(bf16[256,768]{1,0:T(8,128)(2,1)S(1)} %get-tuple-element.33), channel_id=1, source_target_pairs={{0,64},{32,96},{64,0},{96,32},{1,65},{33,97},{65,1},{97,33},{2,66}... | collective-permute-start | bytes 1179656 | tf_op jit(solution)/shard_map/ppermute | solution.py:26
  67.1 8.9 %collective-permute-start.18 = (bf16[64,3584]{1,0:T(8,128)(2,1)S(1)}, bf16[64,3584]{1,0:T(8,128)(2,1)S(1)}, u32[]{:S(2)}, u32[]{:S(2)}) collective-permute-start(bf16[64,3584]{1,0:T(8,128)(2,1)S(1)} %get-tuple-element.46), channel_id=1, source_target_pairs={{0,8},{1,9},{2,10},{3,11},{4,12},{5,13},{6,14},{7,15},{8,16},{9,17... | collective-permute-start | bytes 1376264 | tf_op jit(solution)/shard_map/ppermute | solution.py:22
  67.2 8.8 %collective-permute-start.20 = (bf16[64,3584]{1,0:T(8,128)(2,1)S(1)}, bf16[64,3584]{1,0:T(8,128)(2,1)S(1)}, u32[]{:S(2)}, u32[]{:S(2)}) collective-permute-start(bf16[64,3584]{1,0:T(8,128)(2,1)S(1)} %get-tuple-element.45), channel_id=1, source_target_pairs={{0,24},{1,25},{2,26},{3,27},{4,28},{5,29},{6,30},{7,31},{8,0},{9,1... | collective-permute-start | bytes 1376264 | tf_op jit(solution)/shard_map/ppermute | solution.py:22
  71.6 10.2 %collective-permute-start.33 = (bf16[64,3584]{1,0:T(8,128)(2,1)S(1)}, bf16[64,3584]{1,0:T(8,128)(2,1)S(1)}, u32[]{:S(2)}, u32[]{:S(2)}) collective-permute-start(bf16[64,3584]{1,0:T(8,128)(2,1)S(1)} %get-tuple-element.42), channel_id=1, source_target_pairs={{0,1},{1,2},{2,3},{3,0},{4,5},{5,6},{6,7},{7,4},{8,9},{9,10},{10,1... | collective-permute-start | bytes 1376264 | tf_op jit(solution)/shard_map/ppermute | solution.py:22
  71.6 10.2 %collective-permute-start.35 = (bf16[64,3584]{1,0:T(8,128)(2,1)S(1)}, bf16[64,3584]{1,0:T(8,128)(2,1)S(1)}, u32[]{:S(2)}, u32[]{:S(2)}) collective-permute-start(bf16[64,3584]{1,0:T(8,128)(2,1)S(1)} %get-tuple-element.41), channel_id=1, source_target_pairs={{0,3},{1,0},{2,1},{3,2},{4,7},{5,4},{6,5},{7,6},{8,11},{9,8},{10,9... | collective-permute-start | bytes 1376264 | tf_op jit(solution)/shard_map/ppermute | solution.py:22
  76.2 8.6 %collective-permute-start.19 = (bf16[32,3584]{1,0:T(8,128)(2,1)S(1)}, bf16[32,3584]{1,0:T(8,128)(2,1)S(1)}, u32[]{:S(2)}, u32[]{:S(2)}) collective-permute-start(bf16[32,3584]{1,0:T(8,128)(2,1)S(1)} %get-tuple-element.44), channel_id=1, source_target_pairs={{0,8},{1,9},{2,10},{3,11},{4,12},{5,13},{6,14},{7,15},{8,16},{9,17... | collective-permute-start | bytes 688136 | tf_op jit(solution)/shard_map/ppermute | solution.py:22
  76.4 8.5 %collective-permute-start.21 = (bf16[32,3584]{1,0:T(8,128)(2,1)S(1)}, bf16[32,3584]{1,0:T(8,128)(2,1)S(1)}, u32[]{:S(2)}, u32[]{:S(2)}) collective-permute-start(bf16[32,3584]{1,0:T(8,128)(2,1)S(1)} %get-tuple-element.43), channel_id=1, source_target_pairs={{0,24},{1,25},{2,26},{3,27},{4,28},{5,29},{6,30},{7,31},{8,0},{9,1... | collective-permute-start | bytes 688136 | tf_op jit(solution)/shard_map/ppermute | solution.py:22
  81.9 7.0 %collective-permute-start.34 = (bf16[32,3584]{1,0:T(8,128)(2,1)S(1)}, bf16[32,3584]{1,0:T(8,128)(2,1)S(1)}, u32[]{:S(2)}, u32[]{:S(2)}) collective-permute-start(bf16[32,3584]{1,0:T(8,128)(2,1)S(1)} %get-tuple-element.40), channel_id=1, source_target_pairs={{0,1},{1,2},{2,3},{3,0},{4,5},{5,6},{6,7},{7,4},{8,9},{9,10},{10,1... | collective-permute-start | bytes 688136 | tf_op jit(solution)/shard_map/ppermute | solution.py:22
  82.0 7.2 %collective-permute-start.36 = (bf16[32,3584]{1,0:T(8,128)(2,1)S(1)}, bf16[32,3584]{1,0:T(8,128)(2,1)S(1)}, u32[]{:S(2)}, u32[]{:S(2)}) collective-permute-start(bf16[32,3584]{1,0:T(8,128)(2,1)S(1)} %get-tuple-element.39), channel_id=1, source_target_pairs={{0,3},{1,0},{2,1},{3,2},{4,7},{5,4},{6,5},{7,6},{8,11},{9,8},{10,9... | collective-permute-start | bytes 688136 | tf_op jit(solution)/shard_map/ppermute | solution.py:22
  85.1 8.1 %collective-permute-start.22 = (bf16[16,3584]{1,0:T(8,128)(2,1)S(1)}, bf16[16,3584]{1,0:T(8,128)(2,1)S(1)}, u32[]{:S(2)}, u32[]{:S(2)}) collective-permute-start(bf16[16,3584]{1,0:T(8,128)(2,1)S(1)} %get-tuple-element.50), channel_id=1, source_target_pairs={{0,2},{1,3},{2,0},{3,1},{4,6},{5,7},{6,4},{7,5},{8,10},{9,11},{10,... | collective-permute-start | bytes 344072 | tf_op jit(solution)/shard_map/ppermute | solution.py:22
  86.2 7.7 %collective-permute-start.23 = (bf16[16,3584]{1,0:T(8,128)(2,1)S(1)}, bf16[16,3584]{1,0:T(8,128)(2,1)S(1)}, u32[]{:S(2)}, u32[]{:S(2)}) collective-permute-start(bf16[16,3584]{1,0:T(8,128)(2,1)S(1)} %get-tuple-element.52), channel_id=1, source_target_pairs={{0,1},{1,2},{2,3},{3,0},{4,5},{5,6},{6,7},{7,4},{8,9},{9,10},{10,1... | collective-permute-start | bytes 344072 | tf_op jit(solution)/shard_map/ppermute | solution.py:22
  87.1 6.9 %collective-permute-start.24 = (bf16[16,3584]{1,0:T(8,128)(2,1)S(1)}, bf16[16,3584]{1,0:T(8,128)(2,1)S(1)}, u32[]{:S(2)}, u32[]{:S(2)}) collective-permute-start(bf16[16,3584]{1,0:T(8,128)(2,1)S(1)} %get-tuple-element.51), channel_id=1, source_target_pairs={{0,3},{1,0},{2,1},{3,2},{4,7},{5,4},{6,5},{7,6},{8,11},{9,8},{10,9... | collective-permute-start | bytes 344072 | tf_op jit(solution)/shard_map/ppermute | solution.py:22
  89.4 7.7 %collective-permute-start.37 = (bf16[16,3584]{1,0:T(8,128)(2,1)S(1)}, bf16[16,3584]{1,0:T(8,128)(2,1)S(1)}, u32[]{:S(2)}, u32[]{:S(2)}) collective-permute-start(bf16[16,3584]{1,0:T(8,128)(2,1)S(1)} %get-tuple-element.47), channel_id=1, source_target_pairs={{0,16},{1,17},{2,18},{3,19},{4,20},{5,21},{6,22},{7,23},{8,24},{9,... | collective-permute-start | bytes 344072 | tf_op jit(solution)/shard_map/ppermute | solution.py:22
  89.7 7.9 %collective-permute-start.38 = (bf16[16,3584]{1,0:T(8,128)(2,1)S(1)}, bf16[16,3584]{1,0:T(8,128)(2,1)S(1)}, u32[]{:S(2)}, u32[]{:S(2)}) collective-permute-start(bf16[16,3584]{1,0:T(8,128)(2,1)S(1)} %get-tuple-element.49), channel_id=1, source_target_pairs={{0,8},{1,9},{2,10},{3,11},{4,12},{5,13},{6,14},{7,15},{8,16},{9,17... | collective-permute-start | bytes 344072 | tf_op jit(solution)/shard_map/ppermute | solution.py:22
  93.2 5.9 %collective-permute-start.39 = (bf16[16,3584]{1,0:T(8,128)(2,1)S(1)}, bf16[16,3584]{1,0:T(8,128)(2,1)S(1)}, u32[]{:S(2)}, u32[]{:S(2)}) collective-permute-start(bf16[16,3584]{1,0:T(8,128)(2,1)S(1)} %get-tuple-element.48), channel_id=1, source_target_pairs={{0,24},{1,25},{2,26},{3,27},{4,28},{5,29},{6,30},{7,31},{8,0},{9,1... | collective-permute-start | bytes 344072 | tf_op jit(solution)/shard_map/ppermute | solution.py:22
  94.0 8.2 %collective-permute-start.25 = (bf16[16,3584]{1,0:T(8,128)(2,1)S(1)}, bf16[16,3584]{1,0:T(8,128)(2,1)S(1)}, u32[]{:S(2)}, u32[]{:S(2)}) collective-permute-start(bf16[16,3584]{1,0:T(8,128)(2,1)S(1)} %fusion.32), channel_id=1, source_target_pairs={{0,4},{1,5},{2,6},{3,7},{4,0},{5,1},{6,2},{7,3},{8,12},{9,13},{10,... | collective-permute-start | bytes 344072 | tf_op jit(solution)/shard_map/ppermute | solution.py:22
  99.2 5.7 %collective-permute-start.40 = (bf16[16,3584]{1,0:T(8,128)(2,1)S(1)}, bf16[16,3584]{1,0:T(8,128)(2,1)S(1)}, u32[]{:S(2)}, u32[]{:S(2)}) collective-permute-start(bf16[16,3584]{1,0:T(8,128)(2,1)S(1)} %fusion.33), channel_id=1, source_target_pairs={{0,4},{1,5},{2,6},{3,7},{4,0},{5,1},{6,2},{7,3},{8,12},{9,13},{10,... | collective-permute-start | bytes 344072 | tf_op jit(solution)/shard_map/ppermute | solution.py:22
  105.1 6.7 %collective-permute-start.41 = (bf16[16,3584]{1,0:T(8,128)(2,1)S(1)}, bf16[16,3584]{1,0:T(8,128)(2,1)S(1)}, u32[]{:S(2)}, u32[]{:S(2)}) collective-permute-start(bf16[16,3584]{1,0:T(8,128)(2,1)S(1)} %get-tuple-element.30), channel_id=1, source_target_pairs={{0,24},{1,25},{2,26},{3,27},{4,28},{5,29},{6,30},{7,31},{8,0},{9,1... | collective-permute-start | bytes 344072 | tf_op jit(solution)/shard_map/ppermute | solution.py:22
  107.0 5.3 %collective-permute-start.42 = (bf16[16,3584]{1,0:T(8,128)(2,1)S(1)}, bf16[16,3584]{1,0:T(8,128)(2,1)S(1)}, u32[]{:S(2)}, u32[]{:S(2)}) collective-permute-start(bf16[16,3584]{1,0:T(8,128)(2,1)S(1)} %get-tuple-element.30), channel_id=1, source_target_pairs={{0,16},{1,17},{2,18},{3,19},{4,20},{5,21},{6,22},{7,23},{8,24},{9,... | collective-permute-start | bytes 344072 | tf_op jit(solution)/shard_map/ppermute | solution.py:22
  107.0 6.1 %collective-permute-start.43 = (bf16[16,3584]{1,0:T(8,128)(2,1)S(1)}, bf16[16,3584]{1,0:T(8,128)(2,1)S(1)}, u32[]{:S(2)}, u32[]{:S(2)}) collective-permute-start(bf16[16,3584]{1,0:T(8,128)(2,1)S(1)} %get-tuple-element.30), channel_id=1, source_target_pairs={{0,8},{1,9},{2,10},{3,11},{4,12},{5,13},{6,14},{7,15},{8,16},{9,17... | collective-permute-start | bytes 344072 | tf_op jit(solution)/shard_map/ppermute | solution.py:22
  107.7 9.6 %collective-permute-start.26 = (bf16[16,3584]{1,0:T(8,128)(2,1)S(1)}, bf16[16,3584]{1,0:T(8,128)(2,1)S(1)}, u32[]{:S(2)}, u32[]{:S(2)}) collective-permute-start(bf16[16,3584]{1,0:T(8,128)(2,1)S(1)} %get-tuple-element.64), channel_id=1, source_target_pairs={{0,3},{1,0},{2,1},{3,2},{4,7},{5,4},{6,5},{7,6},{8,11},{9,8},{10,9... | collective-permute-start | bytes 344072 | tf_op jit(solution)/shard_map/ppermute | solution.py:22
  111.8 5.5 %collective-permute-start.27 = (bf16[16,3584]{1,0:T(8,128)(2,1)S(1)}, bf16[16,3584]{1,0:T(8,128)(2,1)S(1)}, u32[]{:S(2)}, u32[]{:S(2)}) collective-permute-start(bf16[16,3584]{1,0:T(8,128)(2,1)S(1)} %get-tuple-element.64), channel_id=1, source_target_pairs={{0,2},{1,3},{2,0},{3,1},{4,6},{5,7},{6,4},{7,5},{8,10},{9,11},{10,... | collective-permute-start | bytes 344072 | tf_op jit(solution)/shard_map/ppermute | solution.py:22
  111.8 7.1 %collective-permute-start.28 = (bf16[16,3584]{1,0:T(8,128)(2,1)S(1)}, bf16[16,3584]{1,0:T(8,128)(2,1)S(1)}, u32[]{:S(2)}, u32[]{:S(2)}) collective-permute-start(bf16[16,3584]{1,0:T(8,128)(2,1)S(1)} %get-tuple-element.64), channel_id=1, source_target_pairs={{0,1},{1,2},{2,3},{3,0},{4,5},{5,6},{6,7},{7,4},{8,9},{9,10},{10,1... | collective-permute-start | bytes 344072 | tf_op jit(solution)/shard_map/ppermute | solution.py:22
  113.1 9.6 %collective-permute-start.44 = (bf16[64,3584]{1,0:T(8,128)(2,1)S(1)}, bf16[64,3584]{1,0:T(8,128)(2,1)S(1)}, u32[]{:S(2)}, u32[]{:S(2)}) collective-permute-start(bf16[64,3584]{1,0:T(8,128)(2,1)S(1)} %pad_maximum_fusion.3), channel_id=1, source_target_pairs={{0,3},{1,0},{2,1},{3,2},{4,7},{5,4},{6,5},{7,6},{8,11},{9,8},{10,9... | collective-permute-start | bytes 1376264 | tf_op jit(solution)/shard_map/ppermute | solution.py:22
  117.3 8.9 %collective-permute-start.46 = (bf16[64,3584]{1,0:T(8,128)(2,1)S(1)}, bf16[64,3584]{1,0:T(8,128)(2,1)S(1)}, u32[]{:S(2)}, u32[]{:S(2)}) collective-permute-start(bf16[64,3584]{1,0:T(8,128)(2,1)S(1)} %pad_maximum_fusion.3), channel_id=1, source_target_pairs={{0,1},{1,2},{2,3},{3,0},{4,5},{5,6},{6,7},{7,4},{8,9},{9,10},{10,1... | collective-permute-start | bytes 1376264 | tf_op jit(solution)/shard_map/ppermute | solution.py:22
  118.9 13.1 %collective-permute-start.29 = (bf16[64,3584]{1,0:T(8,128)(2,1)S(1)}, bf16[64,3584]{1,0:T(8,128)(2,1)S(1)}, u32[]{:S(2)}, u32[]{:S(2)}) collective-permute-start(bf16[64,3584]{1,0:T(8,128)(2,1)S(1)} %pad_maximum_fusion.2), channel_id=1, source_target_pairs={{0,24},{1,25},{2,26},{3,27},{4,28},{5,29},{6,30},{7,31},{8,0},{9,1... | collective-permute-start | bytes 1376264 | tf_op jit(solution)/shard_map/ppermute | solution.py:22
  120.2 11.9 %collective-permute-start.31 = (bf16[64,3584]{1,0:T(8,128)(2,1)S(1)}, bf16[64,3584]{1,0:T(8,128)(2,1)S(1)}, u32[]{:S(2)}, u32[]{:S(2)}) collective-permute-start(bf16[64,3584]{1,0:T(8,128)(2,1)S(1)} %pad_maximum_fusion.2), channel_id=1, source_target_pairs={{0,8},{1,9},{2,10},{3,11},{4,12},{5,13},{6,14},{7,15},{8,16},{9,17... | collective-permute-start | bytes 1376264 | tf_op jit(solution)/shard_map/ppermute | solution.py:22
  122.7 11.0 %collective-permute-start.45 = (bf16[32,3584]{1,0:T(8,128)(2,1)S(1)}, bf16[32,3584]{1,0:T(8,128)(2,1)S(1)}, u32[]{:S(2)}, u32[]{:S(2)}) collective-permute-start(bf16[32,3584]{1,0:T(8,128)(2,1)S(1)} %slice.238), channel_id=1, source_target_pairs={{0,3},{1,0},{2,1},{3,2},{4,7},{5,4},{6,5},{7,6},{8,11},{9,8},{10,9... | collective-permute-start | bytes 688136 | tf_op jit(solution)/shard_map/ppermute | solution.py:22
  126.2 7.6 %collective-permute-start.47 = (bf16[32,3584]{1,0:T(8,128)(2,1)S(1)}, bf16[32,3584]{1,0:T(8,128)(2,1)S(1)}, u32[]{:S(2)}, u32[]{:S(2)}) collective-permute-start(bf16[32,3584]{1,0:T(8,128)(2,1)S(1)} %slice.239), channel_id=1, source_target_pairs={{0,1},{1,2},{2,3},{3,0},{4,5},{5,6},{6,7},{7,4},{8,9},{9,10},{10,1... | collective-permute-start | bytes 688136 | tf_op jit(solution)/shard_map/ppermute | solution.py:22
  132.0 5.4 %collective-permute-start.30 = (bf16[32,3584]{1,0:T(8,128)(2,1)S(1)}, bf16[32,3584]{1,0:T(8,128)(2,1)S(1)}, u32[]{:S(2)}, u32[]{:S(2)}) collective-permute-start(bf16[32,3584]{1,0:T(8,128)(2,1)S(1)} %slice.221), channel_id=1, source_target_pairs={{0,24},{1,25},{2,26},{3,27},{4,28},{5,29},{6,30},{7,31},{8,0},{9,1... | collective-permute-start | bytes 688136 | tf_op jit(solution)/shard_map/ppermute | solution.py:22
  132.2 6.2 %collective-permute-start.32 = (bf16[32,3584]{1,0:T(8,128)(2,1)S(1)}, bf16[32,3584]{1,0:T(8,128)(2,1)S(1)}, u32[]{:S(2)}, u32[]{:S(2)}) collective-permute-start(bf16[32,3584]{1,0:T(8,128)(2,1)S(1)} %slice.222), channel_id=1, source_target_pairs={{0,8},{1,9},{2,10},{3,11},{4,12},{5,13},{6,14},{7,15},{8,16},{9,17... | collective-permute-start | bytes 688136 | tf_op jit(solution)/shard_map/ppermute | solution.py:22
  140.0 9.1 %collective-permute-start.48 = (bf16[264,768]{1,0:T(8,128)(2,1)S(1)}, bf16[264,768]{1,0:T(8,128)(2,1)S(1)}, u32[]{:S(2)}, u32[]{:S(2)}) collective-permute-start(bf16[264,768]{1,0:T(8,128)(2,1)S(1)} %pad_maximum_fusion.4), channel_id=1, source_target_pairs={{0,32},{32,0},{64,96},{96,64},{1,33},{33,1},{65,97},{97,65},{2,34}... | collective-permute-start | bytes 1216520 | tf_op jit(solution)/shard_map/ppermute | solution.py:26
  149.4 11.0 %collective-permute-start.49 = (bf16[264,768]{1,0:T(8,128)(2,1)S(1)}, bf16[264,768]{1,0:T(8,128)(2,1)S(1)}, u32[]{:S(2)}, u32[]{:S(2)}) collective-permute-start(bf16[264,768]{1,0:T(8,128)(2,1)S(1)} %pad_maximum_fusion.5), channel_id=1, source_target_pairs={{0,64},{32,96},{64,0},{96,32},{1,65},{33,97},{65,1},{97,33},{2,66}... | collective-permute-start | bytes 1216520 | tf_op jit(solution)/shard_map/ppermute | solution.py:26
  (8 other events, 48.2 us)

commit v5 on v4

--- a/solution.py
+++ b/solution.py
@@ -54,16 +54,16 @@
     return join(rows, after, far, before)
 
 
-def ring_scatter(rows, slot, stage):
-    n = rows.shape[0] // 4
+def ring_scatter(first, second, slot, stage):
+    n = first.shape[0] // 2
     half = n // 2
-    up = shift(rows[n + half : 2 * n + half], slot, stage, 1)
-    down = shift(rows[2 * n + half : 3 * n + half], slot, stage, -1)
-    up_far = narrow(wide(rows[n : n + half]) + wide(up[half:]))
-    down_far = narrow(wide(rows[3 * n + half :]) + wide(down[:half]))
+    up = shift(first[:n], slot, stage, 1)
+    down = shift(first[n:], slot, stage, -1)
+    up_far = narrow(wide(second[n : n + half]) + wide(up[half:]))
+    down_far = narrow(wide(second[n + half :]) + wide(down[:half]))
     up_far, down_far = shift(up_far, slot, stage, 1), shift(down_far, slot, stage, -1)
     return (
-        wide(rows[:n])
+        wide(second[:n])
         + join(wide(up_far), wide(up[:half]))
         + join(wide(down[half:]), wide(down_far))
     )
@@ -81,8 +81,8 @@
     return ring_gather(near_gather(pair, slot, 0), slot, 1)
 
 
-def scatter_sum(rows, slot):
-    pair = rounded(near_scatter(narrow(ring_scatter(rows, slot, 1)), slot, 0))
+def scatter_sum(first, second, slot):
+    pair = rounded(near_scatter(narrow(ring_scatter(first, second, slot, 1)), slot, 0))
     other = wide(shift(narrow(pair), slot, "zh", 1))
     half = pair.shape[0] // 2
     return pair + join(other[half:], other[:half])
@@ -102,22 +102,34 @@
     low, high = join(own_rows[:8], other_rows[:8]), join(own_rows[8:], other_rows[8:])
     pairs = [jnp.where(upper, high, low), jnp.where(upper, low, high)]
     gathered = [gather_rows(pairs[slot], slot) for slot in (0, 1)]
-    gathered = list(lax.optimization_barrier(tuple(gathered)))
     pre = [jnp.dot(rows, enc_local, preferred_element_type=jnp.float32) for rows in gathered]
     part = core_sum(*pre)
-    other = layer_swap(narrow(part), 2)
+    first, second = part[96:224], join(part[:96], part[224:])
+    other = [layer_swap(narrow(rows), 2) for rows in (first, second)]
     part, dec_local = lax.optimization_barrier((part, dec_local))
     row_norms = jnp.sqrt(jnp.sum(jnp.square(wide(dec_local)), axis=1) + 1e-06)
-    other, row_norms = lax.optimization_barrier((other, row_norms))
-    pre = part + wide(other) + enc_bias[None, :]
-    kept = narrow(jax.nn.softplus(sharpness * pre) / sharpness)
-    gate = jax.nn.sigmoid(sharpness * pre)
-    latents = [kept, layer_swap(kept, 1)]
-    latents = list(lax.optimization_barrier(tuple(latents)))
+    other[0], row_norms = lax.optimization_barrier((other[0], row_norms))
+    dec_copy = dec_local
+    gates, latents, products = [], [], []
+    for rows in (first, second):
+        got = other[len(gates)]
+        pre = rows + wide(got) + enc_bias[None, :]
+        gates.append(jax.nn.sigmoid(sharpness * pre))
+        kept = narrow(jax.nn.softplus(sharpness * pre) / sharpness)
+        latents.append((kept, layer_swap(kept, 1)))
+        products.append(
+            [
+                narrow(jnp.dot(rows, dec_copy, preferred_element_type=jnp.float32))
+                for rows in latents[-1]
+            ]
+        )
+        if len(gates) == 1:
+            other[1], products[0] = lax.optimization_barrier((other[1], products[0]))
+    gate = join(gates[1][:96], gates[0], gates[1][96:])
+    latents = [join(b[:96], a, b[96:]) for a, b in zip(*latents)]
     errors = []
     for slot in (0, 1):
-        rebuilt = jnp.dot(latents[slot], dec_local, preferred_element_type=jnp.float32)
-        rebuilt = scatter_sum(narrow(rebuilt), slot)
+        rebuilt = scatter_sum(products[0][slot], products[1][slot], slot)
         misfit = rebuilt + dec_bias[0][None, :] - wide(pairs[slot])
         errors.append(narrow(2.0 * misfit))
     errors = [gather_rows(errors[slot], slot) for slot in (0, 1)]

time: 169 us -> 166 us (0.982)
  waiting for transfers between devices: 56.6 us -> 48.8 us
  starting transfers between devices: 83.2 us -> 88.3 us
    ppermute x6 -> x8, waiting for transfers between devices: 15.8 us -> 9.59 us  [layer_swap(): return lax.ppermute(value, 'layer', [(i, i ^ bit) for i in range(4)])]
    ppermute x45, starting transfers between devices: 69.6 us -> 73.5 us  [shift(): return lax.ppermute(value, ('layer', 'latent'), pairs)]
    ppermute x6 -> x8, starting transfers between devices: 13.5 us -> 14.8 us  [layer_swap(): return lax.ppermute(value, 'layer', [(i, i ^ bit) for i in range(4)])]
    dot_general x2 -> x4, matrix products: 3.17 us -> 3.58 us  [per_device(): jnp.dot(rows, dec_copy, preferred_element_type=jnp.float32)]
  transfers between devices with their start and end apart: 51 -> 53, of which waited for: 24 -> 27; matrix products, arithmetic and copies ran while one was open for 9% -> 11% of each run, Pallas kernels for 0% -> 0%
where the time goes in v5:
time: 166 us
  starting transfers between devices  88.3 us (53%)
  waiting for transfers between devices  48.8 us (29%)
  matrix products  20.2 us (12%)
  other arithmetic  5.23 us (3%)
  local copies, waits for them, and re-layouts  2.19 us (1%)
    ppermute x45, starting transfers between devices, shift(): return lax.ppermute(value, ('layer', 'latent'), pairs)  73.5 us
    ppermute x45, waiting for transfers between devices, shift(): return lax.ppermute(value, ('layer', 'latent'), pairs)  39.2 us
    ppermute x8, starting transfers between devices, layer_swap(): return lax.ppermute(value, 'layer', [(i, i ^ bit) for i in range(4)])  14.8 us
    ppermute x8, waiting for transfers between devices, layer_swap(): return lax.ppermute(value, 'layer', [(i, i ^ bit) for i in range(4)])  9.59 us
    dot_general x1, matrix products, per_device(): lax.dot_general(join(*latents), join(*errors), (((0,), (0,)), ((), ())),...  5.42 us
    dot_general x1, matrix products, per_device(): lax.dot_general(join(*gathered), join(*pre_grads), (((0,), (0,)), ((), ()...  4.84 us
    dot_general x4, matrix products, per_device(): jnp.dot(rows, dec_copy, preferred_element_type=jnp.float32)  3.58 us
  transfers between devices with their start and end apart: 53, of which 27 were waited for; matrix products, arithmetic and copies ran while one was open for 11% of the time, Pallas kernels for 0%

profile of v5, /device:TPU:1, one launch (start us, length us, event | category | flops | bytes accessed | tf_op | source)
XLA Modules:
  0.0 166.1 jit_solution(15180633427073814292)
XLA Ops:
  0.6 4.5 %collective-permute-start = (bf16[16,3584]{1,0:T(8,128)(2,1)}, bf16[16,3584]{1,0:T(8,128)(2,1)S(1)}, u32[]{:S(2)}, u32[]{:S(2)}) collective-permute-start(bf16[16,3584]{1,0:T(8,128)(2,1)} %bitcast.42), channel_id=1, source_target_pairs={{0,4},{1,5},{2,6},{3,7},{4,0},{5,1},{6,2},{7,3},{8,12},{9,13},{10,... | collective-permute-start | bytes 344072 | tf_op jit(solution)/shard_map/ppermute | solution.py:22
  6.8 1.4 collective-permute-done
  8.3 2.5 %collective-permute-start.1 = (bf16[16,3584]{1,0:T(8,128)(2,1)S(1)}, bf16[16,3584]{1,0:T(8,128)(2,1)S(1)}, u32[]{:S(2)}, u32[]{:S(2)}) collective-permute-start(bf16[16,3584]{1,0:T(8,128)(2,1)S(1)} %get-tuple-element.68), channel_id=1, source_target_pairs={{0,3},{1,0},{2,1},{3,2},{4,7},{5,4},{6,5},{7,6},{8,11},{9,8},{10,9... | collective-permute-start | bytes 344072 | tf_op jit(solution)/shard_map/ppermute | solution.py:22
  12.0 2.8 %collective-permute-start.8 = (bf16[16,3584]{1,0:T(8,128)(2,1)S(1)}, bf16[16,3584]{1,0:T(8,128)(2,1)S(1)}, u32[]{:S(2)}, u32[]{:S(2)}) collective-permute-start(bf16[16,3584]{1,0:T(8,128)(2,1)S(1)} %get-tuple-element.30), channel_id=1, source_target_pairs={{0,24},{1,25},{2,26},{3,27},{4,28},{5,29},{6,30},{7,31},{8,0},{9,1... | collective-permute-start | bytes 344072 | tf_op jit(solution)/shard_map/ppermute | solution.py:22
  16.1 1.4 collective-permute-done.3
  17.6 2.5 %collective-permute-start.4 = (bf16[64,3584]{1,0:T(8,128)(2,1)S(1)}, bf16[64,3584]{1,0:T(8,128)(2,1)S(1)}, u32[]{:S(2)}, u32[]{:S(2)}) collective-permute-start(bf16[64,3584]{1,0:T(8,128)(2,1)S(1)} %pad_maximum_fusion), channel_id=1, source_target_pairs={{0,24},{1,25},{2,26},{3,27},{4,28},{5,29},{6,30},{7,31},{8,0},{9,1... | collective-permute-start | bytes 1376264 | tf_op jit(solution)/shard_map/ppermute | solution.py:22
  20.7 1.5 collective-permute-done.10
  22.2 2.4 %collective-permute-start.11 = (bf16[64,3584]{1,0:T(8,128)(2,1)S(1)}, bf16[64,3584]{1,0:T(8,128)(2,1)S(1)}, u32[]{:S(2)}, u32[]{:S(2)}) collective-permute-start(bf16[64,3584]{1,0:T(8,128)(2,1)S(1)} %pad_maximum_fusion.1), channel_id=1, source_target_pairs={{0,3},{1,0},{2,1},{3,2},{4,7},{5,4},{6,5},{7,6},{8,11},{9,8},{10,9... | collective-permute-start | bytes 1376264 | tf_op jit(solution)/shard_map/ppermute | solution.py:22
  25.5 3.5 %collective-permute-start.5 = (bf16[32,3584]{1,0:T(8,128)(2,1)S(1)}, bf16[32,3584]{1,0:T(8,128)(2,1)S(1)}, u32[]{:S(2)}, u32[]{:S(2)}) collective-permute-start(bf16[32,3584]{1,0:T(8,128)(2,1)S(1)} %slice.238), channel_id=1, source_target_pairs={{0,24},{1,25},{2,26},{3,27},{4,28},{5,29},{6,30},{7,31},{8,0},{9,1... | collective-permute-start | bytes 688136 | tf_op jit(solution)/shard_map/ppermute | solution.py:22
  29.1 5.5 %collective-permute-done.11 = bf16[64,3584]{1,0:T(8,128)(2,1)S(1)} collective-permute-done((bf16[64,3584]{1,0:T(8,128)(2,1)S(1)}, bf16[64,3584]{1,0:T(8,128)(2,1)S(1)}, u32[]{:S(2)}, u32[]{:S(2)}) %collective-permute-start.11) | collective-permute-done | bytes 458784 | tf_op jit(solution)/shard_map/ppermute | solution.py:22
  34.6 3.0 %collective-permute-start.12 = (bf16[32,3584]{1,0:T(8,128)(2,1)S(1)}, bf16[32,3584]{1,0:T(8,128)(2,1)S(1)}, u32[]{:S(2)}, u32[]{:S(2)}) collective-permute-start(bf16[32,3584]{1,0:T(8,128)(2,1)S(1)} %slice.240), channel_id=1, source_target_pairs={{0,3},{1,0},{2,1},{3,2},{4,7},{5,4},{6,5},{7,6},{8,11},{9,8},{10,9... | collective-permute-start | bytes 688136 | tf_op jit(solution)/shard_map/ppermute | solution.py:22
  38.2 3.0 %collective-permute-done.12 = bf16[32,3584]{1,0:T(8,128)(2,1)S(1)} collective-permute-done((bf16[32,3584]{1,0:T(8,128)(2,1)S(1)}, bf16[32,3584]{1,0:T(8,128)(2,1)S(1)}, u32[]{:S(2)}, u32[]{:S(2)}) %collective-permute-start.12) | collective-permute-done | bytes 229408 | tf_op jit(solution)/shard_map/ppermute | solution.py:22
  41.3 3.2 %collective-permute-done.14 = bf16[32,3584]{1,0:T(8,128)(2,1)S(1)} collective-permute-done((bf16[32,3584]{1,0:T(8,128)(2,1)S(1)}, bf16[32,3584]{1,0:T(8,128)(2,1)S(1)}, u32[]{:S(2)}, u32[]{:S(2)}) %collective-permute-start.14) | collective-permute-done | bytes 229408 | tf_op jit(solution)/shard_map/ppermute | solution.py:22
  44.6 1.6 fusion.12
  46.2 2.8 %collective-permute-start.15 = (bf16[256,768]{1,0:T(8,128)(2,1)S(1)}, bf16[256,768]{1,0:T(8,128)(2,1)S(1)}, u32[]{:S(2)}, u32[]{:S(2)}) collective-permute-start(bf16[256,768]{1,0:T(8,128)(2,1)S(1)} %fusion.12), channel_id=1, source_target_pairs={{0,32},{32,0},{64,96},{96,64},{1,33},{33,1},{65,97},{97,65},{2,34}... | collective-permute-start | bytes 1179656 | tf_op jit(solution)/shard_map/ppermute | solution.py:26
  49.1 1.6 fusion.7
  50.9 1.2 collective-permute-start.17
  54.0 3.3 %collective-permute-done.17 = bf16[128,768]{1,0:T(8,128)(2,1)S(1)} collective-permute-done((bf16[128,768]{1,0:T(8,128)(2,1)S(1)}, bf16[128,768]{1,0:T(8,128)(2,1)S(1)}, u32[]{:S(2)}, u32[]{:S(2)}) %collective-permute-start.17) | collective-permute-done | bytes 196640 | tf_op jit(solution)/shard_map/ppermute | solution.py:26
  57.7 1.8 %collective-permute-start.18 = (bf16[128,768]{1,0:T(8,128)(2,1)S(1)}, bf16[128,768]{1,0:T(8,128)(2,1)S(1)}, u32[]{:S(2)}, u32[]{:S(2)}) collective-permute-start(bf16[128,768]{1,0:T(8,128)(2,1)S(1)} %get-tuple-element.34), channel_id=1, source_target_pairs={{0,32},{32,0},{64,96},{96,64},{1,33},{33,1},{65,97},{97,65},{2,34}... | collective-permute-start | bytes 589832 | tf_op jit(solution)/shard_map/ppermute | solution.py:26
  64.0 2.7 %collective-permute-start.21 = (bf16[64,3584]{1,0:T(8,128)(2,1)S(1)}, bf16[64,3584]{1,0:T(8,128)(2,1)S(1)}, u32[]{:S(2)}, u32[]{:S(2)}) collective-permute-start(bf16[64,3584]{1,0:T(8,128)(2,1)S(1)} %get-tuple-element.41), channel_id=1, source_target_pairs={{0,24},{1,25},{2,26},{3,27},{4,28},{5,29},{6,30},{7,31},{8,0},{9,1... | collective-permute-start | bytes 1376264 | tf_op jit(solution)/shard_map/ppermute | solution.py:22
  66.8 2.7 %collective-permute-start.37 = (bf16[64,3584]{1,0:T(8,128)(2,1)S(1)}, bf16[64,3584]{1,0:T(8,128)(2,1)S(1)}, u32[]{:S(2)}, u32[]{:S(2)}) collective-permute-start(bf16[64,3584]{1,0:T(8,128)(2,1)S(1)} %get-tuple-element.37), channel_id=1, source_target_pairs={{0,3},{1,0},{2,1},{3,2},{4,7},{5,4},{6,5},{7,6},{8,11},{9,8},{10,9... | collective-permute-start | bytes 1376264 | tf_op jit(solution)/shard_map/ppermute | solution.py:22
  70.6 3.2 %collective-permute-done.19 = bf16[64,3584]{1,0:T(8,128)(2,1)S(1)} collective-permute-done((bf16[64,3584]{1,0:T(8,128)(2,1)S(1)}, bf16[64,3584]{1,0:T(8,128)(2,1)S(1)}, u32[]{:S(2)}, u32[]{:S(2)}) %collective-permute-start.19) | collective-permute-done | bytes 458784 | tf_op jit(solution)/shard_map/ppermute | solution.py:22
  74.1 2.7 %collective-permute-start.22 = (bf16[32,3584]{1,0:T(8,128)(2,1)S(1)}, bf16[32,3584]{1,0:T(8,128)(2,1)S(1)}, u32[]{:S(2)}, u32[]{:S(2)}) collective-permute-start(bf16[32,3584]{1,0:T(8,128)(2,1)S(1)} %get-tuple-element.39), channel_id=1, source_target_pairs={{0,24},{1,25},{2,26},{3,27},{4,28},{5,29},{6,30},{7,31},{8,0},{9,1... | collective-permute-start | bytes 688136 | tf_op jit(solution)/shard_map/ppermute | solution.py:22
  76.7 1.2 collective-permute-done.35
  78.7 2.5 %collective-permute-start.38 = (bf16[32,3584]{1,0:T(8,128)(2,1)S(1)}, bf16[32,3584]{1,0:T(8,128)(2,1)S(1)}, u32[]{:S(2)}, u32[]{:S(2)}) collective-permute-start(bf16[32,3584]{1,0:T(8,128)(2,1)S(1)} %get-tuple-element.35), channel_id=1, source_target_pairs={{0,3},{1,0},{2,1},{3,2},{4,7},{5,4},{6,5},{7,6},{8,11},{9,8},{10,9... | collective-permute-start | bytes 688136 | tf_op jit(solution)/shard_map/ppermute | solution.py:22
  81.5 1.2 collective-permute-start.23
  82.7 1.9 %collective-permute-start.24 = (bf16[16,3584]{1,0:T(8,128)(2,1)S(1)}, bf16[16,3584]{1,0:T(8,128)(2,1)S(1)}, u32[]{:S(2)}, u32[]{:S(2)}) collective-permute-start(bf16[16,3584]{1,0:T(8,128)(2,1)S(1)} %get-tuple-element.50), channel_id=1, source_target_pairs={{0,1},{1,2},{2,3},{3,0},{4,5},{5,6},{6,7},{7,4},{8,9},{9,10},{10,1... | collective-permute-start | bytes 344072 | tf_op jit(solution)/shard_map/ppermute | solution.py:22
  87.0 1.6 collective-permute-start.39
  88.7 2.7 %collective-permute-start.41 = (bf16[16,3584]{1,0:T(8,128)(2,1)S(1)}, bf16[16,3584]{1,0:T(8,128)(2,1)S(1)}, u32[]{:S(2)}, u32[]{:S(2)}) collective-permute-start(bf16[16,3584]{1,0:T(8,128)(2,1)S(1)} %get-tuple-element.46), channel_id=1, source_target_pairs={{0,24},{1,25},{2,26},{3,27},{4,28},{5,29},{6,30},{7,31},{8,0},{9,1... | collective-permute-start | bytes 344072 | tf_op jit(solution)/shard_map/ppermute | solution.py:22
  91.4 2.8 %collective-permute-start.26 = (bf16[16,3584]{1,0:T(8,128)(2,1)S(1)}, bf16[16,3584]{1,0:T(8,128)(2,1)S(1)}, u32[]{:S(2)}, u32[]{:S(2)}) collective-permute-start(bf16[16,3584]{1,0:T(8,128)(2,1)S(1)} %fusion.33), channel_id=1, source_target_pairs={{0,4},{1,5},{2,6},{3,7},{4,0},{5,1},{6,2},{7,3},{8,12},{9,13},{10,... | collective-permute-start | bytes 344072 | tf_op jit(solution)/shard_map/ppermute | solution.py:22
  95.3 2.7 %collective-permute-start.42 = (bf16[16,3584]{1,0:T(8,128)(2,1)S(1)}, bf16[16,3584]{1,0:T(8,128)(2,1)S(1)}, u32[]{:S(2)}, u32[]{:S(2)}) collective-permute-start(bf16[16,3584]{1,0:T(8,128)(2,1)S(1)} %fusion.34), channel_id=1, source_target_pairs={{0,4},{1,5},{2,6},{3,7},{4,0},{5,1},{6,2},{7,3},{8,12},{9,13},{10,... | collective-permute-start | bytes 344072 | tf_op jit(solution)/shard_map/ppermute | solution.py:22
  98.0 2.5 %collective-permute-done.42 = bf16[16,3584]{1,0:T(8,128)(2,1)S(1)} collective-permute-done((bf16[16,3584]{1,0:T(8,128)(2,1)S(1)}, bf16[16,3584]{1,0:T(8,128)(2,1)S(1)}, u32[]{:S(2)}, u32[]{:S(2)}) %collective-permute-start.42) | collective-permute-done | bytes 114720 | tf_op jit(solution)/shard_map/ppermute | solution.py:22
  101.8 2.7 %collective-permute-start.44 = (bf16[16,3584]{1,0:T(8,128)(2,1)S(1)}, bf16[16,3584]{1,0:T(8,128)(2,1)S(1)}, u32[]{:S(2)}, u32[]{:S(2)}) collective-permute-start(bf16[16,3584]{1,0:T(8,128)(2,1)S(1)} %get-tuple-element.26), channel_id=1, source_target_pairs={{0,16},{1,17},{2,18},{3,19},{4,20},{5,21},{6,22},{7,23},{8,24},{9,... | collective-permute-start | bytes 344072 | tf_op jit(solution)/shard_map/ppermute | solution.py:22
  104.5 4.2 %collective-permute-start.27 = (bf16[16,3584]{1,0:T(8,128)(2,1)S(1)}, bf16[16,3584]{1,0:T(8,128)(2,1)S(1)}, u32[]{:S(2)}, u32[]{:S(2)}) collective-permute-start(bf16[16,3584]{1,0:T(8,128)(2,1)S(1)} %get-tuple-element.90), channel_id=1, source_target_pairs={{0,3},{1,0},{2,1},{3,2},{4,7},{5,4},{6,5},{7,6},{8,11},{9,8},{10,9... | collective-permute-start | bytes 344072 | tf_op jit(solution)/shard_map/ppermute | solution.py:22
  109.4 4.2 %collective-permute-start.46 = (bf16[64,3584]{1,0:T(8,128)(2,1)S(1)}, bf16[64,3584]{1,0:T(8,128)(2,1)S(1)}, u32[]{:S(2)}, u32[]{:S(2)}) collective-permute-start(bf16[64,3584]{1,0:T(8,128)(2,1)S(1)} %pad_maximum_fusion.3), channel_id=1, source_target_pairs={{0,3},{1,0},{2,1},{3,2},{4,7},{5,4},{6,5},{7,6},{8,11},{9,8},{10,9... | collective-permute-start | bytes 1376264 | tf_op jit(solution)/shard_map/ppermute | solution.py:22
  114.8 5.0 %collective-permute-start.30 = (bf16[64,3584]{1,0:T(8,128)(2,1)S(1)}, bf16[64,3584]{1,0:T(8,128)(2,1)S(1)}, u32[]{:S(2)}, u32[]{:S(2)}) collective-permute-start(bf16[64,3584]{1,0:T(8,128)(2,1)S(1)} %pad_maximum_fusion.2), channel_id=1, source_target_pairs={{0,24},{1,25},{2,26},{3,27},{4,28},{5,29},{6,30},{7,31},{8,0},{9,1... | collective-permute-start | bytes 1376264 | tf_op jit(solution)/shard_map/ppermute | solution.py:22
  120.5 3.5 %collective-permute-start.47 = (bf16[32,3584]{1,0:T(8,128)(2,1)S(1)}, bf16[32,3584]{1,0:T(8,128)(2,1)S(1)}, u32[]{:S(2)}, u32[]{:S(2)}) collective-permute-start(bf16[32,3584]{1,0:T(8,128)(2,1)S(1)} %slice.273), channel_id=1, source_target_pairs={{0,3},{1,0},{2,1},{3,2},{4,7},{5,4},{6,5},{7,6},{8,11},{9,8},{10,9... | collective-permute-start | bytes 688136 | tf_op jit(solution)/shard_map/ppermute | solution.py:22
  124.0 4.3 %collective-permute-done.30 = bf16[64,3584]{1,0:T(8,128)(2,1)S(1)} collective-permute-done((bf16[64,3584]{1,0:T(8,128)(2,1)S(1)}, bf16[64,3584]{1,0:T(8,128)(2,1)S(1)}, u32[]{:S(2)}, u32[]{:S(2)}) %collective-permute-start.30) | collective-permute-done | bytes 458784 | tf_op jit(solution)/shard_map/ppermute | solution.py:22
  128.4 3.5 %collective-permute-start.31 = (bf16[32,3584]{1,0:T(8,128)(2,1)S(1)}, bf16[32,3584]{1,0:T(8,128)(2,1)S(1)}, u32[]{:S(2)}, u32[]{:S(2)}) collective-permute-start(bf16[32,3584]{1,0:T(8,128)(2,1)S(1)} %slice.258), channel_id=1, source_target_pairs={{0,24},{1,25},{2,26},{3,27},{4,28},{5,29},{6,30},{7,31},{8,0},{9,1... | collective-permute-start | bytes 688136 | tf_op jit(solution)/shard_map/ppermute | solution.py:22
  132.2 2.7 %collective-permute-done.31 = bf16[32,3584]{1,0:T(8,128)(2,1)S(1)} collective-permute-done((bf16[32,3584]{1,0:T(8,128)(2,1)S(1)}, bf16[32,3584]{1,0:T(8,128)(2,1)S(1)}, u32[]{:S(2)}, u32[]{:S(2)}) %collective-permute-start.31) | collective-permute-done | bytes 229408 | tf_op jit(solution)/shard_map/ppermute | solution.py:22
  134.9 3.2 %collective-permute-done.33 = bf16[32,3584]{1,0:T(8,128)(2,1)S(1)} collective-permute-done((bf16[32,3584]{1,0:T(8,128)(2,1)S(1)}, bf16[32,3584]{1,0:T(8,128)(2,1)S(1)}, u32[]{:S(2)}, u32[]{:S(2)}) %collective-permute-start.33) | collective-permute-done | bytes 229408 | tf_op jit(solution)/shard_map/ppermute | solution.py:22
  138.1 1.6 convolution_convert_fusion.5
  139.8 5.4 %collective-permute-start.50 = (bf16[264,768]{1,0:T(8,128)(2,1)S(1)}, bf16[264,768]{1,0:T(8,128)(2,1)S(1)}, u32[]{:S(2)}, u32[]{:S(2)}) collective-permute-start(bf16[264,768]{1,0:T(8,128)(2,1)S(1)} %pad_maximum_fusion.4), channel_id=1, source_target_pairs={{0,32},{32,0},{64,96},{96,64},{1,33},{33,1},{65,97},{97,65},{2,34}... | collective-permute-start | bytes 1216520 | tf_op jit(solution)/shard_map/ppermute | solution.py:26
  145.1 1.6 fusion.51
  147.8 5.4 %fusion.3 = bf16[768,3584]{1,0:T(8,128)(2,1)} fusion(bf16[768,3584]{1,0:T(8,128)(2,1)S(1)} %bitcast.41, bf16[512,768]{1,0:T(8,128)(2,1)S(1)} %constant_dynamic-update-slice_fusion.48, f32[768]{0:T(1024)S(1)} %add_sqrt_fusion, f32[768]{0:T(1024)S(1)} %broadcast_multiply_fusion, bf16[256,3584]{1,0:T(8,128)(2,1)S(1)} %constant_dynamic-update-slice_fusion.40, ...), kind=kOutput, calls=%fused_computation.5 | convolution fusion | flops 2839674880 | bytes 15472640 | tf_op jit(solution)/shard_map/dot_general | solution.py:154
  153.3 4.8 %collective-permute-done.51 = bf16[264,768]{1,0:T(8,128)(2,1)S(1)} collective-permute-done((bf16[264,768]{1,0:T(8,128)(2,1)S(1)}, bf16[264,768]{1,0:T(8,128)(2,1)S(1)}, u32[]{:S(2)}, u32[]{:S(2)}) %collective-permute-start.51) | collective-permute-done | bytes 405536 | tf_op jit(solution)/shard_map/ppermute | solution.py:26
  159.3 1.3 collective-permute-done.52
  161.3 4.8 %fusion.4 = bf16[1,3584,768]{2,1,0:T(8,128)(2,1)} fusion(bf16[512,3584]{1,0:T(8,128)(2,1)S(1)} %get-tuple-element.52, bf16[256,768]{1,0:T(8,128)(2,1)S(1)} %collective-permute-done.52, bf16[256,768]{1,0:T(8,128)(2,1)S(1)} %get-tuple-element.24), kind=kOutput, calls=%fused_computation.7 | convolution fusion | flops 2822897664 | bytes 9961472 | tf_op jit(solution)/shard_map/dot_general | solution.py:168
  (176 shorter events, 26.7 us)
Async XLA Ops:
  0.6 7.6 %collective-permute-start = (bf16[16,3584]{1,0:T(8,128)(2,1)}, bf16[16,3584]{1,0:T(8,128)(2,1)S(1)}, u32[]{:S(2)}, u32[]{:S(2)}) collective-permute-start(bf16[16,3584]{1,0:T(8,128)(2,1)} %bitcast.42), channel_id=1, source_target_pairs={{0,4},{1,5},{2,6},{3,7},{4,0},{5,1},{6,2},{7,3},{8,12},{9,13},{10,... | collective-permute-start | bytes 344072 | tf_op jit(solution)/shard_map/ppermute | solution.py:22
  8.3 6.8 %collective-permute-start.1 = (bf16[16,3584]{1,0:T(8,128)(2,1)S(1)}, bf16[16,3584]{1,0:T(8,128)(2,1)S(1)}, u32[]{:S(2)}, u32[]{:S(2)}) collective-permute-start(bf16[16,3584]{1,0:T(8,128)(2,1)S(1)} %get-tuple-element.68), channel_id=1, source_target_pairs={{0,3},{1,0},{2,1},{3,2},{4,7},{5,4},{6,5},{7,6},{8,11},{9,8},{10,9... | collective-permute-start | bytes 344072 | tf_op jit(solution)/shard_map/ppermute | solution.py:22
  10.8 5.3 %collective-permute-start.2 = (bf16[16,3584]{1,0:T(8,128)(2,1)S(1)}, bf16[16,3584]{1,0:T(8,128)(2,1)S(1)}, u32[]{:S(2)}, u32[]{:S(2)}) collective-permute-start(bf16[16,3584]{1,0:T(8,128)(2,1)S(1)} %get-tuple-element.68), channel_id=1, source_target_pairs={{0,2},{1,3},{2,0},{3,1},{4,6},{5,7},{6,4},{7,5},{8,10},{9,11},{10,... | collective-permute-start | bytes 344072 | tf_op jit(solution)/shard_map/ppermute | solution.py:22
  11.4 6.2 %collective-permute-start.3 = (bf16[16,3584]{1,0:T(8,128)(2,1)S(1)}, bf16[16,3584]{1,0:T(8,128)(2,1)S(1)}, u32[]{:S(2)}, u32[]{:S(2)}) collective-permute-start(bf16[16,3584]{1,0:T(8,128)(2,1)S(1)} %get-tuple-element.68), channel_id=1, source_target_pairs={{0,1},{1,2},{2,3},{3,0},{4,5},{5,6},{6,7},{7,4},{8,9},{9,10},{10,1... | collective-permute-start | bytes 344072 | tf_op jit(solution)/shard_map/ppermute | solution.py:22
  12.0 8.1 %collective-permute-start.8 = (bf16[16,3584]{1,0:T(8,128)(2,1)S(1)}, bf16[16,3584]{1,0:T(8,128)(2,1)S(1)}, u32[]{:S(2)}, u32[]{:S(2)}) collective-permute-start(bf16[16,3584]{1,0:T(8,128)(2,1)S(1)} %get-tuple-element.30), channel_id=1, source_target_pairs={{0,24},{1,25},{2,26},{3,27},{4,28},{5,29},{6,30},{7,31},{8,0},{9,1... | collective-permute-start | bytes 344072 | tf_op jit(solution)/shard_map/ppermute | solution.py:22
  14.8 5.9 %collective-permute-start.9 = (bf16[16,3584]{1,0:T(8,128)(2,1)S(1)}, bf16[16,3584]{1,0:T(8,128)(2,1)S(1)}, u32[]{:S(2)}, u32[]{:S(2)}) collective-permute-start(bf16[16,3584]{1,0:T(8,128)(2,1)S(1)} %get-tuple-element.30), channel_id=1, source_target_pairs={{0,16},{1,17},{2,18},{3,19},{4,20},{5,21},{6,22},{7,23},{8,24},{9,... | collective-permute-start | bytes 344072 | tf_op jit(solution)/shard_map/ppermute | solution.py:22
  15.1 7.1 %collective-permute-start.10 = (bf16[16,3584]{1,0:T(8,128)(2,1)S(1)}, bf16[16,3584]{1,0:T(8,128)(2,1)S(1)}, u32[]{:S(2)}, u32[]{:S(2)}) collective-permute-start(bf16[16,3584]{1,0:T(8,128)(2,1)S(1)} %get-tuple-element.30), channel_id=1, source_target_pairs={{0,8},{1,9},{2,10},{3,11},{4,12},{5,13},{6,14},{7,15},{8,16},{9,17... | collective-permute-start | bytes 344072 | tf_op jit(solution)/shard_map/ppermute | solution.py:22
  17.6 7.9 %collective-permute-start.4 = (bf16[64,3584]{1,0:T(8,128)(2,1)S(1)}, bf16[64,3584]{1,0:T(8,128)(2,1)S(1)}, u32[]{:S(2)}, u32[]{:S(2)}) collective-permute-start(bf16[64,3584]{1,0:T(8,128)(2,1)S(1)} %pad_maximum_fusion), channel_id=1, source_target_pairs={{0,24},{1,25},{2,26},{3,27},{4,28},{5,29},{6,30},{7,31},{8,0},{9,1... | collective-permute-start | bytes 1376264 | tf_op jit(solution)/shard_map/ppermute | solution.py:22
  20.1 8.9 %collective-permute-start.6 = (bf16[64,3584]{1,0:T(8,128)(2,1)S(1)}, bf16[64,3584]{1,0:T(8,128)(2,1)S(1)}, u32[]{:S(2)}, u32[]{:S(2)}) collective-permute-start(bf16[64,3584]{1,0:T(8,128)(2,1)S(1)} %pad_maximum_fusion), channel_id=1, source_target_pairs={{0,8},{1,9},{2,10},{3,11},{4,12},{5,13},{6,14},{7,15},{8,16},{9,17... | collective-permute-start | bytes 1376264 | tf_op jit(solution)/shard_map/ppermute | solution.py:22
  22.2 12.4 %collective-permute-start.11 = (bf16[64,3584]{1,0:T(8,128)(2,1)S(1)}, bf16[64,3584]{1,0:T(8,128)(2,1)S(1)}, u32[]{:S(2)}, u32[]{:S(2)}) collective-permute-start(bf16[64,3584]{1,0:T(8,128)(2,1)S(1)} %pad_maximum_fusion.1), channel_id=1, source_target_pairs={{0,3},{1,0},{2,1},{3,2},{4,7},{5,4},{6,5},{7,6},{8,11},{9,8},{10,9... | collective-permute-start | bytes 1376264 | tf_op jit(solution)/shard_map/ppermute | solution.py:22
  24.6 13.0 %collective-permute-start.13 = (bf16[64,3584]{1,0:T(8,128)(2,1)S(1)}, bf16[64,3584]{1,0:T(8,128)(2,1)S(1)}, u32[]{:S(2)}, u32[]{:S(2)}) collective-permute-start(bf16[64,3584]{1,0:T(8,128)(2,1)S(1)} %pad_maximum_fusion.1), channel_id=1, source_target_pairs={{0,1},{1,2},{2,3},{3,0},{4,5},{5,6},{6,7},{7,4},{8,9},{9,10},{10,1... | collective-permute-start | bytes 1376264 | tf_op jit(solution)/shard_map/ppermute | solution.py:22
  25.5 12.3 %collective-permute-start.5 = (bf16[32,3584]{1,0:T(8,128)(2,1)S(1)}, bf16[32,3584]{1,0:T(8,128)(2,1)S(1)}, u32[]{:S(2)}, u32[]{:S(2)}) collective-permute-start(bf16[32,3584]{1,0:T(8,128)(2,1)S(1)} %slice.238), channel_id=1, source_target_pairs={{0,24},{1,25},{2,26},{3,27},{4,28},{5,29},{6,30},{7,31},{8,0},{9,1... | collective-permute-start | bytes 688136 | tf_op jit(solution)/shard_map/ppermute | solution.py:22
  29.0 9.0 %collective-permute-start.7 = (bf16[32,3584]{1,0:T(8,128)(2,1)S(1)}, bf16[32,3584]{1,0:T(8,128)(2,1)S(1)}, u32[]{:S(2)}, u32[]{:S(2)}) collective-permute-start(bf16[32,3584]{1,0:T(8,128)(2,1)S(1)} %slice.239), channel_id=1, source_target_pairs={{0,8},{1,9},{2,10},{3,11},{4,12},{5,13},{6,14},{7,15},{8,16},{9,17... | collective-permute-start | bytes 688136 | tf_op jit(solution)/shard_map/ppermute | solution.py:22
  34.6 6.7 %collective-permute-start.12 = (bf16[32,3584]{1,0:T(8,128)(2,1)S(1)}, bf16[32,3584]{1,0:T(8,128)(2,1)S(1)}, u32[]{:S(2)}, u32[]{:S(2)}) collective-permute-start(bf16[32,3584]{1,0:T(8,128)(2,1)S(1)} %slice.240), channel_id=1, source_target_pairs={{0,3},{1,0},{2,1},{3,2},{4,7},{5,4},{6,5},{7,6},{8,11},{9,8},{10,9... | collective-permute-start | bytes 688136 | tf_op jit(solution)/shard_map/ppermute | solution.py:22
  37.6 6.9 %collective-permute-start.14 = (bf16[32,3584]{1,0:T(8,128)(2,1)S(1)}, bf16[32,3584]{1,0:T(8,128)(2,1)S(1)}, u32[]{:S(2)}, u32[]{:S(2)}) collective-permute-start(bf16[32,3584]{1,0:T(8,128)(2,1)S(1)} %slice.241), channel_id=1, source_target_pairs={{0,1},{1,2},{2,3},{3,0},{4,5},{5,6},{6,7},{7,4},{8,9},{9,10},{10,1... | collective-permute-start | bytes 688136 | tf_op jit(solution)/shard_map/ppermute | solution.py:22
  50.9 6.4 %collective-permute-start.17 = (bf16[128,768]{1,0:T(8,128)(2,1)S(1)}, bf16[128,768]{1,0:T(8,128)(2,1)S(1)}, u32[]{:S(2)}, u32[]{:S(2)}) collective-permute-start(bf16[128,768]{1,0:T(8,128)(2,1)S(1)} %slice.329), channel_id=1, source_target_pairs={{0,64},{32,96},{64,0},{96,32},{1,65},{33,97},{65,1},{97,33},{2,66}... | collective-permute-start | bytes 589832 | tf_op jit(solution)/shard_map/ppermute | solution.py:26
  53.2 8.3 %collective-permute-start.16 = (bf16[128,768]{1,0:T(8,128)(2,1)S(1)}, bf16[128,768]{1,0:T(8,128)(2,1)S(1)}, u32[]{:S(2)}, u32[]{:S(2)}) collective-permute-start(bf16[128,768]{1,0:T(8,128)(2,1)S(1)} %fusion.24), channel_id=1, source_target_pairs={{0,64},{32,96},{64,0},{96,32},{1,65},{33,97},{65,1},{97,33},{2,66}... | collective-permute-start | bytes 589832 | tf_op jit(solution)/shard_map/ppermute | solution.py:26
  61.9 7.6 %collective-permute-start.34 = (bf16[128,768]{1,0:T(8,128)(2,1)S(1)}, bf16[128,768]{1,0:T(8,128)(2,1)S(1)}, u32[]{:S(2)}, u32[]{:S(2)}) collective-permute-start(bf16[128,768]{1,0:T(8,128)(2,1)S(1)} %get-tuple-element.43), channel_id=1, source_target_pairs={{0,32},{32,0},{64,96},{96,64},{1,33},{33,1},{65,97},{97,65},{2,34}... | collective-permute-start | bytes 589832 | tf_op jit(solution)/shard_map/ppermute | solution.py:26
  64.0 9.9 %collective-permute-start.19 = (bf16[64,3584]{1,0:T(8,128)(2,1)S(1)}, bf16[64,3584]{1,0:T(8,128)(2,1)S(1)}, u32[]{:S(2)}, u32[]{:S(2)}) collective-permute-start(bf16[64,3584]{1,0:T(8,128)(2,1)S(1)} %get-tuple-element.42), channel_id=1, source_target_pairs={{0,8},{1,9},{2,10},{3,11},{4,12},{5,13},{6,14},{7,15},{8,16},{9,17... | collective-permute-start | bytes 1376264 | tf_op jit(solution)/shard_map/ppermute | solution.py:22
  64.0 9.8 %collective-permute-start.21 = (bf16[64,3584]{1,0:T(8,128)(2,1)S(1)}, bf16[64,3584]{1,0:T(8,128)(2,1)S(1)}, u32[]{:S(2)}, u32[]{:S(2)}) collective-permute-start(bf16[64,3584]{1,0:T(8,128)(2,1)S(1)} %get-tuple-element.41), channel_id=1, source_target_pairs={{0,24},{1,25},{2,26},{3,27},{4,28},{5,29},{6,30},{7,31},{8,0},{9,1... | collective-permute-start | bytes 1376264 | tf_op jit(solution)/shard_map/ppermute | solution.py:22
  66.8 11.2 %collective-permute-start.35 = (bf16[64,3584]{1,0:T(8,128)(2,1)S(1)}, bf16[64,3584]{1,0:T(8,128)(2,1)S(1)}, u32[]{:S(2)}, u32[]{:S(2)}) collective-permute-start(bf16[64,3584]{1,0:T(8,128)(2,1)S(1)} %get-tuple-element.38), channel_id=1, source_target_pairs={{0,1},{1,2},{2,3},{3,0},{4,5},{5,6},{6,7},{7,4},{8,9},{9,10},{10,1... | collective-permute-start | bytes 1376264 | tf_op jit(solution)/shard_map/ppermute | solution.py:22
  66.8 11.1 %collective-permute-start.37 = (bf16[64,3584]{1,0:T(8,128)(2,1)S(1)}, bf16[64,3584]{1,0:T(8,128)(2,1)S(1)}, u32[]{:S(2)}, u32[]{:S(2)}) collective-permute-start(bf16[64,3584]{1,0:T(8,128)(2,1)S(1)} %get-tuple-element.37), channel_id=1, source_target_pairs={{0,3},{1,0},{2,1},{3,2},{4,7},{5,4},{6,5},{7,6},{8,11},{9,8},{10,9... | collective-permute-start | bytes 1376264 | tf_op jit(solution)/shard_map/ppermute | solution.py:22
  74.0 7.3 %collective-permute-start.20 = (bf16[32,3584]{1,0:T(8,128)(2,1)S(1)}, bf16[32,3584]{1,0:T(8,128)(2,1)S(1)}, u32[]{:S(2)}, u32[]{:S(2)}) collective-permute-start(bf16[32,3584]{1,0:T(8,128)(2,1)S(1)} %get-tuple-element.40), channel_id=1, source_target_pairs={{0,8},{1,9},{2,10},{3,11},{4,12},{5,13},{6,14},{7,15},{8,16},{9,17... | collective-permute-start | bytes 688136 | tf_op jit(solution)/shard_map/ppermute | solution.py:22
  74.1 7.2 %collective-permute-start.22 = (bf16[32,3584]{1,0:T(8,128)(2,1)S(1)}, bf16[32,3584]{1,0:T(8,128)(2,1)S(1)}, u32[]{:S(2)}, u32[]{:S(2)}) collective-permute-start(bf16[32,3584]{1,0:T(8,128)(2,1)S(1)} %get-tuple-element.39), channel_id=1, source_target_pairs={{0,24},{1,25},{2,26},{3,27},{4,28},{5,29},{6,30},{7,31},{8,0},{9,1... | collective-permute-start | bytes 688136 | tf_op jit(solution)/shard_map/ppermute | solution.py:22
  78.1 7.9 %collective-permute-start.36 = (bf16[32,3584]{1,0:T(8,128)(2,1)S(1)}, bf16[32,3584]{1,0:T(8,128)(2,1)S(1)}, u32[]{:S(2)}, u32[]{:S(2)}) collective-permute-start(bf16[32,3584]{1,0:T(8,128)(2,1)S(1)} %get-tuple-element.36), channel_id=1, source_target_pairs={{0,1},{1,2},{2,3},{3,0},{4,5},{5,6},{6,7},{7,4},{8,9},{9,10},{10,1... | collective-permute-start | bytes 688136 | tf_op jit(solution)/shard_map/ppermute | solution.py:22
  78.7 8.2 %collective-permute-start.38 = (bf16[32,3584]{1,0:T(8,128)(2,1)S(1)}, bf16[32,3584]{1,0:T(8,128)(2,1)S(1)}, u32[]{:S(2)}, u32[]{:S(2)}) collective-permute-start(bf16[32,3584]{1,0:T(8,128)(2,1)S(1)} %get-tuple-element.35), channel_id=1, source_target_pairs={{0,3},{1,0},{2,1},{3,2},{4,7},{5,4},{6,5},{7,6},{8,11},{9,8},{10,9... | collective-permute-start | bytes 688136 | tf_op jit(solution)/shard_map/ppermute | solution.py:22
  81.5 7.2 %collective-permute-start.23 = (bf16[16,3584]{1,0:T(8,128)(2,1)S(1)}, bf16[16,3584]{1,0:T(8,128)(2,1)S(1)}, u32[]{:S(2)}, u32[]{:S(2)}) collective-permute-start(bf16[16,3584]{1,0:T(8,128)(2,1)S(1)} %get-tuple-element.48), channel_id=1, source_target_pairs={{0,2},{1,3},{2,0},{3,1},{4,6},{5,7},{6,4},{7,5},{8,10},{9,11},{10,... | collective-permute-start | bytes 344072 | tf_op jit(solution)/shard_map/ppermute | solution.py:22
  82.7 8.7 %collective-permute-start.24 = (bf16[16,3584]{1,0:T(8,128)(2,1)S(1)}, bf16[16,3584]{1,0:T(8,128)(2,1)S(1)}, u32[]{:S(2)}, u32[]{:S(2)}) collective-permute-start(bf16[16,3584]{1,0:T(8,128)(2,1)S(1)} %get-tuple-element.50), channel_id=1, source_target_pairs={{0,1},{1,2},{2,3},{3,0},{4,5},{5,6},{6,7},{7,4},{8,9},{9,10},{10,1... | collective-permute-start | bytes 344072 | tf_op jit(solution)/shard_map/ppermute | solution.py:22
  84.5 6.8 %collective-permute-start.25 = (bf16[16,3584]{1,0:T(8,128)(2,1)S(1)}, bf16[16,3584]{1,0:T(8,128)(2,1)S(1)}, u32[]{:S(2)}, u32[]{:S(2)}) collective-permute-start(bf16[16,3584]{1,0:T(8,128)(2,1)S(1)} %get-tuple-element.49), channel_id=1, source_target_pairs={{0,3},{1,0},{2,1},{3,2},{4,7},{5,4},{6,5},{7,6},{8,11},{9,8},{10,9... | collective-permute-start | bytes 344072 | tf_op jit(solution)/shard_map/ppermute | solution.py:22
  87.0 7.1 %collective-permute-start.39 = (bf16[16,3584]{1,0:T(8,128)(2,1)S(1)}, bf16[16,3584]{1,0:T(8,128)(2,1)S(1)}, u32[]{:S(2)}, u32[]{:S(2)}) collective-permute-start(bf16[16,3584]{1,0:T(8,128)(2,1)S(1)} %get-tuple-element.45), channel_id=1, source_target_pairs={{0,16},{1,17},{2,18},{3,19},{4,20},{5,21},{6,22},{7,23},{8,24},{9,... | collective-permute-start | bytes 344072 | tf_op jit(solution)/shard_map/ppermute | solution.py:22
  88.6 6.5 %collective-permute-start.40 = (bf16[16,3584]{1,0:T(8,128)(2,1)S(1)}, bf16[16,3584]{1,0:T(8,128)(2,1)S(1)}, u32[]{:S(2)}, u32[]{:S(2)}) collective-permute-start(bf16[16,3584]{1,0:T(8,128)(2,1)S(1)} %get-tuple-element.47), channel_id=1, source_target_pairs={{0,8},{1,9},{2,10},{3,11},{4,12},{5,13},{6,14},{7,15},{8,16},{9,17... | collective-permute-start | bytes 344072 | tf_op jit(solution)/shard_map/ppermute | solution.py:22
  88.7 6.5 %collective-permute-start.41 = (bf16[16,3584]{1,0:T(8,128)(2,1)S(1)}, bf16[16,3584]{1,0:T(8,128)(2,1)S(1)}, u32[]{:S(2)}, u32[]{:S(2)}) collective-permute-start(bf16[16,3584]{1,0:T(8,128)(2,1)S(1)} %get-tuple-element.46), channel_id=1, source_target_pairs={{0,24},{1,25},{2,26},{3,27},{4,28},{5,29},{6,30},{7,31},{8,0},{9,1... | collective-permute-start | bytes 344072 | tf_op jit(solution)/shard_map/ppermute | solution.py:22
  91.4 6.6 %collective-permute-start.26 = (bf16[16,3584]{1,0:T(8,128)(2,1)S(1)}, bf16[16,3584]{1,0:T(8,128)(2,1)S(1)}, u32[]{:S(2)}, u32[]{:S(2)}) collective-permute-start(bf16[16,3584]{1,0:T(8,128)(2,1)S(1)} %fusion.33), channel_id=1, source_target_pairs={{0,4},{1,5},{2,6},{3,7},{4,0},{5,1},{6,2},{7,3},{8,12},{9,13},{10,... | collective-permute-start | bytes 344072 | tf_op jit(solution)/shard_map/ppermute | solution.py:22
  100.7 8.0 %collective-permute-start.43 = (bf16[16,3584]{1,0:T(8,128)(2,1)S(1)}, bf16[16,3584]{1,0:T(8,128)(2,1)S(1)}, u32[]{:S(2)}, u32[]{:S(2)}) collective-permute-start(bf16[16,3584]{1,0:T(8,128)(2,1)S(1)} %get-tuple-element.26), channel_id=1, source_target_pairs={{0,24},{1,25},{2,26},{3,27},{4,28},{5,29},{6,30},{7,31},{8,0},{9,1... | collective-permute-start | bytes 344072 | tf_op jit(solution)/shard_map/ppermute | solution.py:22
  101.8 7.6 %collective-permute-start.44 = (bf16[16,3584]{1,0:T(8,128)(2,1)S(1)}, bf16[16,3584]{1,0:T(8,128)(2,1)S(1)}, u32[]{:S(2)}, u32[]{:S(2)}) collective-permute-start(bf16[16,3584]{1,0:T(8,128)(2,1)S(1)} %get-tuple-element.26), channel_id=1, source_target_pairs={{0,16},{1,17},{2,18},{3,19},{4,20},{5,21},{6,22},{7,23},{8,24},{9,... | collective-permute-start | bytes 344072 | tf_op jit(solution)/shard_map/ppermute | solution.py:22
  104.5 9.1 %collective-permute-start.27 = (bf16[16,3584]{1,0:T(8,128)(2,1)S(1)}, bf16[16,3584]{1,0:T(8,128)(2,1)S(1)}, u32[]{:S(2)}, u32[]{:S(2)}) collective-permute-start(bf16[16,3584]{1,0:T(8,128)(2,1)S(1)} %get-tuple-element.90), channel_id=1, source_target_pairs={{0,3},{1,0},{2,1},{3,2},{4,7},{5,4},{6,5},{7,6},{8,11},{9,8},{10,9... | collective-permute-start | bytes 344072 | tf_op jit(solution)/shard_map/ppermute | solution.py:22
  108.7 5.3 %collective-permute-start.28 = (bf16[16,3584]{1,0:T(8,128)(2,1)S(1)}, bf16[16,3584]{1,0:T(8,128)(2,1)S(1)}, u32[]{:S(2)}, u32[]{:S(2)}) collective-permute-start(bf16[16,3584]{1,0:T(8,128)(2,1)S(1)} %get-tuple-element.90), channel_id=1, source_target_pairs={{0,2},{1,3},{2,0},{3,1},{4,6},{5,7},{6,4},{7,5},{8,10},{9,11},{10,... | collective-permute-start | bytes 344072 | tf_op jit(solution)/shard_map/ppermute | solution.py:22
  108.7 6.1 %collective-permute-start.29 = (bf16[16,3584]{1,0:T(8,128)(2,1)S(1)}, bf16[16,3584]{1,0:T(8,128)(2,1)S(1)}, u32[]{:S(2)}, u32[]{:S(2)}) collective-permute-start(bf16[16,3584]{1,0:T(8,128)(2,1)S(1)} %get-tuple-element.90), channel_id=1, source_target_pairs={{0,1},{1,2},{2,3},{3,0},{4,5},{5,6},{6,7},{7,4},{8,9},{9,10},{10,1... | collective-permute-start | bytes 344072 | tf_op jit(solution)/shard_map/ppermute | solution.py:22
  109.4 11.0 %collective-permute-start.46 = (bf16[64,3584]{1,0:T(8,128)(2,1)S(1)}, bf16[64,3584]{1,0:T(8,128)(2,1)S(1)}, u32[]{:S(2)}, u32[]{:S(2)}) collective-permute-start(bf16[64,3584]{1,0:T(8,128)(2,1)S(1)} %pad_maximum_fusion.3), channel_id=1, source_target_pairs={{0,3},{1,0},{2,1},{3,2},{4,7},{5,4},{6,5},{7,6},{8,11},{9,8},{10,9... | collective-permute-start | bytes 1376264 | tf_op jit(solution)/shard_map/ppermute | solution.py:22
  113.6 10.3 %collective-permute-start.48 = (bf16[64,3584]{1,0:T(8,128)(2,1)S(1)}, bf16[64,3584]{1,0:T(8,128)(2,1)S(1)}, u32[]{:S(2)}, u32[]{:S(2)}) collective-permute-start(bf16[64,3584]{1,0:T(8,128)(2,1)S(1)} %pad_maximum_fusion.3), channel_id=1, source_target_pairs={{0,1},{1,2},{2,3},{3,0},{4,5},{5,6},{6,7},{7,4},{8,9},{9,10},{10,1... | collective-permute-start | bytes 1376264 | tf_op jit(solution)/shard_map/ppermute | solution.py:22
  114.8 13.6 %collective-permute-start.30 = (bf16[64,3584]{1,0:T(8,128)(2,1)S(1)}, bf16[64,3584]{1,0:T(8,128)(2,1)S(1)}, u32[]{:S(2)}, u32[]{:S(2)}) collective-permute-start(bf16[64,3584]{1,0:T(8,128)(2,1)S(1)} %pad_maximum_fusion.2), channel_id=1, source_target_pairs={{0,24},{1,25},{2,26},{3,27},{4,28},{5,29},{6,30},{7,31},{8,0},{9,1... | collective-permute-start | bytes 1376264 | tf_op jit(solution)/shard_map/ppermute | solution.py:22
  119.9 12.0 %collective-permute-start.32 = (bf16[64,3584]{1,0:T(8,128)(2,1)S(1)}, bf16[64,3584]{1,0:T(8,128)(2,1)S(1)}, u32[]{:S(2)}, u32[]{:S(2)}) collective-permute-start(bf16[64,3584]{1,0:T(8,128)(2,1)S(1)} %pad_maximum_fusion.2), channel_id=1, source_target_pairs={{0,8},{1,9},{2,10},{3,11},{4,12},{5,13},{6,14},{7,15},{8,16},{9,17... | collective-permute-start | bytes 1376264 | tf_op jit(solution)/shard_map/ppermute | solution.py:22
  120.5 11.6 %collective-permute-start.47 = (bf16[32,3584]{1,0:T(8,128)(2,1)S(1)}, bf16[32,3584]{1,0:T(8,128)(2,1)S(1)}, u32[]{:S(2)}, u32[]{:S(2)}) collective-permute-start(bf16[32,3584]{1,0:T(8,128)(2,1)S(1)} %slice.273), channel_id=1, source_target_pairs={{0,3},{1,0},{2,1},{3,2},{4,7},{5,4},{6,5},{7,6},{8,11},{9,8},{10,9... | collective-permute-start | bytes 688136 | tf_op jit(solution)/shard_map/ppermute | solution.py:22
  124.0 8.1 %collective-permute-start.49 = (bf16[32,3584]{1,0:T(8,128)(2,1)S(1)}, bf16[32,3584]{1,0:T(8,128)(2,1)S(1)}, u32[]{:S(2)}, u32[]{:S(2)}) collective-permute-start(bf16[32,3584]{1,0:T(8,128)(2,1)S(1)} %slice.274), channel_id=1, source_target_pairs={{0,1},{1,2},{2,3},{3,0},{4,5},{5,6},{6,7},{7,4},{8,9},{9,10},{10,1... | collective-permute-start | bytes 688136 | tf_op jit(solution)/shard_map/ppermute | solution.py:22
  128.4 6.4 %collective-permute-start.31 = (bf16[32,3584]{1,0:T(8,128)(2,1)S(1)}, bf16[32,3584]{1,0:T(8,128)(2,1)S(1)}, u32[]{:S(2)}, u32[]{:S(2)}) collective-permute-start(bf16[32,3584]{1,0:T(8,128)(2,1)S(1)} %slice.258), channel_id=1, source_target_pairs={{0,24},{1,25},{2,26},{3,27},{4,28},{5,29},{6,30},{7,31},{8,0},{9,1... | collective-permute-start | bytes 688136 | tf_op jit(solution)/shard_map/ppermute | solution.py:22
  131.9 6.2 %collective-permute-start.33 = (bf16[32,3584]{1,0:T(8,128)(2,1)S(1)}, bf16[32,3584]{1,0:T(8,128)(2,1)S(1)}, u32[]{:S(2)}, u32[]{:S(2)}) collective-permute-start(bf16[32,3584]{1,0:T(8,128)(2,1)S(1)} %slice.259), channel_id=1, source_target_pairs={{0,8},{1,9},{2,10},{3,11},{4,12},{5,13},{6,14},{7,15},{8,16},{9,17... | collective-permute-start | bytes 688136 | tf_op jit(solution)/shard_map/ppermute | solution.py:22
  139.8 7.0 %collective-permute-start.50 = (bf16[264,768]{1,0:T(8,128)(2,1)S(1)}, bf16[264,768]{1,0:T(8,128)(2,1)S(1)}, u32[]{:S(2)}, u32[]{:S(2)}) collective-permute-start(bf16[264,768]{1,0:T(8,128)(2,1)S(1)} %pad_maximum_fusion.4), channel_id=1, source_target_pairs={{0,32},{32,0},{64,96},{96,64},{1,33},{33,1},{65,97},{97,65},{2,34}... | collective-permute-start | bytes 1216520 | tf_op jit(solution)/shard_map/ppermute | solution.py:26
  147.0 11.0 %collective-permute-start.51 = (bf16[264,768]{1,0:T(8,128)(2,1)S(1)}, bf16[264,768]{1,0:T(8,128)(2,1)S(1)}, u32[]{:S(2)}, u32[]{:S(2)}) collective-permute-start(bf16[264,768]{1,0:T(8,128)(2,1)S(1)} %pad_maximum_fusion.5), channel_id=1, source_target_pairs={{0,64},{32,96},{64,0},{96,32},{1,65},{33,97},{65,1},{97,33},{2,66}... | collective-permute-start | bytes 1216520 | tf_op jit(solution)/shard_map/ppermute | solution.py:26
  (10 other events, 74.0 us)

commit v6 on v5

--- a/solution.py
+++ b/solution.py
@@ -133,13 +133,13 @@
         misfit = rebuilt + dec_bias[0][None, :] - wide(pairs[slot])
         errors.append(narrow(2.0 * misfit))
     errors = [gather_rows(errors[slot], slot) for slot in (0, 1)]
-    errors = list(lax.optimization_barrier(tuple(errors)))
-    back = [
-        lax.dot_general(
-            rows, dec_local, (((1,), (1,)), ((), ())), preferred_element_type=jnp.float32
+    back = [None, None]
+    for slot in (1, 0):
+        back[slot] = lax.dot_general(
+            errors[slot], dec_local, (((1,), (1,)), ((), ())), preferred_element_type=jnp.float32
         )
-        for rows in errors
-    ]
+        if slot == 1:
+            errors[0], back[1] = lax.optimization_barrier((errors[0], back[1]))
     def norm_rows(norms):
         head = rounded(norms)
         tail = rounded(norms - head)

time: 166 us -> 174 us (1.048)
  waiting for transfers between devices: 48.8 us -> 59.9 us
  starting transfers between devices: 88.3 us -> 83.8 us
    ppermute x45, starting transfers between devices: 73.5 us -> 65.9 us  [shift(): return lax.ppermute(value, ('layer', 'latent'), pairs)]
    ppermute x45, waiting for transfers between devices: 39.2 us -> 44.9 us  [shift(): return lax.ppermute(value, ('layer', 'latent'), pairs)]
    ppermute x8, waiting for transfers between devices: 9.59 us -> 15.1 us  [layer_swap(): return lax.ppermute(value, 'layer', [(i, i ^ bit) for i in range(4)])]
    ppermute x8, starting transfers between devices: 14.8 us -> 17.9 us  [layer_swap(): return lax.ppermute(value, 'layer', [(i, i ^ bit) for i in range(4)])]
  transfers between devices with their start and end apart: 53 -> 53, of which waited for: 27 -> 26; matrix products, arithmetic and copies ran while one was open for 11% -> 10% of each run, Pallas kernels for 0% -> 0%
where the time goes in v6:
time: 174 us; the launch traced here: 173 us
  starting transfers between devices  83.8 us (48%)
  waiting for transfers between devices  59.9 us (34%)
  matrix products  20.5 us (12%)
  other arithmetic  5.25 us (3%)
  local copies, waits for them, and re-layouts  2.45 us (1%)
    ppermute x45, starting transfers between devices, shift(): return lax.ppermute(value, ('layer', 'latent'), pairs)  65.9 us
    ppermute x45, waiting for transfers between devices, shift(): return lax.ppermute(value, ('layer', 'latent'), pairs)  44.9 us
    ppermute x8, starting transfers between devices, layer_swap(): return lax.ppermute(value, 'layer', [(i, i ^ bit) for i in range(4)])  17.9 us
    ppermute x8, waiting for transfers between devices, layer_swap(): return lax.ppermute(value, 'layer', [(i, i ^ bit) for i in range(4)])  15.1 us
    dot_general x1, matrix products, per_device(): lax.dot_general(join(*latents), join(*errors), (((0,), (0,)), ((), ())),...  5.76 us
    dot_general x1, matrix products, per_device(): lax.dot_general(join(*gathered), join(*pre_grads), (((0,), (0,)), ((), ()...  4.84 us
    dot_general x4, matrix products, per_device(): jnp.dot(rows, dec_copy, preferred_element_type=jnp.float32)  3.56 us
  transfers between devices with their start and end apart: 53, of which 26 were waited for; matrix products, arithmetic and copies ran while one was open for 10% of the time, Pallas kernels for 0%

profile of v6, /device:TPU:1, one launch (start us, length us, event | category | flops | bytes accessed | tf_op | source)
XLA Modules:
  0.0 173.5 jit_solution(975532549758381688)
XLA Ops:
  0.6 4.5 %collective-permute-start = (bf16[16,3584]{1,0:T(8,128)(2,1)}, bf16[16,3584]{1,0:T(8,128)(2,1)S(1)}, u32[]{:S(2)}, u32[]{:S(2)}) collective-permute-start(bf16[16,3584]{1,0:T(8,128)(2,1)} %bitcast.43), channel_id=1, source_target_pairs={{0,4},{1,5},{2,6},{3,7},{4,0},{5,1},{6,2},{7,3},{8,12},{9,13},{10,... | collective-permute-start | bytes 344072 | tf_op jit(solution)/shard_map/ppermute | solution.py:22
  6.8 1.4 collective-permute-done
  8.3 2.5 %collective-permute-start.1 = (bf16[16,3584]{1,0:T(8,128)(2,1)S(1)}, bf16[16,3584]{1,0:T(8,128)(2,1)S(1)}, u32[]{:S(2)}, u32[]{:S(2)}) collective-permute-start(bf16[16,3584]{1,0:T(8,128)(2,1)S(1)} %get-tuple-element.68), channel_id=1, source_target_pairs={{0,3},{1,0},{2,1},{3,2},{4,7},{5,4},{6,5},{7,6},{8,11},{9,8},{10,9... | collective-permute-start | bytes 344072 | tf_op jit(solution)/shard_map/ppermute | solution.py:22
  12.0 2.8 %collective-permute-start.8 = (bf16[16,3584]{1,0:T(8,128)(2,1)S(1)}, bf16[16,3584]{1,0:T(8,128)(2,1)S(1)}, u32[]{:S(2)}, u32[]{:S(2)}) collective-permute-start(bf16[16,3584]{1,0:T(8,128)(2,1)S(1)} %get-tuple-element.30), channel_id=1, source_target_pairs={{0,24},{1,25},{2,26},{3,27},{4,28},{5,29},{6,30},{7,31},{8,0},{9,1... | collective-permute-start | bytes 344072 | tf_op jit(solution)/shard_map/ppermute | solution.py:22
  16.1 1.4 collective-permute-done.3
  17.6 2.5 %collective-permute-start.4 = (bf16[64,3584]{1,0:T(8,128)(2,1)S(1)}, bf16[64,3584]{1,0:T(8,128)(2,1)S(1)}, u32[]{:S(2)}, u32[]{:S(2)}) collective-permute-start(bf16[64,3584]{1,0:T(8,128)(2,1)S(1)} %pad_maximum_fusion), channel_id=1, source_target_pairs={{0,24},{1,25},{2,26},{3,27},{4,28},{5,29},{6,30},{7,31},{8,0},{9,1... | collective-permute-start | bytes 1376264 | tf_op jit(solution)/shard_map/ppermute | solution.py:22
  20.7 1.5 collective-permute-done.10
  22.2 2.4 %collective-permute-start.11 = (bf16[64,3584]{1,0:T(8,128)(2,1)S(1)}, bf16[64,3584]{1,0:T(8,128)(2,1)S(1)}, u32[]{:S(2)}, u32[]{:S(2)}) collective-permute-start(bf16[64,3584]{1,0:T(8,128)(2,1)S(1)} %pad_maximum_fusion.1), channel_id=1, source_target_pairs={{0,3},{1,0},{2,1},{3,2},{4,7},{5,4},{6,5},{7,6},{8,11},{9,8},{10,9... | collective-permute-start | bytes 1376264 | tf_op jit(solution)/shard_map/ppermute | solution.py:22
  25.5 3.5 %collective-permute-start.5 = (bf16[32,3584]{1,0:T(8,128)(2,1)S(1)}, bf16[32,3584]{1,0:T(8,128)(2,1)S(1)}, u32[]{:S(2)}, u32[]{:S(2)}) collective-permute-start(bf16[32,3584]{1,0:T(8,128)(2,1)S(1)} %slice.238), channel_id=1, source_target_pairs={{0,24},{1,25},{2,26},{3,27},{4,28},{5,29},{6,30},{7,31},{8,0},{9,1... | collective-permute-start | bytes 688136 | tf_op jit(solution)/shard_map/ppermute | solution.py:22
  29.1 5.5 %collective-permute-done.11 = bf16[64,3584]{1,0:T(8,128)(2,1)S(1)} collective-permute-done((bf16[64,3584]{1,0:T(8,128)(2,1)S(1)}, bf16[64,3584]{1,0:T(8,128)(2,1)S(1)}, u32[]{:S(2)}, u32[]{:S(2)}) %collective-permute-start.11) | collective-permute-done | bytes 458784 | tf_op jit(solution)/shard_map/ppermute | solution.py:22
  34.6 3.0 %collective-permute-start.12 = (bf16[32,3584]{1,0:T(8,128)(2,1)S(1)}, bf16[32,3584]{1,0:T(8,128)(2,1)S(1)}, u32[]{:S(2)}, u32[]{:S(2)}) collective-permute-start(bf16[32,3584]{1,0:T(8,128)(2,1)S(1)} %slice.240), channel_id=1, source_target_pairs={{0,3},{1,0},{2,1},{3,2},{4,7},{5,4},{6,5},{7,6},{8,11},{9,8},{10,9... | collective-permute-start | bytes 688136 | tf_op jit(solution)/shard_map/ppermute | solution.py:22
  38.2 3.0 %collective-permute-done.12 = bf16[32,3584]{1,0:T(8,128)(2,1)S(1)} collective-permute-done((bf16[32,3584]{1,0:T(8,128)(2,1)S(1)}, bf16[32,3584]{1,0:T(8,128)(2,1)S(1)}, u32[]{:S(2)}, u32[]{:S(2)}) %collective-permute-start.12) | collective-permute-done | bytes 229408 | tf_op jit(solution)/shard_map/ppermute | solution.py:22
  41.3 3.2 %collective-permute-done.14 = bf16[32,3584]{1,0:T(8,128)(2,1)S(1)} collective-permute-done((bf16[32,3584]{1,0:T(8,128)(2,1)S(1)}, bf16[32,3584]{1,0:T(8,128)(2,1)S(1)}, u32[]{:S(2)}, u32[]{:S(2)}) %collective-permute-start.14) | collective-permute-done | bytes 229408 | tf_op jit(solution)/shard_map/ppermute | solution.py:22
  44.6 1.6 fusion.9
  46.2 2.8 %collective-permute-start.15 = (bf16[256,768]{1,0:T(8,128)(2,1)S(1)}, bf16[256,768]{1,0:T(8,128)(2,1)S(1)}, u32[]{:S(2)}, u32[]{:S(2)}) collective-permute-start(bf16[256,768]{1,0:T(8,128)(2,1)S(1)} %fusion.9), channel_id=1, source_target_pairs={{0,32},{32,0},{64,96},{96,64},{1,33},{33,1},{65,97},{97,65},{2,34}... | collective-permute-start | bytes 1179656 | tf_op jit(solution)/shard_map/ppermute | solution.py:26
  49.1 1.6 fusion.7
  53.6 8.0 %collective-permute-done.17 = bf16[128,768]{1,0:T(8,128)(2,1)S(1)} collective-permute-done((bf16[128,768]{1,0:T(8,128)(2,1)S(1)}, bf16[128,768]{1,0:T(8,128)(2,1)S(1)}, u32[]{:S(2)}, u32[]{:S(2)}) %collective-permute-start.17) | collective-permute-done | bytes 196640 | tf_op jit(solution)/shard_map/ppermute | solution.py:26
  67.7 2.7 %collective-permute-start.37 = (bf16[64,3584]{1,0:T(8,128)(2,1)S(1)}, bf16[64,3584]{1,0:T(8,128)(2,1)S(1)}, u32[]{:S(2)}, u32[]{:S(2)}) collective-permute-start(bf16[64,3584]{1,0:T(8,128)(2,1)S(1)} %get-tuple-element.37), channel_id=1, source_target_pairs={{0,3},{1,0},{2,1},{3,2},{4,7},{5,4},{6,5},{7,6},{8,11},{9,8},{10,9... | collective-permute-start | bytes 1376264 | tf_op jit(solution)/shard_map/ppermute | solution.py:22
  70.8 2.4 %collective-permute-start.21 = (bf16[64,3584]{1,0:T(8,128)(2,1)S(1)}, bf16[64,3584]{1,0:T(8,128)(2,1)S(1)}, u32[]{:S(2)}, u32[]{:S(2)}) collective-permute-start(bf16[64,3584]{1,0:T(8,128)(2,1)S(1)} %get-tuple-element.41), channel_id=1, source_target_pairs={{0,24},{1,25},{2,26},{3,27},{4,28},{5,29},{6,30},{7,31},{8,0},{9,1... | collective-permute-start | bytes 1376264 | tf_op jit(solution)/shard_map/ppermute | solution.py:22
  74.4 3.1 %collective-permute-done.35 = bf16[64,3584]{1,0:T(8,128)(2,1)S(1)} collective-permute-done((bf16[64,3584]{1,0:T(8,128)(2,1)S(1)}, bf16[64,3584]{1,0:T(8,128)(2,1)S(1)}, u32[]{:S(2)}, u32[]{:S(2)}) %collective-permute-start.35) | collective-permute-done | bytes 458784 | tf_op jit(solution)/shard_map/ppermute | solution.py:22
  78.1 2.2 %collective-permute-start.38 = (bf16[32,3584]{1,0:T(8,128)(2,1)S(1)}, bf16[32,3584]{1,0:T(8,128)(2,1)S(1)}, u32[]{:S(2)}, u32[]{:S(2)}) collective-permute-start(bf16[32,3584]{1,0:T(8,128)(2,1)S(1)} %get-tuple-element.35), channel_id=1, source_target_pairs={{0,3},{1,0},{2,1},{3,2},{4,7},{5,4},{6,5},{7,6},{8,11},{9,8},{10,9... | collective-permute-start | bytes 688136 | tf_op jit(solution)/shard_map/ppermute | solution.py:22
  80.3 1.5 collective-permute-done.19
  82.1 2.9 %collective-permute-start.22 = (bf16[32,3584]{1,0:T(8,128)(2,1)S(1)}, bf16[32,3584]{1,0:T(8,128)(2,1)S(1)}, u32[]{:S(2)}, u32[]{:S(2)}) collective-permute-start(bf16[32,3584]{1,0:T(8,128)(2,1)S(1)} %get-tuple-element.39), channel_id=1, source_target_pairs={{0,24},{1,25},{2,26},{3,27},{4,28},{5,29},{6,30},{7,31},{8,0},{9,1... | collective-permute-start | bytes 688136 | tf_op jit(solution)/shard_map/ppermute | solution.py:22
  85.3 1.5 collective-permute-start.41
  88.0 1.9 %collective-permute-done.20 = bf16[32,3584]{1,0:T(8,128)(2,1)S(1)} collective-permute-done((bf16[32,3584]{1,0:T(8,128)(2,1)S(1)}, bf16[32,3584]{1,0:T(8,128)(2,1)S(1)}, u32[]{:S(2)}, u32[]{:S(2)}) %collective-permute-start.20) | collective-permute-done | bytes 229408 | tf_op jit(solution)/shard_map/ppermute | solution.py:22
  90.2 3.3 %collective-permute-start.25 = (bf16[16,3584]{1,0:T(8,128)(2,1)S(1)}, bf16[16,3584]{1,0:T(8,128)(2,1)S(1)}, u32[]{:S(2)}, u32[]{:S(2)}) collective-permute-start(bf16[16,3584]{1,0:T(8,128)(2,1)S(1)} %get-tuple-element.49), channel_id=1, source_target_pairs={{0,3},{1,0},{2,1},{3,2},{4,7},{5,4},{6,5},{7,6},{8,11},{9,8},{10,9... | collective-permute-start | bytes 344072 | tf_op jit(solution)/shard_map/ppermute | solution.py:22
  94.9 3.7 %collective-permute-start.42 = (bf16[16,3584]{1,0:T(8,128)(2,1)S(1)}, bf16[16,3584]{1,0:T(8,128)(2,1)S(1)}, u32[]{:S(2)}, u32[]{:S(2)}) collective-permute-start(bf16[16,3584]{1,0:T(8,128)(2,1)S(1)} %fusion.31), channel_id=1, source_target_pairs={{0,4},{1,5},{2,6},{3,7},{4,0},{5,1},{6,2},{7,3},{8,12},{9,13},{10,... | collective-permute-start | bytes 344072 | tf_op jit(solution)/shard_map/ppermute | solution.py:22
  99.8 3.5 %collective-permute-start.26 = (bf16[16,3584]{1,0:T(8,128)(2,1)S(1)}, bf16[16,3584]{1,0:T(8,128)(2,1)S(1)}, u32[]{:S(2)}, u32[]{:S(2)}) collective-permute-start(bf16[16,3584]{1,0:T(8,128)(2,1)S(1)} %fusion.30), channel_id=1, source_target_pairs={{0,4},{1,5},{2,6},{3,7},{4,0},{5,1},{6,2},{7,3},{8,12},{9,13},{10,... | collective-permute-start | bytes 344072 | tf_op jit(solution)/shard_map/ppermute | solution.py:22
  103.3 2.5 %collective-permute-done.26 = bf16[16,3584]{1,0:T(8,128)(2,1)S(1)} collective-permute-done((bf16[16,3584]{1,0:T(8,128)(2,1)S(1)}, bf16[16,3584]{1,0:T(8,128)(2,1)S(1)}, u32[]{:S(2)}, u32[]{:S(2)}) %collective-permute-start.26) | collective-permute-done | bytes 114720 | tf_op jit(solution)/shard_map/ppermute | solution.py:22
  106.0 1.8 %collective-permute-start.27 = (bf16[16,3584]{1,0:T(8,128)(2,1)S(1)}, bf16[16,3584]{1,0:T(8,128)(2,1)S(1)}, u32[]{:S(2)}, u32[]{:S(2)}) collective-permute-start(bf16[16,3584]{1,0:T(8,128)(2,1)S(1)} %get-tuple-element.90), channel_id=1, source_target_pairs={{0,3},{1,0},{2,1},{3,2},{4,7},{5,4},{6,5},{7,6},{8,11},{9,8},{10,9... | collective-permute-start | bytes 344072 | tf_op jit(solution)/shard_map/ppermute | solution.py:22
  108.5 2.3 %collective-permute-start.43 = (bf16[16,3584]{1,0:T(8,128)(2,1)S(1)}, bf16[16,3584]{1,0:T(8,128)(2,1)S(1)}, u32[]{:S(2)}, u32[]{:S(2)}) collective-permute-start(bf16[16,3584]{1,0:T(8,128)(2,1)S(1)} %get-tuple-element.26), channel_id=1, source_target_pairs={{0,24},{1,25},{2,26},{3,27},{4,28},{5,29},{6,30},{7,31},{8,0},{9,1... | collective-permute-start | bytes 344072 | tf_op jit(solution)/shard_map/ppermute | solution.py:22
  111.3 2.0 %collective-permute-done.28 = bf16[16,3584]{1,0:T(8,128)(2,1)S(1)} collective-permute-done((bf16[16,3584]{1,0:T(8,128)(2,1)S(1)}, bf16[16,3584]{1,0:T(8,128)(2,1)S(1)}, u32[]{:S(2)}, u32[]{:S(2)}) %collective-permute-start.28) | collective-permute-done | bytes 114720 | tf_op jit(solution)/shard_map/ppermute | solution.py:22
  114.3 2.2 %collective-permute-start.30 = (bf16[64,3584]{1,0:T(8,128)(2,1)S(1)}, bf16[64,3584]{1,0:T(8,128)(2,1)S(1)}, u32[]{:S(2)}, u32[]{:S(2)}) collective-permute-start(bf16[64,3584]{1,0:T(8,128)(2,1)S(1)} %pad_maximum_fusion.2), channel_id=1, source_target_pairs={{0,24},{1,25},{2,26},{3,27},{4,28},{5,29},{6,30},{7,31},{8,0},{9,1... | collective-permute-start | bytes 1376264 | tf_op jit(solution)/shard_map/ppermute | solution.py:22
  116.9 2.8 %collective-permute-start.46 = (bf16[64,3584]{1,0:T(8,128)(2,1)S(1)}, bf16[64,3584]{1,0:T(8,128)(2,1)S(1)}, u32[]{:S(2)}, u32[]{:S(2)}) collective-permute-start(bf16[64,3584]{1,0:T(8,128)(2,1)S(1)} %pad_maximum_fusion.3), channel_id=1, source_target_pairs={{0,3},{1,0},{2,1},{3,2},{4,7},{5,4},{6,5},{7,6},{8,11},{9,8},{10,9... | collective-permute-start | bytes 1376264 | tf_op jit(solution)/shard_map/ppermute | solution.py:22
  119.8 4.7 %collective-permute-done.30 = bf16[64,3584]{1,0:T(8,128)(2,1)S(1)} collective-permute-done((bf16[64,3584]{1,0:T(8,128)(2,1)S(1)}, bf16[64,3584]{1,0:T(8,128)(2,1)S(1)}, u32[]{:S(2)}, u32[]{:S(2)}) %collective-permute-start.30) | collective-permute-done | bytes 458784 | tf_op jit(solution)/shard_map/ppermute | solution.py:22
  124.5 3.4 %collective-permute-start.31 = (bf16[32,3584]{1,0:T(8,128)(2,1)S(1)}, bf16[32,3584]{1,0:T(8,128)(2,1)S(1)}, u32[]{:S(2)}, u32[]{:S(2)}) collective-permute-start(bf16[32,3584]{1,0:T(8,128)(2,1)S(1)} %slice.258), channel_id=1, source_target_pairs={{0,24},{1,25},{2,26},{3,27},{4,28},{5,29},{6,30},{7,31},{8,0},{9,1... | collective-permute-start | bytes 688136 | tf_op jit(solution)/shard_map/ppermute | solution.py:22
  128.0 2.7 %collective-permute-start.47 = (bf16[32,3584]{1,0:T(8,128)(2,1)S(1)}, bf16[32,3584]{1,0:T(8,128)(2,1)S(1)}, u32[]{:S(2)}, u32[]{:S(2)}) collective-permute-start(bf16[32,3584]{1,0:T(8,128)(2,1)S(1)} %slice.273), channel_id=1, source_target_pairs={{0,3},{1,0},{2,1},{3,2},{4,7},{5,4},{6,5},{7,6},{8,11},{9,8},{10,9... | collective-permute-start | bytes 688136 | tf_op jit(solution)/shard_map/ppermute | solution.py:22
  130.9 5.3 %collective-permute-done.47 = bf16[32,3584]{1,0:T(8,128)(2,1)S(1)} collective-permute-done((bf16[32,3584]{1,0:T(8,128)(2,1)S(1)}, bf16[32,3584]{1,0:T(8,128)(2,1)S(1)}, u32[]{:S(2)}, u32[]{:S(2)}) %collective-permute-start.47) | collective-permute-done | bytes 229408 | tf_op jit(solution)/shard_map/ppermute | solution.py:22
  136.3 3.5 %collective-permute-done.49 = bf16[32,3584]{1,0:T(8,128)(2,1)S(1)} collective-permute-done((bf16[32,3584]{1,0:T(8,128)(2,1)S(1)}, bf16[32,3584]{1,0:T(8,128)(2,1)S(1)}, u32[]{:S(2)}, u32[]{:S(2)}) %collective-permute-start.49) | collective-permute-done | bytes 229408 | tf_op jit(solution)/shard_map/ppermute | solution.py:22
  139.8 1.6 fusion.47
  141.5 1.6 fusion.48
  143.3 9.5 %collective-permute-start.50 = (bf16[264,768]{1,0:T(8,128)(2,1)S(1)}, bf16[264,768]{1,0:T(8,128)(2,1)S(1)}, u32[]{:S(2)}, u32[]{:S(2)}) collective-permute-start(bf16[264,768]{1,0:T(8,128)(2,1)S(1)} %pad_maximum_fusion.4), channel_id=1, source_target_pairs={{0,32},{32,0},{64,96},{96,64},{1,33},{33,1},{65,97},{97,65},{2,34}... | collective-permute-start | bytes 1216520 | tf_op jit(solution)/shard_map/ppermute | solution.py:26
  154.4 1.3 collective-permute-start.51
  155.7 5.8 %fusion.3 = bf16[768,3584]{1,0:T(8,128)(2,1)} fusion(bf16[768,3584]{1,0:T(8,128)(2,1)S(1)} %bitcast.42, bf16[512,768]{1,0:T(8,128)(2,1)S(1)} %constant_dynamic-update-slice_fusion.48, bf16[512,3584]{1,0:T(8,128)(2,1)S(1)} %constant_dynamic-update-slice_fusion.52, f32[768]{0:T(1024)S(1)} %add_sqrt_fusion, f32[768]{0:T(1024)S(1)} %broadcast_multiply_fusion), kind=kOutput, calls=%fused_computation.5 | convolution fusion | flops 2832334848 | bytes 15472640 | tf_op jit(solution)/shard_map/dot_general | solution.py:154
  161.4 3.6 %collective-permute-done.51 = bf16[264,768]{1,0:T(8,128)(2,1)S(1)} collective-permute-done((bf16[264,768]{1,0:T(8,128)(2,1)S(1)}, bf16[264,768]{1,0:T(8,128)(2,1)S(1)}, u32[]{:S(2)}, u32[]{:S(2)}) %collective-permute-start.51) | collective-permute-done | bytes 405536 | tf_op jit(solution)/shard_map/ppermute | solution.py:26
  165.3 1.3 collective-permute-start.52
  166.6 1.3 collective-permute-done.52
  168.7 4.8 %fusion.4 = bf16[1,3584,768]{2,1,0:T(8,128)(2,1)} fusion(bf16[512,3584]{1,0:T(8,128)(2,1)S(1)} %get-tuple-element.52, bf16[256,768]{1,0:T(8,128)(2,1)S(1)} %collective-permute-done.52, bf16[256,768]{1,0:T(8,128)(2,1)S(1)} %get-tuple-element.24), kind=kOutput, calls=%fused_computation.7 | convolution fusion | flops 2822897664 | bytes 9961472 | tf_op jit(solution)/shard_map/dot_general | solution.py:168
  (185 shorter events, 28.3 us)
Async XLA Ops:
  0.6 7.6 %collective-permute-start = (bf16[16,3584]{1,0:T(8,128)(2,1)}, bf16[16,3584]{1,0:T(8,128)(2,1)S(1)}, u32[]{:S(2)}, u32[]{:S(2)}) collective-permute-start(bf16[16,3584]{1,0:T(8,128)(2,1)} %bitcast.43), channel_id=1, source_target_pairs={{0,4},{1,5},{2,6},{3,7},{4,0},{5,1},{6,2},{7,3},{8,12},{9,13},{10,... | collective-permute-start | bytes 344072 | tf_op jit(solution)/shard_map/ppermute | solution.py:22
  8.3 6.8 %collective-permute-start.1 = (bf16[16,3584]{1,0:T(8,128)(2,1)S(1)}, bf16[16,3584]{1,0:T(8,128)(2,1)S(1)}, u32[]{:S(2)}, u32[]{:S(2)}) collective-permute-start(bf16[16,3584]{1,0:T(8,128)(2,1)S(1)} %get-tuple-element.68), channel_id=1, source_target_pairs={{0,3},{1,0},{2,1},{3,2},{4,7},{5,4},{6,5},{7,6},{8,11},{9,8},{10,9... | collective-permute-start | bytes 344072 | tf_op jit(solution)/shard_map/ppermute | solution.py:22
  11.4 6.2 %collective-permute-start.3 = (bf16[16,3584]{1,0:T(8,128)(2,1)S(1)}, bf16[16,3584]{1,0:T(8,128)(2,1)S(1)}, u32[]{:S(2)}, u32[]{:S(2)}) collective-permute-start(bf16[16,3584]{1,0:T(8,128)(2,1)S(1)} %get-tuple-element.68), channel_id=1, source_target_pairs={{0,1},{1,2},{2,3},{3,0},{4,5},{5,6},{6,7},{7,4},{8,9},{9,10},{10,1... | collective-permute-start | bytes 344072 | tf_op jit(solution)/shard_map/ppermute | solution.py:22
  12.0 8.1 %collective-permute-start.8 = (bf16[16,3584]{1,0:T(8,128)(2,1)S(1)}, bf16[16,3584]{1,0:T(8,128)(2,1)S(1)}, u32[]{:S(2)}, u32[]{:S(2)}) collective-permute-start(bf16[16,3584]{1,0:T(8,128)(2,1)S(1)} %get-tuple-element.30), channel_id=1, source_target_pairs={{0,24},{1,25},{2,26},{3,27},{4,28},{5,29},{6,30},{7,31},{8,0},{9,1... | collective-permute-start | bytes 344072 | tf_op jit(solution)/shard_map/ppermute | solution.py:22
  14.8 5.9 %collective-permute-start.9 = (bf16[16,3584]{1,0:T(8,128)(2,1)S(1)}, bf16[16,3584]{1,0:T(8,128)(2,1)S(1)}, u32[]{:S(2)}, u32[]{:S(2)}) collective-permute-start(bf16[16,3584]{1,0:T(8,128)(2,1)S(1)} %get-tuple-element.30), channel_id=1, source_target_pairs={{0,16},{1,17},{2,18},{3,19},{4,20},{5,21},{6,22},{7,23},{8,24},{9,... | collective-permute-start | bytes 344072 | tf_op jit(solution)/shard_map/ppermute | solution.py:22
  15.1 7.1 %collective-permute-start.10 = (bf16[16,3584]{1,0:T(8,128)(2,1)S(1)}, bf16[16,3584]{1,0:T(8,128)(2,1)S(1)}, u32[]{:S(2)}, u32[]{:S(2)}) collective-permute-start(bf16[16,3584]{1,0:T(8,128)(2,1)S(1)} %get-tuple-element.30), channel_id=1, source_target_pairs={{0,8},{1,9},{2,10},{3,11},{4,12},{5,13},{6,14},{7,15},{8,16},{9,17... | collective-permute-start | bytes 344072 | tf_op jit(solution)/shard_map/ppermute | solution.py:22
  17.6 7.9 %collective-permute-start.4 = (bf16[64,3584]{1,0:T(8,128)(2,1)S(1)}, bf16[64,3584]{1,0:T(8,128)(2,1)S(1)}, u32[]{:S(2)}, u32[]{:S(2)}) collective-permute-start(bf16[64,3584]{1,0:T(8,128)(2,1)S(1)} %pad_maximum_fusion), channel_id=1, source_target_pairs={{0,24},{1,25},{2,26},{3,27},{4,28},{5,29},{6,30},{7,31},{8,0},{9,1... | collective-permute-start | bytes 1376264 | tf_op jit(solution)/shard_map/ppermute | solution.py:22
  20.1 8.9 %collective-permute-start.6 = (bf16[64,3584]{1,0:T(8,128)(2,1)S(1)}, bf16[64,3584]{1,0:T(8,128)(2,1)S(1)}, u32[]{:S(2)}, u32[]{:S(2)}) collective-permute-start(bf16[64,3584]{1,0:T(8,128)(2,1)S(1)} %pad_maximum_fusion), channel_id=1, source_target_pairs={{0,8},{1,9},{2,10},{3,11},{4,12},{5,13},{6,14},{7,15},{8,16},{9,17... | collective-permute-start | bytes 1376264 | tf_op jit(solution)/shard_map/ppermute | solution.py:22
  22.2 12.4 %collective-permute-start.11 = (bf16[64,3584]{1,0:T(8,128)(2,1)S(1)}, bf16[64,3584]{1,0:T(8,128)(2,1)S(1)}, u32[]{:S(2)}, u32[]{:S(2)}) collective-permute-start(bf16[64,3584]{1,0:T(8,128)(2,1)S(1)} %pad_maximum_fusion.1), channel_id=1, source_target_pairs={{0,3},{1,0},{2,1},{3,2},{4,7},{5,4},{6,5},{7,6},{8,11},{9,8},{10,9... | collective-permute-start | bytes 1376264 | tf_op jit(solution)/shard_map/ppermute | solution.py:22
  24.6 13.0 %collective-permute-start.13 = (bf16[64,3584]{1,0:T(8,128)(2,1)S(1)}, bf16[64,3584]{1,0:T(8,128)(2,1)S(1)}, u32[]{:S(2)}, u32[]{:S(2)}) collective-permute-start(bf16[64,3584]{1,0:T(8,128)(2,1)S(1)} %pad_maximum_fusion.1), channel_id=1, source_target_pairs={{0,1},{1,2},{2,3},{3,0},{4,5},{5,6},{6,7},{7,4},{8,9},{9,10},{10,1... | collective-permute-start | bytes 1376264 | tf_op jit(solution)/shard_map/ppermute | solution.py:22
  25.5 12.3 %collective-permute-start.5 = (bf16[32,3584]{1,0:T(8,128)(2,1)S(1)}, bf16[32,3584]{1,0:T(8,128)(2,1)S(1)}, u32[]{:S(2)}, u32[]{:S(2)}) collective-permute-start(bf16[32,3584]{1,0:T(8,128)(2,1)S(1)} %slice.238), channel_id=1, source_target_pairs={{0,24},{1,25},{2,26},{3,27},{4,28},{5,29},{6,30},{7,31},{8,0},{9,1... | collective-permute-start | bytes 688136 | tf_op jit(solution)/shard_map/ppermute | solution.py:22
  29.0 9.0 %collective-permute-start.7 = (bf16[32,3584]{1,0:T(8,128)(2,1)S(1)}, bf16[32,3584]{1,0:T(8,128)(2,1)S(1)}, u32[]{:S(2)}, u32[]{:S(2)}) collective-permute-start(bf16[32,3584]{1,0:T(8,128)(2,1)S(1)} %slice.239), channel_id=1, source_target_pairs={{0,8},{1,9},{2,10},{3,11},{4,12},{5,13},{6,14},{7,15},{8,16},{9,17... | collective-permute-start | bytes 688136 | tf_op jit(solution)/shard_map/ppermute | solution.py:22
  34.6 6.7 %collective-permute-start.12 = (bf16[32,3584]{1,0:T(8,128)(2,1)S(1)}, bf16[32,3584]{1,0:T(8,128)(2,1)S(1)}, u32[]{:S(2)}, u32[]{:S(2)}) collective-permute-start(bf16[32,3584]{1,0:T(8,128)(2,1)S(1)} %slice.240), channel_id=1, source_target_pairs={{0,3},{1,0},{2,1},{3,2},{4,7},{5,4},{6,5},{7,6},{8,11},{9,8},{10,9... | collective-permute-start | bytes 688136 | tf_op jit(solution)/shard_map/ppermute | solution.py:22
  37.6 6.9 %collective-permute-start.14 = (bf16[32,3584]{1,0:T(8,128)(2,1)S(1)}, bf16[32,3584]{1,0:T(8,128)(2,1)S(1)}, u32[]{:S(2)}, u32[]{:S(2)}) collective-permute-start(bf16[32,3584]{1,0:T(8,128)(2,1)S(1)} %slice.241), channel_id=1, source_target_pairs={{0,1},{1,2},{2,3},{3,0},{4,5},{5,6},{6,7},{7,4},{8,9},{9,10},{10,1... | collective-permute-start | bytes 688136 | tf_op jit(solution)/shard_map/ppermute | solution.py:22
  50.9 14.9 %collective-permute-start.16 = (bf16[128,768]{1,0:T(8,128)(2,1)S(1)}, bf16[128,768]{1,0:T(8,128)(2,1)S(1)}, u32[]{:S(2)}, u32[]{:S(2)}) collective-permute-start(bf16[128,768]{1,0:T(8,128)(2,1)S(1)} %fusion.21), channel_id=1, source_target_pairs={{0,64},{32,96},{64,0},{96,32},{1,65},{33,97},{65,1},{97,33},{2,66}... | collective-permute-start | bytes 589832 | tf_op jit(solution)/shard_map/ppermute | solution.py:26
  52.1 9.5 %collective-permute-start.17 = (bf16[128,768]{1,0:T(8,128)(2,1)S(1)}, bf16[128,768]{1,0:T(8,128)(2,1)S(1)}, u32[]{:S(2)}, u32[]{:S(2)}) collective-permute-start(bf16[128,768]{1,0:T(8,128)(2,1)S(1)} %slice.329), channel_id=1, source_target_pairs={{0,64},{32,96},{64,0},{96,32},{1,65},{33,97},{65,1},{97,33},{2,66}... | collective-permute-start | bytes 589832 | tf_op jit(solution)/shard_map/ppermute | solution.py:26
  66.2 7.0 %collective-permute-start.34 = (bf16[128,768]{1,0:T(8,128)(2,1)S(1)}, bf16[128,768]{1,0:T(8,128)(2,1)S(1)}, u32[]{:S(2)}, u32[]{:S(2)}) collective-permute-start(bf16[128,768]{1,0:T(8,128)(2,1)S(1)} %get-tuple-element.43), channel_id=1, source_target_pairs={{0,32},{32,0},{64,96},{96,64},{1,33},{33,1},{65,97},{97,65},{2,34}... | collective-permute-start | bytes 589832 | tf_op jit(solution)/shard_map/ppermute | solution.py:26
  67.7 9.8 %collective-permute-start.35 = (bf16[64,3584]{1,0:T(8,128)(2,1)S(1)}, bf16[64,3584]{1,0:T(8,128)(2,1)S(1)}, u32[]{:S(2)}, u32[]{:S(2)}) collective-permute-start(bf16[64,3584]{1,0:T(8,128)(2,1)S(1)} %get-tuple-element.38), channel_id=1, source_target_pairs={{0,1},{1,2},{2,3},{3,0},{4,5},{5,6},{6,7},{7,4},{8,9},{9,10},{10,1... | collective-permute-start | bytes 1376264 | tf_op jit(solution)/shard_map/ppermute | solution.py:22
  67.7 9.7 %collective-permute-start.37 = (bf16[64,3584]{1,0:T(8,128)(2,1)S(1)}, bf16[64,3584]{1,0:T(8,128)(2,1)S(1)}, u32[]{:S(2)}, u32[]{:S(2)}) collective-permute-start(bf16[64,3584]{1,0:T(8,128)(2,1)S(1)} %get-tuple-element.37), channel_id=1, source_target_pairs={{0,3},{1,0},{2,1},{3,2},{4,7},{5,4},{6,5},{7,6},{8,11},{9,8},{10,9... | collective-permute-start | bytes 1376264 | tf_op jit(solution)/shard_map/ppermute | solution.py:22
  70.5 11.3 %collective-permute-start.19 = (bf16[64,3584]{1,0:T(8,128)(2,1)S(1)}, bf16[64,3584]{1,0:T(8,128)(2,1)S(1)}, u32[]{:S(2)}, u32[]{:S(2)}) collective-permute-start(bf16[64,3584]{1,0:T(8,128)(2,1)S(1)} %get-tuple-element.42), channel_id=1, source_target_pairs={{0,8},{1,9},{2,10},{3,11},{4,12},{5,13},{6,14},{7,15},{8,16},{9,17... | collective-permute-start | bytes 1376264 | tf_op jit(solution)/shard_map/ppermute | solution.py:22
  70.8 11.0 %collective-permute-start.21 = (bf16[64,3584]{1,0:T(8,128)(2,1)S(1)}, bf16[64,3584]{1,0:T(8,128)(2,1)S(1)}, u32[]{:S(2)}, u32[]{:S(2)}) collective-permute-start(bf16[64,3584]{1,0:T(8,128)(2,1)S(1)} %get-tuple-element.41), channel_id=1, source_target_pairs={{0,24},{1,25},{2,26},{3,27},{4,28},{5,29},{6,30},{7,31},{8,0},{9,1... | collective-permute-start | bytes 1376264 | tf_op jit(solution)/shard_map/ppermute | solution.py:22
  77.6 7.5 %collective-permute-start.36 = (bf16[32,3584]{1,0:T(8,128)(2,1)S(1)}, bf16[32,3584]{1,0:T(8,128)(2,1)S(1)}, u32[]{:S(2)}, u32[]{:S(2)}) collective-permute-start(bf16[32,3584]{1,0:T(8,128)(2,1)S(1)} %get-tuple-element.36), channel_id=1, source_target_pairs={{0,1},{1,2},{2,3},{3,0},{4,5},{5,6},{6,7},{7,4},{8,9},{9,10},{10,1... | collective-permute-start | bytes 688136 | tf_op jit(solution)/shard_map/ppermute | solution.py:22
  78.1 7.0 %collective-permute-start.38 = (bf16[32,3584]{1,0:T(8,128)(2,1)S(1)}, bf16[32,3584]{1,0:T(8,128)(2,1)S(1)}, u32[]{:S(2)}, u32[]{:S(2)}) collective-permute-start(bf16[32,3584]{1,0:T(8,128)(2,1)S(1)} %get-tuple-element.35), channel_id=1, source_target_pairs={{0,3},{1,0},{2,1},{3,2},{4,7},{5,4},{6,5},{7,6},{8,11},{9,8},{10,9... | collective-permute-start | bytes 688136 | tf_op jit(solution)/shard_map/ppermute | solution.py:22
  81.9 8.1 %collective-permute-start.20 = (bf16[32,3584]{1,0:T(8,128)(2,1)S(1)}, bf16[32,3584]{1,0:T(8,128)(2,1)S(1)}, u32[]{:S(2)}, u32[]{:S(2)}) collective-permute-start(bf16[32,3584]{1,0:T(8,128)(2,1)S(1)} %get-tuple-element.40), channel_id=1, source_target_pairs={{0,8},{1,9},{2,10},{3,11},{4,12},{5,13},{6,14},{7,15},{8,16},{9,17... | collective-permute-start | bytes 688136 | tf_op jit(solution)/shard_map/ppermute | solution.py:22
  82.1 7.8 %collective-permute-start.22 = (bf16[32,3584]{1,0:T(8,128)(2,1)S(1)}, bf16[32,3584]{1,0:T(8,128)(2,1)S(1)}, u32[]{:S(2)}, u32[]{:S(2)}) collective-permute-start(bf16[32,3584]{1,0:T(8,128)(2,1)S(1)} %get-tuple-element.39), channel_id=1, source_target_pairs={{0,24},{1,25},{2,26},{3,27},{4,28},{5,29},{6,30},{7,31},{8,0},{9,1... | collective-permute-start | bytes 688136 | tf_op jit(solution)/shard_map/ppermute | solution.py:22
  85.3 8.2 %collective-permute-start.41 = (bf16[16,3584]{1,0:T(8,128)(2,1)S(1)}, bf16[16,3584]{1,0:T(8,128)(2,1)S(1)}, u32[]{:S(2)}, u32[]{:S(2)}) collective-permute-start(bf16[16,3584]{1,0:T(8,128)(2,1)S(1)} %get-tuple-element.46), channel_id=1, source_target_pairs={{0,24},{1,25},{2,26},{3,27},{4,28},{5,29},{6,30},{7,31},{8,0},{9,1... | collective-permute-start | bytes 344072 | tf_op jit(solution)/shard_map/ppermute | solution.py:22
  86.8 8.0 %collective-permute-start.40 = (bf16[16,3584]{1,0:T(8,128)(2,1)S(1)}, bf16[16,3584]{1,0:T(8,128)(2,1)S(1)}, u32[]{:S(2)}, u32[]{:S(2)}) collective-permute-start(bf16[16,3584]{1,0:T(8,128)(2,1)S(1)} %get-tuple-element.47), channel_id=1, source_target_pairs={{0,8},{1,9},{2,10},{3,11},{4,12},{5,13},{6,14},{7,15},{8,16},{9,17... | collective-permute-start | bytes 344072 | tf_op jit(solution)/shard_map/ppermute | solution.py:22
  86.9 7.9 %collective-permute-start.39 = (bf16[16,3584]{1,0:T(8,128)(2,1)S(1)}, bf16[16,3584]{1,0:T(8,128)(2,1)S(1)}, u32[]{:S(2)}, u32[]{:S(2)}) collective-permute-start(bf16[16,3584]{1,0:T(8,128)(2,1)S(1)} %get-tuple-element.45), channel_id=1, source_target_pairs={{0,16},{1,17},{2,18},{3,19},{4,20},{5,21},{6,22},{7,23},{8,24},{9,... | collective-permute-start | bytes 344072 | tf_op jit(solution)/shard_map/ppermute | solution.py:22
  90.2 8.4 %collective-permute-start.25 = (bf16[16,3584]{1,0:T(8,128)(2,1)S(1)}, bf16[16,3584]{1,0:T(8,128)(2,1)S(1)}, u32[]{:S(2)}, u32[]{:S(2)}) collective-permute-start(bf16[16,3584]{1,0:T(8,128)(2,1)S(1)} %get-tuple-element.49), channel_id=1, source_target_pairs={{0,3},{1,0},{2,1},{3,2},{4,7},{5,4},{6,5},{7,6},{8,11},{9,8},{10,9... | collective-permute-start | bytes 344072 | tf_op jit(solution)/shard_map/ppermute | solution.py:22
  93.5 6.3 %collective-permute-start.24 = (bf16[16,3584]{1,0:T(8,128)(2,1)S(1)}, bf16[16,3584]{1,0:T(8,128)(2,1)S(1)}, u32[]{:S(2)}, u32[]{:S(2)}) collective-permute-start(bf16[16,3584]{1,0:T(8,128)(2,1)S(1)} %get-tuple-element.50), channel_id=1, source_target_pairs={{0,1},{1,2},{2,3},{3,0},{4,5},{5,6},{6,7},{7,4},{8,9},{9,10},{10,1... | collective-permute-start | bytes 344072 | tf_op jit(solution)/shard_map/ppermute | solution.py:22
  93.5 6.3 %collective-permute-start.23 = (bf16[16,3584]{1,0:T(8,128)(2,1)S(1)}, bf16[16,3584]{1,0:T(8,128)(2,1)S(1)}, u32[]{:S(2)}, u32[]{:S(2)}) collective-permute-start(bf16[16,3584]{1,0:T(8,128)(2,1)S(1)} %get-tuple-element.48), channel_id=1, source_target_pairs={{0,2},{1,3},{2,0},{3,1},{4,6},{5,7},{6,4},{7,5},{8,10},{9,11},{10,... | collective-permute-start | bytes 344072 | tf_op jit(solution)/shard_map/ppermute | solution.py:22
  94.9 8.5 %collective-permute-start.42 = (bf16[16,3584]{1,0:T(8,128)(2,1)S(1)}, bf16[16,3584]{1,0:T(8,128)(2,1)S(1)}, u32[]{:S(2)}, u32[]{:S(2)}) collective-permute-start(bf16[16,3584]{1,0:T(8,128)(2,1)S(1)} %fusion.31), channel_id=1, source_target_pairs={{0,4},{1,5},{2,6},{3,7},{4,0},{5,1},{6,2},{7,3},{8,12},{9,13},{10,... | collective-permute-start | bytes 344072 | tf_op jit(solution)/shard_map/ppermute | solution.py:22
  99.8 5.9 %collective-permute-start.26 = (bf16[16,3584]{1,0:T(8,128)(2,1)S(1)}, bf16[16,3584]{1,0:T(8,128)(2,1)S(1)}, u32[]{:S(2)}, u32[]{:S(2)}) collective-permute-start(bf16[16,3584]{1,0:T(8,128)(2,1)S(1)} %fusion.30), channel_id=1, source_target_pairs={{0,4},{1,5},{2,6},{3,7},{4,0},{5,1},{6,2},{7,3},{8,12},{9,13},{10,... | collective-permute-start | bytes 344072 | tf_op jit(solution)/shard_map/ppermute | solution.py:22
  107.8 5.5 %collective-permute-start.28 = (bf16[16,3584]{1,0:T(8,128)(2,1)S(1)}, bf16[16,3584]{1,0:T(8,128)(2,1)S(1)}, u32[]{:S(2)}, u32[]{:S(2)}) collective-permute-start(bf16[16,3584]{1,0:T(8,128)(2,1)S(1)} %get-tuple-element.90), channel_id=1, source_target_pairs={{0,2},{1,3},{2,0},{3,1},{4,6},{5,7},{6,4},{7,5},{8,10},{9,11},{10,... | collective-permute-start | bytes 344072 | tf_op jit(solution)/shard_map/ppermute | solution.py:22
  108.0 6.3 %collective-permute-start.29 = (bf16[16,3584]{1,0:T(8,128)(2,1)S(1)}, bf16[16,3584]{1,0:T(8,128)(2,1)S(1)}, u32[]{:S(2)}, u32[]{:S(2)}) collective-permute-start(bf16[16,3584]{1,0:T(8,128)(2,1)S(1)} %get-tuple-element.90), channel_id=1, source_target_pairs={{0,1},{1,2},{2,3},{3,0},{4,5},{5,6},{6,7},{7,4},{8,9},{9,10},{10,1... | collective-permute-start | bytes 344072 | tf_op jit(solution)/shard_map/ppermute | solution.py:22
  108.5 8.1 %collective-permute-start.43 = (bf16[16,3584]{1,0:T(8,128)(2,1)S(1)}, bf16[16,3584]{1,0:T(8,128)(2,1)S(1)}, u32[]{:S(2)}, u32[]{:S(2)}) collective-permute-start(bf16[16,3584]{1,0:T(8,128)(2,1)S(1)} %get-tuple-element.26), channel_id=1, source_target_pairs={{0,24},{1,25},{2,26},{3,27},{4,28},{5,29},{6,30},{7,31},{8,0},{9,1... | collective-permute-start | bytes 344072 | tf_op jit(solution)/shard_map/ppermute | solution.py:22
  110.7 5.8 %collective-permute-start.44 = (bf16[16,3584]{1,0:T(8,128)(2,1)S(1)}, bf16[16,3584]{1,0:T(8,128)(2,1)S(1)}, u32[]{:S(2)}, u32[]{:S(2)}) collective-permute-start(bf16[16,3584]{1,0:T(8,128)(2,1)S(1)} %get-tuple-element.26), channel_id=1, source_target_pairs={{0,16},{1,17},{2,18},{3,19},{4,20},{5,21},{6,22},{7,23},{8,24},{9,... | collective-permute-start | bytes 344072 | tf_op jit(solution)/shard_map/ppermute | solution.py:22
  110.8 6.1 %collective-permute-start.45 = (bf16[16,3584]{1,0:T(8,128)(2,1)S(1)}, bf16[16,3584]{1,0:T(8,128)(2,1)S(1)}, u32[]{:S(2)}, u32[]{:S(2)}) collective-permute-start(bf16[16,3584]{1,0:T(8,128)(2,1)S(1)} %get-tuple-element.26), channel_id=1, source_target_pairs={{0,8},{1,9},{2,10},{3,11},{4,12},{5,13},{6,14},{7,15},{8,16},{9,17... | collective-permute-start | bytes 344072 | tf_op jit(solution)/shard_map/ppermute | solution.py:22
  114.3 10.2 %collective-permute-start.30 = (bf16[64,3584]{1,0:T(8,128)(2,1)S(1)}, bf16[64,3584]{1,0:T(8,128)(2,1)S(1)}, u32[]{:S(2)}, u32[]{:S(2)}) collective-permute-start(bf16[64,3584]{1,0:T(8,128)(2,1)S(1)} %pad_maximum_fusion.2), channel_id=1, source_target_pairs={{0,24},{1,25},{2,26},{3,27},{4,28},{5,29},{6,30},{7,31},{8,0},{9,1... | collective-permute-start | bytes 1376264 | tf_op jit(solution)/shard_map/ppermute | solution.py:22
  116.5 11.4 %collective-permute-start.32 = (bf16[64,3584]{1,0:T(8,128)(2,1)S(1)}, bf16[64,3584]{1,0:T(8,128)(2,1)S(1)}, u32[]{:S(2)}, u32[]{:S(2)}) collective-permute-start(bf16[64,3584]{1,0:T(8,128)(2,1)S(1)} %pad_maximum_fusion.2), channel_id=1, source_target_pairs={{0,8},{1,9},{2,10},{3,11},{4,12},{5,13},{6,14},{7,15},{8,16},{9,17... | collective-permute-start | bytes 1376264 | tf_op jit(solution)/shard_map/ppermute | solution.py:22
  116.9 11.1 %collective-permute-start.46 = (bf16[64,3584]{1,0:T(8,128)(2,1)S(1)}, bf16[64,3584]{1,0:T(8,128)(2,1)S(1)}, u32[]{:S(2)}, u32[]{:S(2)}) collective-permute-start(bf16[64,3584]{1,0:T(8,128)(2,1)S(1)} %pad_maximum_fusion.3), channel_id=1, source_target_pairs={{0,3},{1,0},{2,1},{3,2},{4,7},{5,4},{6,5},{7,6},{8,11},{9,8},{10,9... | collective-permute-start | bytes 1376264 | tf_op jit(solution)/shard_map/ppermute | solution.py:22
  119.7 11.1 %collective-permute-start.48 = (bf16[64,3584]{1,0:T(8,128)(2,1)S(1)}, bf16[64,3584]{1,0:T(8,128)(2,1)S(1)}, u32[]{:S(2)}, u32[]{:S(2)}) collective-permute-start(bf16[64,3584]{1,0:T(8,128)(2,1)S(1)} %pad_maximum_fusion.3), channel_id=1, source_target_pairs={{0,1},{1,2},{2,3},{3,0},{4,5},{5,6},{6,7},{7,4},{8,9},{9,10},{10,1... | collective-permute-start | bytes 1376264 | tf_op jit(solution)/shard_map/ppermute | solution.py:22
  124.5 16.9 %collective-permute-start.31 = (bf16[32,3584]{1,0:T(8,128)(2,1)S(1)}, bf16[32,3584]{1,0:T(8,128)(2,1)S(1)}, u32[]{:S(2)}, u32[]{:S(2)}) collective-permute-start(bf16[32,3584]{1,0:T(8,128)(2,1)S(1)} %slice.258), channel_id=1, source_target_pairs={{0,24},{1,25},{2,26},{3,27},{4,28},{5,29},{6,30},{7,31},{8,0},{9,1... | collective-permute-start | bytes 688136 | tf_op jit(solution)/shard_map/ppermute | solution.py:22
  127.9 13.5 %collective-permute-start.33 = (bf16[32,3584]{1,0:T(8,128)(2,1)S(1)}, bf16[32,3584]{1,0:T(8,128)(2,1)S(1)}, u32[]{:S(2)}, u32[]{:S(2)}) collective-permute-start(bf16[32,3584]{1,0:T(8,128)(2,1)S(1)} %slice.259), channel_id=1, source_target_pairs={{0,8},{1,9},{2,10},{3,11},{4,12},{5,13},{6,14},{7,15},{8,16},{9,17... | collective-permute-start | bytes 688136 | tf_op jit(solution)/shard_map/ppermute | solution.py:22
  128.0 8.2 %collective-permute-start.47 = (bf16[32,3584]{1,0:T(8,128)(2,1)S(1)}, bf16[32,3584]{1,0:T(8,128)(2,1)S(1)}, u32[]{:S(2)}, u32[]{:S(2)}) collective-permute-start(bf16[32,3584]{1,0:T(8,128)(2,1)S(1)} %slice.273), channel_id=1, source_target_pairs={{0,3},{1,0},{2,1},{3,2},{4,7},{5,4},{6,5},{7,6},{8,11},{9,8},{10,9... | collective-permute-start | bytes 688136 | tf_op jit(solution)/shard_map/ppermute | solution.py:22
  130.8 9.0 %collective-permute-start.49 = (bf16[32,3584]{1,0:T(8,128)(2,1)S(1)}, bf16[32,3584]{1,0:T(8,128)(2,1)S(1)}, u32[]{:S(2)}, u32[]{:S(2)}) collective-permute-start(bf16[32,3584]{1,0:T(8,128)(2,1)S(1)} %slice.274), channel_id=1, source_target_pairs={{0,1},{1,2},{2,3},{3,0},{4,5},{5,6},{6,7},{7,4},{8,9},{9,10},{10,1... | collective-permute-start | bytes 688136 | tf_op jit(solution)/shard_map/ppermute | solution.py:22
  143.3 10.8 %collective-permute-start.50 = (bf16[264,768]{1,0:T(8,128)(2,1)S(1)}, bf16[264,768]{1,0:T(8,128)(2,1)S(1)}, u32[]{:S(2)}, u32[]{:S(2)}) collective-permute-start(bf16[264,768]{1,0:T(8,128)(2,1)S(1)} %pad_maximum_fusion.4), channel_id=1, source_target_pairs={{0,32},{32,0},{64,96},{96,64},{1,33},{33,1},{65,97},{97,65},{2,34}... | collective-permute-start | bytes 1216520 | tf_op jit(solution)/shard_map/ppermute | solution.py:26
  154.4 10.7 %collective-permute-start.51 = (bf16[264,768]{1,0:T(8,128)(2,1)S(1)}, bf16[264,768]{1,0:T(8,128)(2,1)S(1)}, u32[]{:S(2)}, u32[]{:S(2)}) collective-permute-start(bf16[264,768]{1,0:T(8,128)(2,1)S(1)} %pad_maximum_fusion.5), channel_id=1, source_target_pairs={{0,64},{32,96},{64,0},{96,32},{1,65},{33,97},{65,1},{97,33},{2,66}... | collective-permute-start | bytes 1216520 | tf_op jit(solution)/shard_map/ppermute | solution.py:26
  (10 other events, 79.9 us)
